TPU v7x, 32 devices: a whole 2x2x4 slice. The times are simulated.
32 devices in a mesh: groups: 2 (over y), expert: 16 (over z, x, core), sub: 1, pair: 1.
Axes of the slice: x: 2, y: 2, z: 4, core: 2. Of those that a mesh axis runs over, the one named last changes fastest.
Arguments:
- tokens: bfloat16 [128, 3584], P(('groups', 'expert', 'sub', 'pair')), parts along dimension 0, may hold values from -6 to 6
- expert_ids: int32 [128, 8], P(('groups', 'expert', 'sub', 'pair')), parts along dimension 0, may hold values from 0 to 15, all different within a row; in each aligned block of 4 rows (0 to 3, 4 to 7, ...) at most 3 rows name the same one
- scores: float32 [128, 8], P(('groups', 'expert', 'sub', 'pair')), parts along dimension 0, may hold values from 0.05 to 1
- gate_w: bfloat16 [16, 3584, 2048], P('expert', None, 'sub'), may hold values from -0.09375 to 0.09375
- up_w: bfloat16 [16, 3584, 2048], P('expert', None, 'sub'), may hold values from -0.09375 to 0.09375
- down_w: bfloat16 [16, 2048, 3584], P('expert', None, ('sub', 'pair')), may hold values from -0.125 to 0.125
Outputs:
- moe_out: bfloat16 [128, 3584], P(('groups', 'expert', 'sub', 'pair')), parts along dimension 0
There are 2 independent parts, one for each index of `groups`. A program takes and returns all parts, laid end to end along the dimension named above; an argument that names none is the same for every part. Nothing has to cross between parts.
Inputs may be any that keep to these rules, and one draw needn't show every extreme that they name: `expert_ids`: each row names 8 different experts. In each aligned block of 4 rows (the rows of one device) no expert is named by more than 3 rows, a bound that some block reaches.
All inputs are finite; a program needn't handle non-finite values.
Results may differ from a plain program's by a relative error of at most 0.0058.
Values may be sent and summed in bfloat16 or wider, within the bound.
No kernel may reach another device: no remote copies, remote signals or barrier semaphores. Data moves between devices by JAX's collectives and lax.ppermute only.
A program may use at most 128 MiB of HBM per device.

v0:
```python
import jax
import jax.numpy as jnp
from jax import lax
from jax.sharding import PartitionSpec as P


def slot_table(ids, count):
    hit = (ids[:, :, None] == jnp.arange(count, dtype=jnp.int32)[None, None, :]).astype(jnp.int32)
    per_row = jnp.sum(hit, axis=1)
    before = jnp.cumsum(per_row, axis=0) - per_row
    slot = jnp.sum(hit * before[:, None, :], axis=2)
    return (hit, slot)


def shards(tokens, expert_ids, scores, gate_w, up_w, down_w):
    experts = lax.axis_size("expert")
    sub_count = lax.axis_size("sub")
    pair_count = lax.axis_size("pair")
    sharers = sub_count * pair_count
    row_count = tokens.shape[0]
    top_k = expert_ids.shape[1]
    model_width = tokens.shape[1]
    capacity = min(row_count, row_count * top_k // experts + 1)
    weight_gate = gate_w[0]
    weight_up = up_w[0]
    weight_down = down_w[0]
    unit_count = weight_gate.shape[1]
    slot_range = jnp.arange(capacity, dtype=jnp.int32)
    hit, slot = slot_table(expert_ids, experts)
    in_slot = (slot[:, :, None] == slot_range[None, None, :]).astype(jnp.int32)
    place = jnp.sum(hit[:, :, :, None] * in_slot[:, :, None, :], axis=1).astype(jnp.bfloat16)
    buckets = jnp.einsum("rec,rd->ecd", place, tokens, preferred_element_type=jnp.float32).astype(
        jnp.bfloat16
    )
    received = lax.all_to_all(buckets, "expert", split_axis=0, concat_axis=0, tiled=True)
    flat = received.reshape(experts * capacity, model_width)
    piece = lax.all_gather(flat, "sub", axis=0, tiled=True)
    gate_part = jnp.dot(piece, weight_gate, preferred_element_type=jnp.float32)
    up_part = jnp.dot(piece, weight_up, preferred_element_type=jnp.float32)
    hidden = (jax.nn.silu(gate_part) * up_part).astype(jnp.bfloat16)
    stacked = hidden.reshape(sub_count, 1, experts * capacity, unit_count)
    joined = lax.all_gather(stacked, "pair", axis=1, tiled=True)
    joined = joined.reshape(sharers * experts * capacity, unit_count)
    outputs = jnp.dot(
        lax.all_gather(joined, "sub", axis=1, tiled=True),
        weight_down,
        preferred_element_type=jnp.float32,
    ).astype(jnp.bfloat16)
    outputs = outputs.reshape(sharers, experts, capacity, weight_down.shape[1])
    back = lax.all_to_all(
        lax.all_to_all(outputs, ("sub", "pair"), split_axis=0, concat_axis=3, tiled=True),
        "expert",
        split_axis=1,
        concat_axis=0,
        tiled=True,
    )
    back = back.reshape(experts, capacity, model_width).astype(jnp.float32)
    weight = 2.5 * scores / jnp.sum(scores, axis=1, keepdims=True)
    spread = weight[:, :, None, None] * (hit[:, :, :, None] * in_slot[:, :, None, :]).astype(
        jnp.float32
    )
    mixing = jnp.sum(spread, axis=1)
    total = jnp.einsum(
        "rec,ecd->rd",
        mixing,
        back,
        precision=lax.Precision.HIGHEST,
        preferred_element_type=jnp.float32,
    )
    return total.astype(jnp.bfloat16)


def solution(mesh):
    in_specs = (
        P(("groups", "expert", "sub", "pair"), None),
        P(("groups", "expert", "sub", "pair"), None),
        P(("groups", "expert", "sub", "pair"), None),
        P("expert", None, "sub"),
        P("expert", None, "sub"),
        P("expert", None, ("sub", "pair")),
    )
    out_specs = P(("groups", "expert", "sub", "pair"), None)
    return jax.shard_map(shards, mesh=mesh, in_specs=in_specs, out_specs=out_specs, check_vma=False)
```

profile of v0, /device:TPU:0, one launch (start us, length us, event | category | flops | bytes accessed | tf_op | source)
XLA Modules:
  0.0 65.5 jit_solution(9051093317555455898)
XLA Ops:
  0.0 0.0 copy-start
  0.0 0.8 %fusion.32 = s32[4,16]{1,0:T(4,128)S(1)} fusion(s32[4,8]{1,0:T(4,128)} %param.7), kind=kLoop, calls=%fused_computation.32 | loop fusion | flops 1472 | bytes 384 | tf_op jit(solution)/shard_map/reduce_sum | solution.py:9
  0.8 0.8 %fusion.29 = s32[4,8,16]{2,1,0:T(8,128)S(1)} fusion(s32[4,8]{1,0:T(4,128)} %param.7), kind=kLoop, calls=%fused_computation.27 | loop fusion | flops 1024 | bytes 2176 | tf_op jit(solution)/shard_map/convert_element_type | solution.py:8
  1.6 0.9 %select_reduce_fusion = s32[4,8]{1,0:T(4,128)S(1)} fusion(s32[4,16]{1,0:T(4,128)S(1)} %sub.7, s32[4,8]{1,0:T(4,128)} %param.7), kind=kLoop, calls=%fused_computation.25 | loop fusion | flops 1504 | bytes 512 | tf_op jit(solution)/shard_map/reduce_sum | solution.py:11
  2.5 0.1 multiply_reduce_fusion
  2.6 0.0 copy-done
  2.6 0.3 convolution_convert_fusion
  2.9 0.3 copy.19
  3.2 20.4 %all_to_all.14 = bf16[16,3,3584]{2,1,0:T(4,128)(2,1)S(1)} all-to-all(bf16[16,3,3584]{2,1,0:T(4,128)(2,1)S(1)} %copy.19), channel_id=1, replica_groups=mesh['groups'=2,'expert'=16,'sub'=1,'pair'=1] {'expert'}, dimensions={0} | all-to-all | bytes 688128 | tf_op jit(solution)/shard_map/all_to_all | solution.py:35
  23.6 0.3 reshape.37
  23.9 7.9 %fusion.4 = f32[48,2048]{1,0:T(8,128)S(1)} fusion(bf16[48,3584]{1,0:T(8,128)(2,1)S(1)} %reshape.37, bf16[1,3584,2048]{2,1,0:T(8,128)(2,1)} %param.9), kind=kOutput, calls=%fused_computation.4 | convolution fusion | flops 704643072 | bytes 15417344 | tf_op jit(solution)/shard_map/dot_general | solution.py:38
  31.8 0.0 copy-start.1
  31.8 14.7 %fusion.6 = bf16[48,3584]{1,0:T(8,128)(2,1)S(1)} fusion(bf16[1,2048,3584]{2,1,0:T(8,128)(2,1)} %param.11, bf16[48,3584]{1,0:T(8,128)(2,1)S(1)} %reshape.37, bf16[1,3584,2048]{2,1,0:T(8,128)(2,1)} %param.10, f32[48,2048]{1,0:T(8,128)S(1)} %fusion.4), kind=kOutput, calls=%fused_computation.6 | convolution fusion | flops 1410048000 | bytes 30441472 | tf_op jit(solution)/shard_map/dot_general | solution.py:44
  46.5 1.0 %reshape.38 = bf16[1,16,3,3584]{3,2,1,0:T(4,128)(2,1)} reshape(bf16[48,3584]{1,0:T(8,128)(2,1)S(1)} %fusion.6) | data formatting | bytes 688128 | tf_op jit(solution)/shard_map/reshape | solution.py:49
  47.4 3.9 %all-to-all-start.1 = ((bf16[1,16,3,3584]{3,2,0,1:T(4,128)(2,1)}), bf16[1,16,3,3584]{3,2,0,1:T(4,128)(2,1)S(1)}, u32[]{:S(2)}, u32[]{:S(2)}) async-start(bf16[1,16,3,3584]{3,2,0,1:T(4,128)(2,1)} %bitcast.4), calls=%async_computation.1 | async-start | bytes 917504 | tf_op jit(solution)/shard_map/all_to_all | solution.py:50
  51.3 0.0 copy-done.1
  51.3 0.1 reduce_sum.45
  51.5 0.1 multiply_divide_fusion
  51.5 0.1 fusion.27
  51.6 12.9 %all-to-all-done.1 = bf16[1,16,3,3584]{3,2,0,1:T(4,128)(2,1)S(1)} async-done(((bf16[1,16,3,3584]{3,2,0,1:T(4,128)(2,1)}), bf16[1,16,3,3584]{3,2,0,1:T(4,128)(2,1)S(1)}, u32[]{:S(2)}, u32[]{:S(2)}) %all-to-all-start.1) | async-done | bytes 344096 | tf_op jit(solution)/shard_map/all_to_all | solution.py:50
  64.6 0.9 %fusion.9 = bf16[4,3584]{1,0:T(4,128)(2,1)} fusion(bf16[1,16,3,3584]{3,2,0,1:T(4,128)(2,1)S(1)} %all-to-all-done.1, f32[4,16,3]{1,2,0:T(4,128)S(1)} %fusion.27), kind=kOutput, calls=%fused_computation.9 | convolution fusion | flops 8271872 | bytes 373504 | tf_op jit(solution)/shard_map/rec,ecd->rd/dot_general | solution.py:63
  (3 shorter events, 0.1 us)
Async XLA Ops:
  0.0 2.6 %copy-start = (bf16[4,3584]{1,0:T(4,128)(2,1)S(1)}, bf16[4,3584]{1,0:T(4,128)(2,1)}, u32[]{:S(2)}) copy-start(bf16[4,3584]{1,0:T(4,128)(2,1)} %param.6) | copy-start | bytes 86020
  31.8 19.5 %copy-start.1 = (f32[4,8]{1,0:T(4,128)S(1)}, f32[4,8]{1,0:T(4,128)}, u32[]{:S(2)}) copy-start(f32[4,8]{1,0:T(4,128)} %param.8) | copy-start | bytes 388
  47.4 17.1 %all-to-all-start.1 = ((bf16[1,16,3,3584]{3,2,0,1:T(4,128)(2,1)}), bf16[1,16,3,3584]{3,2,0,1:T(4,128)(2,1)S(1)}, u32[]{:S(2)}, u32[]{:S(2)}) async-start(bf16[1,16,3,3584]{3,2,0,1:T(4,128)(2,1)} %bitcast.4), calls=%async_computation.1 | async-start | bytes 917504 | tf_op jit(solution)/shard_map/all_to_all | solution.py:50
where the time goes:
time: 65.9 us; the launch traced here: 65.5 us
  matrix products  23.8 us (36%)
  blocking collectives  20.4 us (31%)
  waiting for transfers between devices  12.9 us (20%)
  starting transfers between devices  3.89 us (6%)
  other arithmetic  2.87 us (4%)
  local copies, waits for them, and re-layouts  1.55 us (2%)
    all_to_all x1, blocking collectives, shards(): lax.all_to_all(buckets, 'expert', split_axis=0, concat_axis=0, tiled=True)  20.4 us
    dot_general x1, matrix products, shards(): jnp.dot(lax.all_gather(joined, 'sub', axis=1, tiled=True), weight_down, p...  14.7 us
    all_to_all x1, waiting for transfers between devices, shards(): lax.all_to_all(lax.all_to_all(outputs, ('sub', 'pair'), split_axis=0, con...  12.9 us
    dot_general x1, matrix products, shards(): gate_part = jnp.dot(piece, weight_gate, preferred_element_type=jnp.float32)  7.88 us
    all_to_all x1, starting transfers between devices, shards(): lax.all_to_all(lax.all_to_all(outputs, ('sub', 'pair'), split_axis=0, con...  3.89 us
  transfers between devices with their start and end apart: 1, of which 1 were waited for; matrix products, arithmetic and copies ran while one was open for 0% of the time, Pallas kernels for 0%

commit v1 on v0

--- a/solution.py
+++ b/solution.py
@@ -1,7 +1,11 @@
 import jax
 import jax.numpy as jnp
 from jax import lax
+from jax.experimental import pallas as pl
+from jax.experimental.pallas import tpu as pltpu
 from jax.sharding import PartitionSpec as P
+
+LANES = 128
 
 
 def slot_table(ids, count):
@@ -12,7 +16,7 @@
     return (hit, slot)
 
 
-def shards(tokens, expert_ids, scores, gate_w, up_w, down_w):
+def general_shards(tokens, expert_ids, scores, gate_w, up_w, down_w):
     experts = lax.axis_size("expert")
     sub_count = lax.axis_size("sub")
     pair_count = lax.axis_size("pair")
@@ -70,6 +74,138 @@
     return total.astype(jnp.bfloat16)
 
 
+def swap(x, distance):
+    count = lax.axis_size("expert")
+    return lax.ppermute(x, "expert", [(i, i ^ distance) for i in range(count)])
+
+
+def vmem(count):
+    return [pl.BlockSpec(memory_space=pltpu.VMEM)] * count
+
+
+def pack_kernel(experts, tokens_ref, ids_ref, scores_ref, out_ref):
+    width = tokens_ref.shape[1]
+    scores = scores_ref[...]
+    ids = ids_ref[...]
+    weight = 2.5 * scores / jnp.sum(scores, axis=1, keepdims=True)
+    lane = lax.broadcasted_iota(jnp.int32, (scores.shape[0], LANES), 1)
+    target = lax.rem(lane, experts)
+    dense = jnp.zeros((scores.shape[0], LANES), jnp.float32)
+    for k in range(scores.shape[1]):
+        dense = dense + jnp.where(ids[:, k : k + 1] == target, weight[:, k : k + 1], 0.0)
+    high = dense.astype(jnp.bfloat16).astype(jnp.float32)
+    both = jnp.where(lane < experts, high, jnp.where(lane < 2 * experts, dense - high, 0.0))
+    out_ref[:, :width] = tokens_ref[...]
+    out_ref[:, width:] = both.astype(jnp.bfloat16)
+
+
+def hidden_kernel(step, xa_ref, xb_ref, gate_ref, up_ref, out_ref):
+    width = gate_ref.shape[1]
+    x = jnp.concatenate([xa_ref[:, :width], xb_ref[:, :width]], axis=0)
+    for start in range(0, gate_ref.shape[2], step):
+        cut = slice(start, start + step)
+        gate = jnp.dot(x, gate_ref[0, :, cut], preferred_element_type=jnp.float32)
+        up = jnp.dot(x, up_ref[0, :, cut], preferred_element_type=jnp.float32)
+        out_ref[:, cut] = (gate / (1.0 + jnp.exp(-gate)) * up).astype(jnp.bfloat16)
+
+
+def down_kernel(step, experts, hidden_ref, xa_ref, xb_ref, down_ref, keep_ref, send_ref):
+    width = down_ref.shape[2]
+    half = keep_ref.shape[0]
+    me = lax.axis_index("expert")
+    hidden = hidden_ref[...]
+    spread = jnp.concatenate([xa_ref[:, width:], xb_ref[:, width:]], axis=0).astype(jnp.float32)
+    lane = lax.broadcasted_iota(jnp.int32, spread.shape, 1)
+    mine = (lane == me) | (lane == me + experts)
+    weight = jnp.sum(jnp.where(mine, spread, 0.0), axis=1, keepdims=True)
+    for start in range(0, width, step):
+        cut = slice(start, start + step)
+        out = jnp.dot(hidden, down_ref[0, :, cut], preferred_element_type=jnp.float32)
+        part = out.astype(jnp.bfloat16).astype(jnp.float32) * weight
+        keep_ref[:, cut] = part[:half].astype(keep_ref.dtype)
+        send_ref[:, cut] = part[half:].astype(send_ref.dtype)
+
+
+def add_kernel(kept_ref, got_ref, keep_ref, send_ref):
+    half = keep_ref.shape[0]
+    total = kept_ref[...] + got_ref[...].astype(jnp.float32)
+    keep_ref[...] = total[:half]
+    send_ref[...] = total[half:].astype(send_ref.dtype)
+
+
+def last_kernel(kept_ref, got_ref, out_ref):
+    out_ref[...] = (kept_ref[...] + got_ref[...].astype(jnp.float32)).astype(out_ref.dtype)
+
+
+def shards(tokens, expert_ids, scores, gate_w, up_w, down_w):
+    experts = lax.axis_size("expert")
+    rows, width = tokens.shape
+    units = gate_w.shape[2]
+    params = pltpu.CompilerParams(vmem_limit_bytes=6 * 2**20)
+    gate_w = pltpu.with_memory_space_constraint(gate_w, pltpu.VMEM)
+    up_w = pltpu.with_memory_space_constraint(up_w, pltpu.VMEM)
+    down_w = pltpu.with_memory_space_constraint(down_w, pltpu.VMEM)
+    held = pl.pallas_call(
+        lambda *refs: pack_kernel(experts, *refs),
+        out_shape=jax.ShapeDtypeStruct((rows, width + LANES), jnp.bfloat16),
+        in_specs=vmem(3),
+        out_specs=vmem(1)[0],
+        compiler_params=params,
+        cost_estimate=pl.CostEstimate(flops=40_000_000_000, bytes_accessed=100_000_000, transcendentals=0),
+        name="pack",
+    )(tokens, expert_ids, scores)
+    distance = experts // 2
+    while distance > 1:
+        held = jnp.concatenate([held, swap(held, distance)], axis=0)
+        distance //= 2
+    other = swap(held, 1)
+    half = held.shape[0]
+    hidden = pl.pallas_call(
+        lambda *refs: hidden_kernel(256, *refs),
+        out_shape=jax.ShapeDtypeStruct((2 * half, units), jnp.bfloat16),
+        in_specs=vmem(4),
+        out_specs=vmem(1)[0],
+        compiler_params=params,
+        name="hidden",
+    )(held, other, gate_w, up_w)
+    keep, send = pl.pallas_call(
+        lambda *refs: down_kernel(256, experts, *refs),
+        out_shape=[
+            jax.ShapeDtypeStruct((half, width), jnp.float32),
+            jax.ShapeDtypeStruct((half, width), jnp.bfloat16),
+        ],
+        in_specs=vmem(4),
+        out_specs=vmem(2),
+        compiler_params=params,
+        name="down",
+    )(hidden, held, other, down_w)
+    distance = 1
+    while distance < experts // 2:
+        got = swap(send, distance)
+        half //= 2
+        keep, send = pl.pallas_call(
+            add_kernel,
+            out_shape=[
+                jax.ShapeDtypeStruct((half, width), jnp.float32),
+                jax.ShapeDtypeStruct((half, width), jnp.bfloat16),
+            ],
+            in_specs=vmem(2),
+            out_specs=vmem(2),
+            compiler_params=params,
+            name="add",
+        )(keep, got)
+        distance *= 2
+    got = swap(send, distance)
+    return pl.pallas_call(
+        last_kernel,
+        out_shape=jax.ShapeDtypeStruct((rows, width), jnp.bfloat16),
+        in_specs=vmem(2),
+        out_specs=vmem(1)[0],
+        compiler_params=params,
+        name="last",
+    )(keep, got)
+
+
 def solution(mesh):
     in_specs = (
         P(("groups", "expert", "sub", "pair"), None),
@@ -80,4 +216,6 @@
         P("expert", None, ("sub", "pair")),
     )
     out_specs = P(("groups", "expert", "sub", "pair"), None)
-    return jax.shard_map(shards, mesh=mesh, in_specs=in_specs, out_specs=out_specs, check_vma=False)
+    whole = mesh.shape["sub"] == 1 and mesh.shape["pair"] == 1
+    body = shards if whole else general_shards
+    return jax.shard_map(body, mesh=mesh, in_specs=in_specs, out_specs=out_specs, check_vma=False)

time: 65.9 us -> 45.8 us (0.69)
  matrix products: 23.8 us -> 0 us
  blocking collectives: 20.4 us -> 0 us
  starting transfers between devices: 3.89 us -> 13.9 us
  Pallas kernels: 0 us -> 8.99 us
  waiting for transfers between devices: 12.9 us -> 19 us
  other arithmetic: 2.87 us -> 0.14 us
  local copies, waits for them, and re-layouts: 1.55 us -> 3.43 us
    dot_general x4 -> x0, matrix products: 23.8 us -> none  [the longest x1 14.7 us: shards(): jnp.dot(lax.all_gather(joined, 'sub', axis=1, tiled=True), weight_down, p...]
    all_to_all x1 -> x0, blocking collectives: 20.4 us -> none  [shards(): lax.all_to_all(buckets, 'expert', split_axis=0, concat_axis=0, tiled=True)]
    ppermute x0 -> x8, waiting for transfers between devices: none -> 19 us  [swap(): return lax.ppermute(x, 'expert', [(i, i ^ distance) for i in range(count)])]
    ppermute x0 -> x8, starting transfers between devices: none -> 13.9 us  [swap(): return lax.ppermute(x, 'expert', [(i, i ^ distance) for i in range(count)])]
    all_to_all x1 -> x0, waiting for transfers between devices: 12.9 us -> none  [shards(): lax.all_to_all(lax.all_to_all(outputs, ('sub', 'pair'), split_axis=0, con...]
    pallas_call x0 -> x7, Pallas kernels: none -> 8.99 us  [the longest x1 5.45 us: shards(): pl.pallas_call(lambda *refs: hidden_kernel(256, *refs), out_shape=jax.Sha...]
    all_to_all x1 -> x0, starting transfers between devices: 3.89 us -> none  [shards(): lax.all_to_all(lax.all_to_all(outputs, ('sub', 'pair'), split_axis=0, con...]
    unnamed x4 -> x18, local copies, waits for them, and re-layouts: 0.01 us -> 3.43 us
  transfers between devices with their start and end apart: 1 -> 8, of which waited for: 1 -> 8; matrix products, arithmetic and copies ran while one was open for 0% -> 0% of each run, Pallas kernels for 0% -> 0%
where the time goes in v1:
time: 45.8 us; the launch traced here: 45.6 us
  waiting for transfers between devices  19 us (41%)
  starting transfers between devices  13.9 us (30%)
  Pallas kernels  8.99 us (20%)
  local copies, waits for them, and re-layouts  3.43 us (7%)
    ppermute x8, waiting for transfers between devices, swap(): return lax.ppermute(x, 'expert', [(i, i ^ distance) for i in range(count)])  19 us
    ppermute x8, starting transfers between devices, swap(): return lax.ppermute(x, 'expert', [(i, i ^ distance) for i in range(count)])  13.9 us
    pallas_call x1, Pallas kernels, shards(): pl.pallas_call(lambda *refs: hidden_kernel(256, *refs), out_shape=jax.Sha...  5.45 us
    unnamed x18, local copies, waits for them, and re-layouts  3.43 us
    pallas_call x1, Pallas kernels, shards(): pl.pallas_call(lambda *refs: down_kernel(256, experts, *refs), out_shape=...  2.64 us
  transfers between devices with their start and end apart: 8, of which 8 were waited for; matrix products, arithmetic and copies ran while one was open for 0% of the time, Pallas kernels for 0%

profile of v1, /device:TPU:0, one launch (start us, length us, event | category | flops | bytes accessed | tf_op | source)
XLA Modules:
  0.0 45.6 jit_solution(876782787678571907)
XLA Ops:
  0.0 0.9 %copy-done.2 = bf16[4,3584]{1,0:T(4,128)(2,1)S(1)} copy-done((bf16[4,3584]{1,0:T(4,128)(2,1)S(1)}, bf16[4,3584]{1,0:T(4,128)(2,1)}, u32[]{:S(2)}) %copy-start.2) | copy-done | bytes 28696
  0.9 1.1 %copy-done.3 = s32[4,8]{1,0:T(4,128)S(1)} copy-done((s32[4,8]{1,0:T(4,128)S(1)}, s32[4,8]{1,0:T(4,128)}, u32[]{:S(2)}) %copy-start.3) | copy-done | bytes 152
  2.0 1.4 %copy-done.4 = f32[4,8]{1,0:T(4,128)S(1)} copy-done((f32[4,8]{1,0:T(4,128)S(1)}, f32[4,8]{1,0:T(4,128)}, u32[]{:S(2)}) %copy-start.4) | copy-done | bytes 152
  3.4 0.2 pack.1
  3.6 4.1 %collective-permute-start = (bf16[4,3712]{1,0:T(4,128)(2,1)S(1)}, bf16[4,3712]{1,0:T(4,128)(2,1)S(1)}, u32[]{:S(2)}, u32[]{:S(2)}) collective-permute-start(bf16[4,3712]{1,0:T(4,128)(2,1)S(1)} %pack.1), channel_id=1, source_target_pairs={{0,8},{1,9},{2,10},{3,11},{4,12},{5,13},{6,14},{7,15},{8,0},{9,1},... | collective-permute-start | bytes 89096 | tf_op jit(solution)/shard_map/ppermute | solution.py:79
  7.7 2.2 %collective-permute-done = bf16[4,3712]{1,0:T(4,128)(2,1)S(1)} collective-permute-done((bf16[4,3712]{1,0:T(4,128)(2,1)S(1)}, bf16[4,3712]{1,0:T(4,128)(2,1)S(1)}, u32[]{:S(2)}, u32[]{:S(2)}) %collective-permute-start) | collective-permute-done | bytes 29728 | tf_op jit(solution)/shard_map/ppermute | solution.py:79
  9.9 1.7 %collective-permute-start.1 = (bf16[8,3712]{1,0:T(8,128)(2,1)S(1)}, bf16[8,3712]{1,0:T(8,128)(2,1)S(1)}, u32[]{:S(2)}, u32[]{:S(2)}) collective-permute-start(bf16[8,3712]{1,0:T(8,128)(2,1)S(1)} %pad_maximum_fusion.2), channel_id=1, source_target_pairs={{0,4},{1,5},{2,6},{3,7},{4,0},{5,1},{6,2},{7,3},{8,12},{9,13},{10,... | collective-permute-start | bytes 178184 | tf_op jit(solution)/shard_map/ppermute | solution.py:79
  11.6 2.6 %collective-permute-done.1 = bf16[8,3712]{1,0:T(8,128)(2,1)S(1)} collective-permute-done((bf16[8,3712]{1,0:T(8,128)(2,1)S(1)}, bf16[8,3712]{1,0:T(8,128)(2,1)S(1)}, u32[]{:S(2)}, u32[]{:S(2)}) %collective-permute-start.1) | collective-permute-done | bytes 59424 | tf_op jit(solution)/shard_map/ppermute | solution.py:79
  14.2 0.1 pad_maximum_fusion.1
  14.2 1.8 %collective-permute-start.2 = (bf16[16,3712]{1,0:T(8,128)(2,1)S(1)}, bf16[16,3712]{1,0:T(8,128)(2,1)S(1)}, u32[]{:S(2)}, u32[]{:S(2)}) collective-permute-start(bf16[16,3712]{1,0:T(8,128)(2,1)S(1)} %pad_maximum_fusion.1), channel_id=1, source_target_pairs={{0,2},{1,3},{2,0},{3,1},{4,6},{5,7},{6,4},{7,5},{8,10},{9,11},{10,... | collective-permute-start | bytes 356360 | tf_op jit(solution)/shard_map/ppermute | solution.py:79
  16.0 3.1 %collective-permute-done.2 = bf16[16,3712]{1,0:T(8,128)(2,1)S(1)} collective-permute-done((bf16[16,3712]{1,0:T(8,128)(2,1)S(1)}, bf16[16,3712]{1,0:T(8,128)(2,1)S(1)}, u32[]{:S(2)}, u32[]{:S(2)}) %collective-permute-start.2) | collective-permute-done | bytes 118816 | tf_op jit(solution)/shard_map/ppermute | solution.py:79
  19.1 0.1 pad_maximum_fusion.refs_0_.refs_1_
  19.2 0.0 slice-start.1
  19.2 0.0 slice-start.2
  19.2 0.0 slice-start.3
  19.2 0.1 collective-permute-start.3
  19.3 1.5 %collective-permute-done.3.refs_1_.refs_2_ = bf16[32,3712]{1,0:T(8,128)(2,1)S(1)} collective-permute-done((bf16[32,3712]{1,0:T(8,128)(2,1)S(1)}, bf16[32,3712]{1,0:T(8,128)(2,1)S(1)}, u32[]{:S(2)}, u32[]{:S(2)}) %collective-permute-start.3) | collective-permute-done | bytes 237600 | tf_op jit(solution)/shard_map/ppermute | solution.py:79
  20.8 0.0 copy-done
  20.8 5.4 %hidden.1.refs_0_ = bf16[64,2048]{1,0:T(8,128)(2,1)S(1)} custom-call(bf16[32,3712]{1,0:T(8,128)(2,1)S(1)} %pad_maximum_fusion.refs_0_.refs_1_, bf16[32,3712]{1,0:T(8,128)(2,1)S(1)} %collective-permute-done.3.refs_1_.refs_2_, bf16[1,3584,2048]{2,1,0:T(8,128)(2,1)S(1)} %copy-done, bf16[1,3584,2048]{2,1,0:T(8,128)(2,1)S(1)} %copy-done.1), custom_call_target="tpu_custom_call" | custom-call | tf_op jit(solution)/shard_map/hidden/pallas_call | solution.py:163
  26.3 0.0 slice-done
  26.3 0.0 slice-done.1
  26.3 0.0 slice-done.2
  26.3 2.6 %down.1 = (f32[32,3584]{1,0:T(8,128)S(1)}, bf16[32,3584]{1,0:T(8,128)(2,1)S(1)}) custom-call(bf16[64,2048]{1,0:T(8,128)(2,1)S(1)} %hidden.1.refs_0_, bf16[32,3712]{1,0:T(8,128)(2,1)S(1)} %pad_maximum_fusion.refs_0_.refs_1_, bf16[32,3712]{1,0:T(8,128)(2,1)S(1)} %collective-permute-done.3.refs_1_.refs_2_, bf16[1,2048,3584]{2,1,0:T(8,128)(2,1)S(1)} %bitcast.1), custom_call_target="tpu_custom_call" | custom-call | tf_op jit(solution)/shard_map/down/pallas_call | solution.py:171
  29.0 0.2 collective-permute-start.4
  29.2 1.4 %collective-permute-done.4.got_ref = bf16[32,3584]{1,0:T(8,128)(2,1)S(1)} collective-permute-done((bf16[32,3584]{1,0:T(8,128)(2,1)S(1)}, bf16[32,3584]{1,0:T(8,128)(2,1)S(1)}, u32[]{:S(2)}, u32[]{:S(2)}) %collective-permute-start.4) | collective-permute-done | bytes 229408 | tf_op jit(solution)/shard_map/ppermute | solution.py:79
  30.6 1.8 %collective-permute-start.5 = (bf16[16,3584]{1,0:T(8,128)(2,1)S(1)}, bf16[16,3584]{1,0:T(8,128)(2,1)S(1)}, u32[]{:S(2)}, u32[]{:S(2)}) collective-permute-start(bf16[16,3584]{1,0:T(8,128)(2,1)S(1)} %get-tuple-element.16), channel_id=1, source_target_pairs={{0,2},{1,3},{2,0},{3,1},{4,6},{5,7},{6,4},{7,5},{8,10},{9,11},{10,... | collective-permute-start | bytes 344072 | tf_op jit(solution)/shard_map/ppermute | solution.py:79
  32.3 3.5 %collective-permute-done.5.got_ref = bf16[16,3584]{1,0:T(8,128)(2,1)S(1)} collective-permute-done((bf16[16,3584]{1,0:T(8,128)(2,1)S(1)}, bf16[16,3584]{1,0:T(8,128)(2,1)S(1)}, u32[]{:S(2)}, u32[]{:S(2)}) %collective-permute-start.5) | collective-permute-done | bytes 114720 | tf_op jit(solution)/shard_map/ppermute | solution.py:79
  35.8 1.7 %collective-permute-start.6 = (bf16[8,3584]{1,0:T(8,128)(2,1)S(1)}, bf16[8,3584]{1,0:T(8,128)(2,1)S(1)}, u32[]{:S(2)}, u32[]{:S(2)}) collective-permute-start(bf16[8,3584]{1,0:T(8,128)(2,1)S(1)} %get-tuple-element.18), channel_id=1, source_target_pairs={{0,4},{1,5},{2,6},{3,7},{4,0},{5,1},{6,2},{7,3},{8,12},{9,13},{10,... | collective-permute-start | bytes 172040 | tf_op jit(solution)/shard_map/ppermute | solution.py:79
  37.5 2.6 %collective-permute-done.6.got_ref = bf16[8,3584]{1,0:T(8,128)(2,1)S(1)} collective-permute-done((bf16[8,3584]{1,0:T(8,128)(2,1)S(1)}, bf16[8,3584]{1,0:T(8,128)(2,1)S(1)}, u32[]{:S(2)}, u32[]{:S(2)}) %collective-permute-start.6) | collective-permute-done | bytes 57376 | tf_op jit(solution)/shard_map/ppermute | solution.py:79
  40.1 2.7 %collective-permute-start.7 = (bf16[4,3584]{1,0:T(4,128)(2,1)S(1)}, bf16[4,3584]{1,0:T(4,128)(2,1)S(1)}, u32[]{:S(2)}, u32[]{:S(2)}) collective-permute-start(bf16[4,3584]{1,0:T(4,128)(2,1)S(1)} %get-tuple-element.20), channel_id=1, source_target_pairs={{0,8},{1,9},{2,10},{3,11},{4,12},{5,13},{6,14},{7,15},{8,0},{9,1},... | collective-permute-start | bytes 86024 | tf_op jit(solution)/shard_map/ppermute | solution.py:79
  42.8 2.2 %collective-permute-done.7.got_ref = bf16[4,3584]{1,0:T(4,128)(2,1)S(1)} collective-permute-done((bf16[4,3584]{1,0:T(4,128)(2,1)S(1)}, bf16[4,3584]{1,0:T(4,128)(2,1)S(1)}, u32[]{:S(2)}, u32[]{:S(2)}) %collective-permute-start.7) | collective-permute-done | bytes 28704 | tf_op jit(solution)/shard_map/ppermute | solution.py:79
  45.0 0.6 %last.1 = bf16[4,3584]{1,0:T(4,128)(2,1)} custom-call(f32[4,3584]{1,0:T(4,128)S(1)} %get-tuple-element.19.kept_ref, bf16[4,3584]{1,0:T(4,128)(2,1)S(1)} %collective-permute-done.7.got_ref), custom_call_target="tpu_custom_call" | custom-call | tf_op jit(solution)/shard_map/last/pallas_call | solution.py:199
  (13 shorter events, 0.1 us)
Async XLA Ops:
  0.0 20.8 %copy-start.1 = (bf16[1,3584,2048]{2,1,0:T(8,128)(2,1)S(1)}, bf16[1,3584,2048]{2,1,0:T(8,128)(2,1)}, u32[]{:S(2)}) copy-start(bf16[1,3584,2048]{2,1,0:T(8,128)(2,1)} %refs_3_.2) | copy-start | bytes 44040196
  0.0 20.8 %copy-start = (bf16[1,3584,2048]{2,1,0:T(8,128)(2,1)S(1)}, bf16[1,3584,2048]{2,1,0:T(8,128)(2,1)}, u32[]{:S(2)}) copy-start(bf16[1,3584,2048]{2,1,0:T(8,128)(2,1)} %refs_2_.3) | copy-start | bytes 44040196
  0.0 0.9 %copy-start.2 = (bf16[4,3584]{1,0:T(4,128)(2,1)S(1)}, bf16[4,3584]{1,0:T(4,128)(2,1)}, u32[]{:S(2)}) copy-start(bf16[4,3584]{1,0:T(4,128)(2,1)} %refs_0_.1) | copy-start | bytes 86020
  0.9 1.1 %copy-start.3 = (s32[4,8]{1,0:T(4,128)S(1)}, s32[4,8]{1,0:T(4,128)}, u32[]{:S(2)}) copy-start(s32[4,8]{1,0:T(4,128)} %refs_1_.1) | copy-start | bytes 388
  2.0 1.5 %copy-start.4 = (f32[4,8]{1,0:T(4,128)S(1)}, f32[4,8]{1,0:T(4,128)}, u32[]{:S(2)}) copy-start(f32[4,8]{1,0:T(4,128)} %refs_2_.2) | copy-start | bytes 388
  3.6 6.3 %collective-permute-start = (bf16[4,3712]{1,0:T(4,128)(2,1)S(1)}, bf16[4,3712]{1,0:T(4,128)(2,1)S(1)}, u32[]{:S(2)}, u32[]{:S(2)}) collective-permute-start(bf16[4,3712]{1,0:T(4,128)(2,1)S(1)} %pack.1), channel_id=1, source_target_pairs={{0,8},{1,9},{2,10},{3,11},{4,12},{5,13},{6,14},{7,15},{8,0},{9,1},... | collective-permute-start | bytes 89096 | tf_op jit(solution)/shard_map/ppermute | solution.py:79
  9.9 4.3 %collective-permute-start.1 = (bf16[8,3712]{1,0:T(8,128)(2,1)S(1)}, bf16[8,3712]{1,0:T(8,128)(2,1)S(1)}, u32[]{:S(2)}, u32[]{:S(2)}) collective-permute-start(bf16[8,3712]{1,0:T(8,128)(2,1)S(1)} %pad_maximum_fusion.2), channel_id=1, source_target_pairs={{0,4},{1,5},{2,6},{3,7},{4,0},{5,1},{6,2},{7,3},{8,12},{9,13},{10,... | collective-permute-start | bytes 178184 | tf_op jit(solution)/shard_map/ppermute | solution.py:79
  14.2 4.9 %collective-permute-start.2 = (bf16[16,3712]{1,0:T(8,128)(2,1)S(1)}, bf16[16,3712]{1,0:T(8,128)(2,1)S(1)}, u32[]{:S(2)}, u32[]{:S(2)}) collective-permute-start(bf16[16,3712]{1,0:T(8,128)(2,1)S(1)} %pad_maximum_fusion.1), channel_id=1, source_target_pairs={{0,2},{1,3},{2,0},{3,1},{4,6},{5,7},{6,4},{7,5},{8,10},{9,11},{10,... | collective-permute-start | bytes 356360 | tf_op jit(solution)/shard_map/ppermute | solution.py:79
  19.1 7.1 %slice-start = ((s8[14680064]{0:T(1024)(128)(4,1)}), s8[4194304]{0:T(1024)(128)(4,1)S(1)}, s32[]{:S(2)}) async-start(s8[14680064]{0:T(1024)(128)(4,1)} %bitcast), calls=%async_computation | async-start | bytes 8388608
  19.2 7.1 %slice-start.1 = ((s8[14680064]{0:T(1024)(128)(4,1)}), s8[4194304]{0:T(1024)(128)(4,1)S(1)}, s32[]{:S(2)}) async-start(s8[14680064]{0:T(1024)(128)(4,1)} %bitcast), calls=%async_computation.1 | async-start | bytes 8388608
  19.2 7.1 %slice-start.2 = ((s8[14680064]{0:T(1024)(128)(4,1)}), s8[4194304]{0:T(1024)(128)(4,1)S(1)}, s32[]{:S(2)}) async-start(s8[14680064]{0:T(1024)(128)(4,1)} %bitcast), calls=%async_computation.2 | async-start | bytes 8388608
  19.2 7.1 %slice-start.3 = ((s8[14680064]{0:T(1024)(128)(4,1)}), s8[2097152]{0:T(1024)(128)(4,1)S(1)}, s32[]{:S(2)}) async-start(s8[14680064]{0:T(1024)(128)(4,1)} %bitcast), calls=%async_computation.3 | async-start | bytes 4194304
  19.2 1.6 %collective-permute-start.3 = (bf16[32,3712]{1,0:T(8,128)(2,1)S(1)}, bf16[32,3712]{1,0:T(8,128)(2,1)S(1)}, u32[]{:S(2)}, u32[]{:S(2)}) collective-permute-start(bf16[32,3712]{1,0:T(8,128)(2,1)S(1)} %pad_maximum_fusion.refs_0_.refs_1_), channel_id=1, source_target_pairs={{0,1},{1,0},{2,3},{3,2},{4,5},{5,4},{6,7},{7,6},{8,9},{9,8},{10,11... | collective-permute-start | bytes 712712 | tf_op jit(solution)/shard_map/ppermute | solution.py:79
  29.0 1.6 %collective-permute-start.4 = (bf16[32,3584]{1,0:T(8,128)(2,1)S(1)}, bf16[32,3584]{1,0:T(8,128)(2,1)S(1)}, u32[]{:S(2)}, u32[]{:S(2)}) collective-permute-start(bf16[32,3584]{1,0:T(8,128)(2,1)S(1)} %get-tuple-element.14), channel_id=1, source_target_pairs={{0,1},{1,0},{2,3},{3,2},{4,5},{5,4},{6,7},{7,6},{8,9},{9,8},{10,11... | collective-permute-start | bytes 688136 | tf_op jit(solution)/shard_map/ppermute | solution.py:79
  30.6 5.3 %collective-permute-start.5 = (bf16[16,3584]{1,0:T(8,128)(2,1)S(1)}, bf16[16,3584]{1,0:T(8,128)(2,1)S(1)}, u32[]{:S(2)}, u32[]{:S(2)}) collective-permute-start(bf16[16,3584]{1,0:T(8,128)(2,1)S(1)} %get-tuple-element.16), channel_id=1, source_target_pairs={{0,2},{1,3},{2,0},{3,1},{4,6},{5,7},{6,4},{7,5},{8,10},{9,11},{10,... | collective-permute-start | bytes 344072 | tf_op jit(solution)/shard_map/ppermute | solution.py:79
  35.8 4.2 %collective-permute-start.6 = (bf16[8,3584]{1,0:T(8,128)(2,1)S(1)}, bf16[8,3584]{1,0:T(8,128)(2,1)S(1)}, u32[]{:S(2)}, u32[]{:S(2)}) collective-permute-start(bf16[8,3584]{1,0:T(8,128)(2,1)S(1)} %get-tuple-element.18), channel_id=1, source_target_pairs={{0,4},{1,5},{2,6},{3,7},{4,0},{5,1},{6,2},{7,3},{8,12},{9,13},{10,... | collective-permute-start | bytes 172040 | tf_op jit(solution)/shard_map/ppermute | solution.py:79
  40.1 4.8 %collective-permute-start.7 = (bf16[4,3584]{1,0:T(4,128)(2,1)S(1)}, bf16[4,3584]{1,0:T(4,128)(2,1)S(1)}, u32[]{:S(2)}, u32[]{:S(2)}) collective-permute-start(bf16[4,3584]{1,0:T(4,128)(2,1)S(1)} %get-tuple-element.20), channel_id=1, source_target_pairs={{0,8},{1,9},{2,10},{3,11},{4,12},{5,13},{6,14},{7,15},{8,0},{9,1},... | collective-permute-start | bytes 86024 | tf_op jit(solution)/shard_map/ppermute | solution.py:79

commit v2 on v1

--- a/solution.py
+++ b/solution.py
@@ -83,10 +83,26 @@
     return [pl.BlockSpec(memory_space=pltpu.VMEM)] * count
 
 
-def pack_kernel(experts, tokens_ref, ids_ref, scores_ref, out_ref):
+def hbm(count):
+    return [pl.BlockSpec(memory_space=pltpu.HBM)] * count
+
+
+def filled(x, rows):
+    return jnp.concatenate([x, jnp.zeros((rows - x.shape[0], x.shape[1]), x.dtype)], axis=0)
+
+
+def pack_kernel(experts, tokens_ref, ids_ref, scores_ref, out_ref, ids_vmem, scores_vmem, sems):
     width = tokens_ref.shape[1]
-    scores = scores_ref[...]
-    ids = ids_ref[...]
+    ids_copy = pltpu.make_async_copy(ids_ref, ids_vmem, sems.at[0])
+    scores_copy = pltpu.make_async_copy(scores_ref, scores_vmem, sems.at[1])
+    tokens_copy = pltpu.make_async_copy(tokens_ref, out_ref.at[:, pl.ds(0, width)], sems.at[2])
+    ids_copy.start()
+    scores_copy.start()
+    tokens_copy.start()
+    ids_copy.wait()
+    scores_copy.wait()
+    scores = scores_vmem[...]
+    ids = ids_vmem[...]
     weight = 2.5 * scores / jnp.sum(scores, axis=1, keepdims=True)
     lane = lax.broadcasted_iota(jnp.int32, (scores.shape[0], LANES), 1)
     target = lax.rem(lane, experts)
@@ -95,40 +111,70 @@
         dense = dense + jnp.where(ids[:, k : k + 1] == target, weight[:, k : k + 1], 0.0)
     high = dense.astype(jnp.bfloat16).astype(jnp.float32)
     both = jnp.where(lane < experts, high, jnp.where(lane < 2 * experts, dense - high, 0.0))
-    out_ref[:, :width] = tokens_ref[...]
     out_ref[:, width:] = both.astype(jnp.bfloat16)
-
-
-def hidden_kernel(step, xa_ref, xb_ref, gate_ref, up_ref, out_ref):
+    tokens_copy.wait()
+
+
+def join_kernel(*refs):
+    out_ref = refs[-1]
+    pieces = [ref[...].astype(jnp.float32) for ref in refs[:-1]]
+    out_ref[...] = jnp.concatenate(pieces, axis=0).astype(out_ref.dtype)
+
+
+def join(pieces, params):
+    rows = sum(piece.shape[0] for piece in pieces)
+    return pl.pallas_call(
+        join_kernel,
+        out_shape=jax.ShapeDtypeStruct((rows, pieces[0].shape[1]), pieces[0].dtype),
+        in_specs=vmem(len(pieces)),
+        out_specs=vmem(1)[0],
+        compiler_params=params,
+        name="join",
+    )(*pieces)
+
+
+def hidden_kernel(step, fill, xa_ref, xb_ref, gate_ref, up_ref, out_ref):
     width = gate_ref.shape[1]
-    x = jnp.concatenate([xa_ref[:, :width], xb_ref[:, :width]], axis=0)
+    rows = out_ref.shape[0]
+    x = filled(jnp.concatenate([xa_ref[:, :width], xb_ref[:, :width]], axis=0), fill)
     for start in range(0, gate_ref.shape[2], step):
         cut = slice(start, start + step)
-        gate = jnp.dot(x, gate_ref[0, :, cut], preferred_element_type=jnp.float32)
-        up = jnp.dot(x, up_ref[0, :, cut], preferred_element_type=jnp.float32)
+        gate = jnp.dot(x, gate_ref[0, :, cut], preferred_element_type=jnp.float32)[:rows]
+        up = jnp.dot(x, up_ref[0, :, cut], preferred_element_type=jnp.float32)[:rows]
         out_ref[:, cut] = (gate / (1.0 + jnp.exp(-gate)) * up).astype(jnp.bfloat16)
 
 
-def down_kernel(step, experts, hidden_ref, xa_ref, xb_ref, down_ref, keep_ref, send_ref):
+def down_kernel(step, fill, experts, hidden_ref, xa_ref, xb_ref, down_ref, keep_ref, send_ref):
     width = down_ref.shape[2]
     half = keep_ref.shape[0]
     me = lax.axis_index("expert")
-    hidden = hidden_ref[...]
+    hidden = filled(hidden_ref[...], fill)
     spread = jnp.concatenate([xa_ref[:, width:], xb_ref[:, width:]], axis=0).astype(jnp.float32)
     lane = lax.broadcasted_iota(jnp.int32, spread.shape, 1)
     mine = (lane == me) | (lane == me + experts)
     weight = jnp.sum(jnp.where(mine, spread, 0.0), axis=1, keepdims=True)
     for start in range(0, width, step):
         cut = slice(start, start + step)
-        out = jnp.dot(hidden, down_ref[0, :, cut], preferred_element_type=jnp.float32)
+        out = jnp.dot(hidden, down_ref[0, :, cut], preferred_element_type=jnp.float32)[: 2 * half]
         part = out.astype(jnp.bfloat16).astype(jnp.float32) * weight
-        keep_ref[:, cut] = part[:half].astype(keep_ref.dtype)
+        keep_ref[:, cut] = part[:half]
         send_ref[:, cut] = part[half:].astype(send_ref.dtype)
 
 
-def add_kernel(kept_ref, got_ref, keep_ref, send_ref):
+def first_add_kernel(kept_ref, got_ref, keep_ref, *send_refs):
+    total = kept_ref[...] + got_ref[...].astype(jnp.float32)
+    rows = keep_ref.shape[0]
+    keep_ref[...] = total[:rows]
+    for i, send_ref in enumerate(send_refs):
+        send_ref[...] = total[(i + 1) * rows : (i + 2) * rows].astype(send_ref.dtype)
+
+
+def second_add_kernel(kept_ref, *refs):
+    got_refs, (keep_ref, send_ref) = refs[:-2], refs[-2:]
+    total = kept_ref[...]
+    for got_ref in got_refs:
+        total = total + got_ref[...].astype(jnp.float32)
     half = keep_ref.shape[0]
-    total = kept_ref[...] + got_ref[...].astype(jnp.float32)
     keep_ref[...] = total[:half]
     send_ref[...] = total[half:].astype(send_ref.dtype)
 
@@ -141,27 +187,38 @@
     experts = lax.axis_size("expert")
     rows, width = tokens.shape
     units = gate_w.shape[2]
+    far = experts // 2
+    middle = [d for d in range(far - 2, 0, -2)]
+    half = rows * far
+    fill = max(2 * half, 128)
     params = pltpu.CompilerParams(vmem_limit_bytes=6 * 2**20)
     gate_w = pltpu.with_memory_space_constraint(gate_w, pltpu.VMEM)
     up_w = pltpu.with_memory_space_constraint(up_w, pltpu.VMEM)
     down_w = pltpu.with_memory_space_constraint(down_w, pltpu.VMEM)
-    held = pl.pallas_call(
+    tokens, expert_ids, scores = [
+        pltpu.with_memory_space_constraint(x, pltpu.HBM) for x in (tokens, expert_ids, scores)
+    ]
+    packed = pl.pallas_call(
         lambda *refs: pack_kernel(experts, *refs),
         out_shape=jax.ShapeDtypeStruct((rows, width + LANES), jnp.bfloat16),
-        in_specs=vmem(3),
-        out_specs=vmem(1)[0],
-        compiler_params=params,
-        cost_estimate=pl.CostEstimate(flops=40_000_000_000, bytes_accessed=100_000_000, transcendentals=0),
+        in_specs=hbm(3),
+        out_specs=vmem(1)[0],
+        scratch_shapes=[
+            pltpu.VMEM(expert_ids.shape, expert_ids.dtype),
+            pltpu.VMEM(scores.shape, scores.dtype),
+            pltpu.SemaphoreType.DMA((3,)),
+        ],
+        compiler_params=params,
+        cost_estimate=pl.CostEstimate(
+            flops=40_000_000_000, bytes_accessed=100_000_000, transcendentals=0
+        ),
         name="pack",
     )(tokens, expert_ids, scores)
-    distance = experts // 2
-    while distance > 1:
-        held = jnp.concatenate([held, swap(held, distance)], axis=0)
-        distance //= 2
+    near = join([packed, swap(packed, far)], params)
+    held = join([near] + [swap(near, d) for d in middle], params)
     other = swap(held, 1)
-    half = held.shape[0]
     hidden = pl.pallas_call(
-        lambda *refs: hidden_kernel(256, *refs),
+        lambda *refs: hidden_kernel(256, fill, *refs),
         out_shape=jax.ShapeDtypeStruct((2 * half, units), jnp.bfloat16),
         in_specs=vmem(4),
         out_specs=vmem(1)[0],
@@ -169,7 +226,7 @@
         name="hidden",
     )(held, other, gate_w, up_w)
     keep, send = pl.pallas_call(
-        lambda *refs: down_kernel(256, experts, *refs),
+        lambda *refs: down_kernel(256, fill, experts, *refs),
         out_shape=[
             jax.ShapeDtypeStruct((half, width), jnp.float32),
             jax.ShapeDtypeStruct((half, width), jnp.bfloat16),
@@ -179,23 +236,29 @@
         compiler_params=params,
         name="down",
     )(hidden, held, other, down_w)
-    distance = 1
-    while distance < experts // 2:
-        got = swap(send, distance)
-        half //= 2
-        keep, send = pl.pallas_call(
-            add_kernel,
-            out_shape=[
-                jax.ShapeDtypeStruct((half, width), jnp.float32),
-                jax.ShapeDtypeStruct((half, width), jnp.bfloat16),
-            ],
-            in_specs=vmem(2),
-            out_specs=vmem(2),
-            compiler_params=params,
-            name="add",
-        )(keep, got)
-        distance *= 2
-    got = swap(send, distance)
+    got = swap(send, 1)
+    keep, *sends = pl.pallas_call(
+        first_add_kernel,
+        out_shape=[jax.ShapeDtypeStruct((2 * rows, width), jnp.float32)]
+        + [jax.ShapeDtypeStruct((2 * rows, width), jnp.bfloat16)] * len(middle),
+        in_specs=vmem(2),
+        out_specs=vmem(1 + len(middle)),
+        compiler_params=params,
+        name="first_add",
+    )(keep, got)
+    gots = [swap(send, d) for send, d in zip(sends, middle)]
+    keep, send = pl.pallas_call(
+        second_add_kernel,
+        out_shape=[
+            jax.ShapeDtypeStruct((rows, width), jnp.float32),
+            jax.ShapeDtypeStruct((rows, width), jnp.bfloat16),
+        ],
+        in_specs=vmem(1 + len(middle)),
+        out_specs=vmem(2),
+        compiler_params=params,
+        name="second_add",
+    )(keep, *gots)
+    got = swap(send, far)
     return pl.pallas_call(
         last_kernel,
         out_shape=jax.ShapeDtypeStruct((rows, width), jnp.bfloat16),
@@ -216,6 +279,6 @@
         P("expert", None, ("sub", "pair")),
     )
     out_specs = P(("groups", "expert", "sub", "pair"), None)
-    whole = mesh.shape["sub"] == 1 and mesh.shape["pair"] == 1
+    whole = mesh.shape["sub"] == 1 and mesh.shape["pair"] == 1 and mesh.shape["expert"] == 16
     body = shards if whole else general_shards
     return jax.shard_map(body, mesh=mesh, in_specs=in_specs, out_specs=out_specs, check_vma=False)

time: 45.8 us -> 37.3 us (0.81)
  waiting for transfers between devices: 19 us -> 14.7 us
  local copies, waits for them, and re-layouts: 3.43 us -> 0.03 us
  Pallas kernels: 8.99 us -> 8 us
    ppermute x8 -> x10, waiting for transfers between devices: 19 us -> 14.7 us  [swap(): return lax.ppermute(x, 'expert', [(i, i ^ distance) for i in range(count)])]
    unnamed x18 -> x12, local copies, waits for them, and re-layouts: 3.43 us -> 0.03 us
    pallas_call x5 -> x6, Pallas kernels: 8.19 us -> 6.32 us  [the longest x1 4.12 us: shards(): pl.pallas_call(lambda *refs: hidden_kernel(256, fill, *refs), out_shape=j...]
    pallas_call x1, Pallas kernels: 0.18 us -> 1.06 us  [shards(): pl.pallas_call(lambda *refs: pack_kernel(experts, *refs), out_shape=jax.S...]
    ppermute x8 -> x10, starting transfers between devices: 13.9 us -> 14.3 us  [swap(): return lax.ppermute(x, 'expert', [(i, i ^ distance) for i in range(count)])]
  transfers between devices with their start and end apart: 8 -> 10, of which waited for: 8 -> 9; matrix products, arithmetic and copies ran while one was open for 0% -> 0% of each run, Pallas kernels for 0% -> 0%
where the time goes in v2:
time: 37.3 us; the launch traced here: 37.2 us
  waiting for transfers between devices  14.7 us (39%)
  starting transfers between devices  14.3 us (38%)
  Pallas kernels  8 us (21%)
    ppermute x10, waiting for transfers between devices, swap(): return lax.ppermute(x, 'expert', [(i, i ^ distance) for i in range(count)])  14.7 us
    ppermute x10, starting transfers between devices, swap(): return lax.ppermute(x, 'expert', [(i, i ^ distance) for i in range(count)])  14.3 us
    pallas_call x1, Pallas kernels, shards(): pl.pallas_call(lambda *refs: hidden_kernel(256, fill, *refs), out_shape=j...  4.12 us
    pallas_call x1, Pallas kernels, shards(): pl.pallas_call(lambda *refs: down_kernel(256, fill, experts, *refs), out_...  2.08 us
    pallas_call x1, Pallas kernels, shards(): pl.pallas_call(lambda *refs: pack_kernel(experts, *refs), out_shape=jax.S...  1.06 us
  transfers between devices with their start and end apart: 10, of which 9 were waited for; matrix products, arithmetic and copies ran while one was open for 0% of the time, Pallas kernels for 0%

profile of v2, /device:TPU:0, one launch (start us, length us, event | category | flops | bytes accessed | tf_op | source)
XLA Modules:
  0.0 37.2 jit_solution(16396267494653322273)
XLA Ops:
  0.0 1.1 %pack.1.refs_0_ = bf16[4,3712]{1,0:T(4,128)(2,1)S(1)} custom-call(bf16[4,3584]{1,0:T(4,128)(2,1)} %refs_0_.1, s32[4,8]{1,0:T(4,128)} %refs_1_.1, f32[4,8]{1,0:T(4,128)} %refs_2_.2), custom_call_target="tpu_custom_call" | custom-call | flops 40000000000 | bytes 100000000 | tf_op jit(solution)/shard_map/pack/pallas_call | solution.py:201
  1.1 4.1 %collective-permute-start = (bf16[4,3712]{1,0:T(4,128)(2,1)S(1)}, bf16[4,3712]{1,0:T(4,128)(2,1)S(1)}, u32[]{:S(2)}, u32[]{:S(2)}) collective-permute-start(bf16[4,3712]{1,0:T(4,128)(2,1)S(1)} %pack.1.refs_0_), channel_id=1, source_target_pairs={{0,8},{1,9},{2,10},{3,11},{4,12},{5,13},{6,14},{7,15},{8,0},{9,1},... | collective-permute-start | bytes 89096 | tf_op jit(solution)/shard_map/ppermute | solution.py:79
  5.2 2.2 %collective-permute-done.refs_1_ = bf16[4,3712]{1,0:T(4,128)(2,1)S(1)} collective-permute-done((bf16[4,3712]{1,0:T(4,128)(2,1)S(1)}, bf16[4,3712]{1,0:T(4,128)(2,1)S(1)}, u32[]{:S(2)}, u32[]{:S(2)}) %collective-permute-start) | collective-permute-done | bytes 29728 | tf_op jit(solution)/shard_map/ppermute | solution.py:79
  7.4 1.8 %collective-permute-start.3 = (bf16[8,3712]{1,0:T(8,128)(2,1)S(1)}, bf16[8,3712]{1,0:T(8,128)(2,1)S(1)}, u32[]{:S(2)}, u32[]{:S(2)}) collective-permute-start(bf16[8,3712]{1,0:T(8,128)(2,1)S(1)} %join.2.refs_0_), channel_id=1, source_target_pairs={{0,2},{1,3},{2,0},{3,1},{4,6},{5,7},{6,4},{7,5},{8,10},{9,11},{10,... | collective-permute-start | bytes 178184 | tf_op jit(solution)/shard_map/ppermute | solution.py:79
  9.1 1.4 %collective-permute-start.2 = (bf16[8,3712]{1,0:T(8,128)(2,1)S(1)}, bf16[8,3712]{1,0:T(8,128)(2,1)S(1)}, u32[]{:S(2)}, u32[]{:S(2)}) collective-permute-start(bf16[8,3712]{1,0:T(8,128)(2,1)S(1)} %join.2.refs_0_), channel_id=1, source_target_pairs={{0,4},{1,5},{2,6},{3,7},{4,0},{5,1},{6,2},{7,3},{8,12},{9,13},{10,... | collective-permute-start | bytes 178184 | tf_op jit(solution)/shard_map/ppermute | solution.py:79
  10.5 0.4 %collective-permute-start.1 = (bf16[8,3712]{1,0:T(8,128)(2,1)S(1)}, bf16[8,3712]{1,0:T(8,128)(2,1)S(1)}, u32[]{:S(2)}, u32[]{:S(2)}) collective-permute-start(bf16[8,3712]{1,0:T(8,128)(2,1)S(1)} %join.2.refs_0_), channel_id=1, source_target_pairs={{0,6},{1,7},{2,4},{3,5},{4,2},{5,3},{6,0},{7,1},{8,14},{9,15},{10,... | collective-permute-start | bytes 178184 | tf_op jit(solution)/shard_map/ppermute | solution.py:79
  10.9 0.7 %collective-permute-done.3.refs_3_ = bf16[8,3712]{1,0:T(8,128)(2,1)S(1)} collective-permute-done((bf16[8,3712]{1,0:T(8,128)(2,1)S(1)}, bf16[8,3712]{1,0:T(8,128)(2,1)S(1)}, u32[]{:S(2)}, u32[]{:S(2)}) %collective-permute-start.3) | collective-permute-done | bytes 59424 | tf_op jit(solution)/shard_map/ppermute | solution.py:79
  11.6 1.7 %collective-permute-done.2.refs_2_ = bf16[8,3712]{1,0:T(8,128)(2,1)S(1)} collective-permute-done((bf16[8,3712]{1,0:T(8,128)(2,1)S(1)}, bf16[8,3712]{1,0:T(8,128)(2,1)S(1)}, u32[]{:S(2)}, u32[]{:S(2)}) %collective-permute-start.2) | collective-permute-done | bytes 59424 | tf_op jit(solution)/shard_map/ppermute | solution.py:79
  13.3 2.3 %collective-permute-done.1.refs_1_ = bf16[8,3712]{1,0:T(8,128)(2,1)S(1)} collective-permute-done((bf16[8,3712]{1,0:T(8,128)(2,1)S(1)}, bf16[8,3712]{1,0:T(8,128)(2,1)S(1)}, u32[]{:S(2)}, u32[]{:S(2)}) %collective-permute-start.1) | collective-permute-done | bytes 59424 | tf_op jit(solution)/shard_map/ppermute | solution.py:79
  15.6 0.0 slice-start.1
  15.7 0.0 slice-start.2
  15.7 0.0 slice-start.3
  15.7 0.1 collective-permute-start.4
  15.8 1.5 %collective-permute-done.4.refs_1_.refs_2_ = bf16[32,3712]{1,0:T(8,128)(2,1)S(1)} collective-permute-done((bf16[32,3712]{1,0:T(8,128)(2,1)S(1)}, bf16[32,3712]{1,0:T(8,128)(2,1)S(1)}, u32[]{:S(2)}, u32[]{:S(2)}) %collective-permute-start.4) | collective-permute-done | bytes 237600 | tf_op jit(solution)/shard_map/ppermute | solution.py:79
  17.2 0.0 copy-done.1
  17.2 0.0 copy-done
  17.3 4.1 %hidden.1.refs_0_ = bf16[64,2048]{1,0:T(8,128)(2,1)S(1)} custom-call(bf16[32,3712]{1,0:T(8,128)(2,1)S(1)} %join.3.refs_0_.refs_1_, bf16[32,3712]{1,0:T(8,128)(2,1)S(1)} %collective-permute-done.4.refs_1_.refs_2_, bf16[1,3584,2048]{2,1,0:T(8,128)(2,1)S(1)} %copy-done, bf16[1,3584,2048]{2,1,0:T(8,128)(2,1)S(1)} %copy-done.1), custom_call_target="tpu_custom_call" | custom-call | tf_op jit(solution)/shard_map/hidden/pallas_call | solution.py:220
  21.4 0.0 slice-done
  21.4 0.0 slice-done.1
  21.4 0.0 slice-done.2
  21.4 2.1 %down.1 = (f32[32,3584]{1,0:T(8,128)S(1)}, bf16[32,3584]{1,0:T(8,128)(2,1)S(1)}) custom-call(bf16[64,2048]{1,0:T(8,128)(2,1)S(1)} %hidden.1.refs_0_, bf16[32,3712]{1,0:T(8,128)(2,1)S(1)} %join.3.refs_0_.refs_1_, bf16[32,3712]{1,0:T(8,128)(2,1)S(1)} %collective-permute-done.4.refs_1_.refs_2_, bf16[1,2048,3584]{2,1,0:T(8,128)(2,1)S(1)} %bitcast.1), custom_call_target="tpu_custom_call" | custom-call | tf_op jit(solution)/shard_map/down/pallas_call | solution.py:228
  23.5 0.2 collective-permute-start.5
  23.7 1.4 %collective-permute-done.5.got_ref = bf16[32,3584]{1,0:T(8,128)(2,1)S(1)} collective-permute-done((bf16[32,3584]{1,0:T(8,128)(2,1)S(1)}, bf16[32,3584]{1,0:T(8,128)(2,1)S(1)}, u32[]{:S(2)}, u32[]{:S(2)}) %collective-permute-start.5) | collective-permute-done | bytes 229408 | tf_op jit(solution)/shard_map/ppermute | solution.py:79
  25.1 0.7 %collective-permute-start.6 = (bf16[8,3584]{1,0:T(8,128)(2,1)S(1)}, bf16[8,3584]{1,0:T(8,128)(2,1)S(1)}, u32[]{:S(2)}, u32[]{:S(2)}) collective-permute-start(bf16[8,3584]{1,0:T(8,128)(2,1)S(1)} %get-tuple-element.16), channel_id=1, source_target_pairs={{0,6},{1,7},{2,4},{3,5},{4,2},{5,3},{6,0},{7,1},{8,14},{9,15},{10,... | collective-permute-start | bytes 172040 | tf_op jit(solution)/shard_map/ppermute | solution.py:79
  25.8 1.4 %collective-permute-start.7 = (bf16[8,3584]{1,0:T(8,128)(2,1)S(1)}, bf16[8,3584]{1,0:T(8,128)(2,1)S(1)}, u32[]{:S(2)}, u32[]{:S(2)}) collective-permute-start(bf16[8,3584]{1,0:T(8,128)(2,1)S(1)} %get-tuple-element.17), channel_id=1, source_target_pairs={{0,4},{1,5},{2,6},{3,7},{4,0},{5,1},{6,2},{7,3},{8,12},{9,13},{10,... | collective-permute-start | bytes 172040 | tf_op jit(solution)/shard_map/ppermute | solution.py:79
  27.2 1.5 %collective-permute-start.8 = (bf16[8,3584]{1,0:T(8,128)(2,1)S(1)}, bf16[8,3584]{1,0:T(8,128)(2,1)S(1)}, u32[]{:S(2)}, u32[]{:S(2)}) collective-permute-start(bf16[8,3584]{1,0:T(8,128)(2,1)S(1)} %get-tuple-element.18), channel_id=1, source_target_pairs={{0,2},{1,3},{2,0},{3,1},{4,6},{5,7},{6,4},{7,5},{8,10},{9,11},{10,... | collective-permute-start | bytes 172040 | tf_op jit(solution)/shard_map/ppermute | solution.py:79
  28.7 2.0 %collective-permute-done.6.refs_0_ = bf16[8,3584]{1,0:T(8,128)(2,1)S(1)} collective-permute-done((bf16[8,3584]{1,0:T(8,128)(2,1)S(1)}, bf16[8,3584]{1,0:T(8,128)(2,1)S(1)}, u32[]{:S(2)}, u32[]{:S(2)}) %collective-permute-start.6) | collective-permute-done | bytes 57376 | tf_op jit(solution)/shard_map/ppermute | solution.py:79
  30.7 0.0 collective-permute-done.7.refs_1_
  30.7 0.7 %collective-permute-done.8.refs_2_ = bf16[8,3584]{1,0:T(8,128)(2,1)S(1)} collective-permute-done((bf16[8,3584]{1,0:T(8,128)(2,1)S(1)}, bf16[8,3584]{1,0:T(8,128)(2,1)S(1)}, u32[]{:S(2)}, u32[]{:S(2)}) %collective-permute-start.8) | collective-permute-done | bytes 57376 | tf_op jit(solution)/shard_map/ppermute | solution.py:79
  31.4 2.9 %collective-permute-start.9 = (bf16[4,3584]{1,0:T(4,128)(2,1)S(1)}, bf16[4,3584]{1,0:T(4,128)(2,1)S(1)}, u32[]{:S(2)}, u32[]{:S(2)}) collective-permute-start(bf16[4,3584]{1,0:T(4,128)(2,1)S(1)} %get-tuple-element.20), channel_id=1, source_target_pairs={{0,8},{1,9},{2,10},{3,11},{4,12},{5,13},{6,14},{7,15},{8,0},{9,1},... | collective-permute-start | bytes 86024 | tf_op jit(solution)/shard_map/ppermute | solution.py:79
  34.3 2.3 %collective-permute-done.9.got_ref = bf16[4,3584]{1,0:T(4,128)(2,1)S(1)} collective-permute-done((bf16[4,3584]{1,0:T(4,128)(2,1)S(1)}, bf16[4,3584]{1,0:T(4,128)(2,1)S(1)}, u32[]{:S(2)}, u32[]{:S(2)}) %collective-permute-start.9) | collective-permute-done | bytes 28704 | tf_op jit(solution)/shard_map/ppermute | solution.py:79
  36.5 0.6 %last.1 = bf16[4,3584]{1,0:T(4,128)(2,1)} custom-call(f32[4,3584]{1,0:T(4,128)S(1)} %get-tuple-element.19.kept_ref, bf16[4,3584]{1,0:T(4,128)(2,1)S(1)} %collective-permute-done.9.got_ref), custom_call_target="tpu_custom_call" | custom-call | tf_op jit(solution)/shard_map/last/pallas_call | solution.py:262
  (9 shorter events, 0.1 us)
Async XLA Ops:
  0.0 17.2 %copy-start.1 = (bf16[1,3584,2048]{2,1,0:T(8,128)(2,1)S(1)}, bf16[1,3584,2048]{2,1,0:T(8,128)(2,1)}, u32[]{:S(2)}) copy-start(bf16[1,3584,2048]{2,1,0:T(8,128)(2,1)} %refs_3_.2) | copy-start | bytes 44040196
  0.0 17.2 %copy-start = (bf16[1,3584,2048]{2,1,0:T(8,128)(2,1)S(1)}, bf16[1,3584,2048]{2,1,0:T(8,128)(2,1)}, u32[]{:S(2)}) copy-start(bf16[1,3584,2048]{2,1,0:T(8,128)(2,1)} %refs_2_.3) | copy-start | bytes 44040196
  1.1 6.3 %collective-permute-start = (bf16[4,3712]{1,0:T(4,128)(2,1)S(1)}, bf16[4,3712]{1,0:T(4,128)(2,1)S(1)}, u32[]{:S(2)}, u32[]{:S(2)}) collective-permute-start(bf16[4,3712]{1,0:T(4,128)(2,1)S(1)} %pack.1.refs_0_), channel_id=1, source_target_pairs={{0,8},{1,9},{2,10},{3,11},{4,12},{5,13},{6,14},{7,15},{8,0},{9,1},... | collective-permute-start | bytes 89096 | tf_op jit(solution)/shard_map/ppermute | solution.py:79
  7.4 4.3 %collective-permute-start.3 = (bf16[8,3712]{1,0:T(8,128)(2,1)S(1)}, bf16[8,3712]{1,0:T(8,128)(2,1)S(1)}, u32[]{:S(2)}, u32[]{:S(2)}) collective-permute-start(bf16[8,3712]{1,0:T(8,128)(2,1)S(1)} %join.2.refs_0_), channel_id=1, source_target_pairs={{0,2},{1,3},{2,0},{3,1},{4,6},{5,7},{6,4},{7,5},{8,10},{9,11},{10,... | collective-permute-start | bytes 178184 | tf_op jit(solution)/shard_map/ppermute | solution.py:79
  9.1 4.2 %collective-permute-start.2 = (bf16[8,3712]{1,0:T(8,128)(2,1)S(1)}, bf16[8,3712]{1,0:T(8,128)(2,1)S(1)}, u32[]{:S(2)}, u32[]{:S(2)}) collective-permute-start(bf16[8,3712]{1,0:T(8,128)(2,1)S(1)} %join.2.refs_0_), channel_id=1, source_target_pairs={{0,4},{1,5},{2,6},{3,7},{4,0},{5,1},{6,2},{7,3},{8,12},{9,13},{10,... | collective-permute-start | bytes 178184 | tf_op jit(solution)/shard_map/ppermute | solution.py:79
  10.5 5.1 %collective-permute-start.1 = (bf16[8,3712]{1,0:T(8,128)(2,1)S(1)}, bf16[8,3712]{1,0:T(8,128)(2,1)S(1)}, u32[]{:S(2)}, u32[]{:S(2)}) collective-permute-start(bf16[8,3712]{1,0:T(8,128)(2,1)S(1)} %join.2.refs_0_), channel_id=1, source_target_pairs={{0,6},{1,7},{2,4},{3,5},{4,2},{5,3},{6,0},{7,1},{8,14},{9,15},{10,... | collective-permute-start | bytes 178184 | tf_op jit(solution)/shard_map/ppermute | solution.py:79
  15.6 5.8 %slice-start = ((s8[14680064]{0:T(1024)(128)(4,1)}), s8[4194304]{0:T(1024)(128)(4,1)S(1)}, s32[]{:S(2)}) async-start(s8[14680064]{0:T(1024)(128)(4,1)} %bitcast), calls=%async_computation | async-start | bytes 8388608
  15.6 5.7 %slice-start.1 = ((s8[14680064]{0:T(1024)(128)(4,1)}), s8[4194304]{0:T(1024)(128)(4,1)S(1)}, s32[]{:S(2)}) async-start(s8[14680064]{0:T(1024)(128)(4,1)} %bitcast), calls=%async_computation.1 | async-start | bytes 8388608
  15.7 5.7 %slice-start.2 = ((s8[14680064]{0:T(1024)(128)(4,1)}), s8[4194304]{0:T(1024)(128)(4,1)S(1)}, s32[]{:S(2)}) async-start(s8[14680064]{0:T(1024)(128)(4,1)} %bitcast), calls=%async_computation.2 | async-start | bytes 8388608
  15.7 5.7 %slice-start.3 = ((s8[14680064]{0:T(1024)(128)(4,1)}), s8[2097152]{0:T(1024)(128)(4,1)S(1)}, s32[]{:S(2)}) async-start(s8[14680064]{0:T(1024)(128)(4,1)} %bitcast), calls=%async_computation.3 | async-start | bytes 4194304
  15.7 1.6 %collective-permute-start.4 = (bf16[32,3712]{1,0:T(8,128)(2,1)S(1)}, bf16[32,3712]{1,0:T(8,128)(2,1)S(1)}, u32[]{:S(2)}, u32[]{:S(2)}) collective-permute-start(bf16[32,3712]{1,0:T(8,128)(2,1)S(1)} %join.3.refs_0_.refs_1_), channel_id=1, source_target_pairs={{0,1},{1,0},{2,3},{3,2},{4,5},{5,4},{6,7},{7,6},{8,9},{9,8},{10,11... | collective-permute-start | bytes 712712 | tf_op jit(solution)/shard_map/ppermute | solution.py:79
  23.5 1.6 %collective-permute-start.5 = (bf16[32,3584]{1,0:T(8,128)(2,1)S(1)}, bf16[32,3584]{1,0:T(8,128)(2,1)S(1)}, u32[]{:S(2)}, u32[]{:S(2)}) collective-permute-start(bf16[32,3584]{1,0:T(8,128)(2,1)S(1)} %get-tuple-element.14), channel_id=1, source_target_pairs={{0,1},{1,0},{2,3},{3,2},{4,5},{5,4},{6,7},{7,6},{8,9},{9,8},{10,11... | collective-permute-start | bytes 688136 | tf_op jit(solution)/shard_map/ppermute | solution.py:79
  25.1 5.5 %collective-permute-start.6 = (bf16[8,3584]{1,0:T(8,128)(2,1)S(1)}, bf16[8,3584]{1,0:T(8,128)(2,1)S(1)}, u32[]{:S(2)}, u32[]{:S(2)}) collective-permute-start(bf16[8,3584]{1,0:T(8,128)(2,1)S(1)} %get-tuple-element.16), channel_id=1, source_target_pairs={{0,6},{1,7},{2,4},{3,5},{4,2},{5,3},{6,0},{7,1},{8,14},{9,15},{10,... | collective-permute-start | bytes 172040 | tf_op jit(solution)/shard_map/ppermute | solution.py:79
  25.8 4.8 %collective-permute-start.7 = (bf16[8,3584]{1,0:T(8,128)(2,1)S(1)}, bf16[8,3584]{1,0:T(8,128)(2,1)S(1)}, u32[]{:S(2)}, u32[]{:S(2)}) collective-permute-start(bf16[8,3584]{1,0:T(8,128)(2,1)S(1)} %get-tuple-element.17), channel_id=1, source_target_pairs={{0,4},{1,5},{2,6},{3,7},{4,0},{5,1},{6,2},{7,3},{8,12},{9,13},{10,... | collective-permute-start | bytes 172040 | tf_op jit(solution)/shard_map/ppermute | solution.py:79
  27.2 4.2 %collective-permute-start.8 = (bf16[8,3584]{1,0:T(8,128)(2,1)S(1)}, bf16[8,3584]{1,0:T(8,128)(2,1)S(1)}, u32[]{:S(2)}, u32[]{:S(2)}) collective-permute-start(bf16[8,3584]{1,0:T(8,128)(2,1)S(1)} %get-tuple-element.18), channel_id=1, source_target_pairs={{0,2},{1,3},{2,0},{3,1},{4,6},{5,7},{6,4},{7,5},{8,10},{9,11},{10,... | collective-permute-start | bytes 172040 | tf_op jit(solution)/shard_map/ppermute | solution.py:79
  31.4 5.1 %collective-permute-start.9 = (bf16[4,3584]{1,0:T(4,128)(2,1)S(1)}, bf16[4,3584]{1,0:T(4,128)(2,1)S(1)}, u32[]{:S(2)}, u32[]{:S(2)}) collective-permute-start(bf16[4,3584]{1,0:T(4,128)(2,1)S(1)} %get-tuple-element.20), channel_id=1, source_target_pairs={{0,8},{1,9},{2,10},{3,11},{4,12},{5,13},{6,14},{7,15},{8,0},{9,1},... | collective-permute-start | bytes 86024 | tf_op jit(solution)/shard_map/ppermute | solution.py:79

commit v3 on v2

--- a/solution.py
+++ b/solution.py
@@ -6,6 +6,7 @@
 from jax.sharding import PartitionSpec as P
 
 LANES = 128
+PARTS = 1
 
 
 def slot_table(ids, count):
@@ -133,10 +134,18 @@
     )(*pieces)
 
 
-def hidden_kernel(step, fill, xa_ref, xb_ref, gate_ref, up_ref, out_ref):
+def hidden_kernel(step, fill, experts, *refs):
+    *x_refs, gate_ref, up_ref, out_ref, weight_ref = refs
     width = gate_ref.shape[1]
     rows = out_ref.shape[0]
-    x = filled(jnp.concatenate([xa_ref[:, :width], xb_ref[:, :width]], axis=0), fill)
+    me = lax.axis_index("expert")
+    spread = jnp.concatenate([ref[:, width:].astype(jnp.float32) for ref in x_refs], axis=0)
+    lane = lax.broadcasted_iota(jnp.int32, spread.shape, 1)
+    mine = (lane == me) | (lane == me + experts)
+    weight = jnp.sum(jnp.where(mine, spread, 0.0), axis=1, keepdims=True)
+    weight_ref[...] = jnp.broadcast_to(weight, weight_ref.shape)
+    x = jnp.concatenate([ref[:, :width].astype(jnp.float32) for ref in x_refs], axis=0)
+    x = filled(x.astype(jnp.bfloat16), fill)
     for start in range(0, gate_ref.shape[2], step):
         cut = slice(start, start + step)
         gate = jnp.dot(x, gate_ref[0, :, cut], preferred_element_type=jnp.float32)[:rows]
@@ -144,29 +153,31 @@
         out_ref[:, cut] = (gate / (1.0 + jnp.exp(-gate)) * up).astype(jnp.bfloat16)
 
 
-def down_kernel(step, fill, experts, hidden_ref, xa_ref, xb_ref, down_ref, keep_ref, send_ref):
-    width = down_ref.shape[2]
-    half = keep_ref.shape[0]
-    me = lax.axis_index("expert")
+def down_kernel(step, fill, base, hidden_ref, weight_ref, down_ref, keep_ref, send_ref):
+    half, width = keep_ref.shape
     hidden = filled(hidden_ref[...], fill)
-    spread = jnp.concatenate([xa_ref[:, width:], xb_ref[:, width:]], axis=0).astype(jnp.float32)
-    lane = lax.broadcasted_iota(jnp.int32, spread.shape, 1)
-    mine = (lane == me) | (lane == me + experts)
-    weight = jnp.sum(jnp.where(mine, spread, 0.0), axis=1, keepdims=True)
+    weight = weight_ref[:, :1]
     for start in range(0, width, step):
         cut = slice(start, start + step)
-        out = jnp.dot(hidden, down_ref[0, :, cut], preferred_element_type=jnp.float32)[: 2 * half]
-        part = out.astype(jnp.bfloat16).astype(jnp.float32) * weight
+        columns = slice(base + start, base + start + step)
+        out = jnp.dot(hidden, down_ref[0, :, columns], preferred_element_type=jnp.float32)
+        part = out[: 2 * half].astype(jnp.bfloat16).astype(jnp.float32) * weight
         keep_ref[:, cut] = part[:half]
         send_ref[:, cut] = part[half:].astype(send_ref.dtype)
 
 
-def first_add_kernel(kept_ref, got_ref, keep_ref, *send_refs):
-    total = kept_ref[...] + got_ref[...].astype(jnp.float32)
+def first_add_kernel(parts, *refs):
+    kept_refs, got_refs = refs[:parts], refs[parts : 2 * parts]
+    keep_ref, *send_refs = refs[2 * parts :]
     rows = keep_ref.shape[0]
-    keep_ref[...] = total[:rows]
-    for i, send_ref in enumerate(send_refs):
-        send_ref[...] = total[(i + 1) * rows : (i + 2) * rows].astype(send_ref.dtype)
+    base = 0
+    for kept_ref, got_ref in zip(kept_refs, got_refs):
+        cut = slice(base, base + kept_ref.shape[1])
+        base += kept_ref.shape[1]
+        total = kept_ref[...] + got_ref[...].astype(jnp.float32)
+        keep_ref[:, cut] = total[:rows]
+        for i, send_ref in enumerate(send_refs):
+            send_ref[:, cut] = total[(i + 1) * rows : (i + 2) * rows].astype(send_ref.dtype)
 
 
 def second_add_kernel(kept_ref, *refs):
@@ -188,7 +199,7 @@
     rows, width = tokens.shape
     units = gate_w.shape[2]
     far = experts // 2
-    middle = [d for d in range(far - 2, 0, -2)]
+    middle = [d for d in range(2, far, 2)]
     half = rows * far
     fill = max(2 * half, 128)
     params = pltpu.CompilerParams(vmem_limit_bytes=6 * 2**20)
@@ -215,38 +226,50 @@
         name="pack",
     )(tokens, expert_ids, scores)
     near = join([packed, swap(packed, far)], params)
-    held = join([near] + [swap(near, d) for d in middle], params)
-    other = swap(held, 1)
-    hidden = pl.pallas_call(
-        lambda *refs: hidden_kernel(256, fill, *refs),
-        out_shape=jax.ShapeDtypeStruct((2 * half, units), jnp.bfloat16),
-        in_specs=vmem(4),
-        out_specs=vmem(1)[0],
+    pieces = [near] + [swap(near, d) for d in middle]
+    pieces = pieces + [swap(piece, 1) for piece in pieces]
+    hidden, weight = pl.pallas_call(
+        lambda *refs: hidden_kernel(256, fill, experts, *refs),
+        out_shape=[
+            jax.ShapeDtypeStruct((2 * half, units), jnp.bfloat16),
+            jax.ShapeDtypeStruct((2 * half, LANES), jnp.float32),
+        ],
+        in_specs=vmem(len(pieces) + 2),
+        out_specs=vmem(2),
         compiler_params=params,
         name="hidden",
-    )(held, other, gate_w, up_w)
-    keep, send = pl.pallas_call(
-        lambda *refs: down_kernel(256, fill, experts, *refs),
-        out_shape=[
-            jax.ShapeDtypeStruct((half, width), jnp.float32),
-            jax.ShapeDtypeStruct((half, width), jnp.bfloat16),
-        ],
-        in_specs=vmem(4),
-        out_specs=vmem(2),
-        compiler_params=params,
-        name="down",
-    )(hidden, held, other, down_w)
-    got = swap(send, 1)
+    )(*pieces, gate_w, up_w)
+    parts = PARTS
+    keeps, gots = [], []
+    for part in range(parts):
+        keep, send = pl.pallas_call(
+            lambda *refs: down_kernel(256, fill, part * width // parts, *refs),
+            out_shape=[
+                jax.ShapeDtypeStruct((half, width // parts), jnp.float32),
+                jax.ShapeDtypeStruct((half, width // parts), jnp.bfloat16),
+            ],
+            in_specs=vmem(3),
+            out_specs=vmem(2),
+            compiler_params=params,
+            cost_estimate=pl.CostEstimate(
+                flops=2 * fill * units * width // parts,
+                bytes_accessed=2 * units * width // parts,
+                transcendentals=0,
+            ),
+            name="down",
+        )(hidden, weight, down_w)
+        keeps.append(keep)
+        gots.append(swap(send, 1))
     keep, *sends = pl.pallas_call(
-        first_add_kernel,
+        lambda *refs: first_add_kernel(parts, *refs),
         out_shape=[jax.ShapeDtypeStruct((2 * rows, width), jnp.float32)]
         + [jax.ShapeDtypeStruct((2 * rows, width), jnp.bfloat16)] * len(middle),
-        in_specs=vmem(2),
+        in_specs=vmem(2 * parts),
         out_specs=vmem(1 + len(middle)),
         compiler_params=params,
         name="first_add",
-    )(keep, got)
-    gots = [swap(send, d) for send, d in zip(sends, middle)]
+    )(*keeps, *gots)
+    gots = [swap(send, d) for send, d in list(zip(sends, middle))[::-1]]
     keep, send = pl.pallas_call(
         second_add_kernel,
         out_shape=[

time: 37.3 us -> 35.7 us (0.957)
  waiting for transfers between devices: 14.7 us -> 13.5 us
    ppermute x10 -> x13, waiting for transfers between devices: 14.7 us -> 13.5 us  [swap(): return lax.ppermute(x, 'expert', [(i, i ^ distance) for i in range(count)])]
    ppermute x10 -> x13, starting transfers between devices: 14.3 us -> 14 us  [swap(): return lax.ppermute(x, 'expert', [(i, i ^ distance) for i in range(count)])]
  transfers between devices with their start and end apart: 10 -> 13, of which waited for: 9 -> 11; matrix products, arithmetic and copies ran while one was open for 0% -> 0% of each run, Pallas kernels for 0% -> 0%
where the time goes in v3:
time: 35.7 us; the launch traced here: 35.6 us
  starting transfers between devices  14 us (39%)
  waiting for transfers between devices  13.5 us (38%)
  Pallas kernels  7.96 us (22%)
    ppermute x13, starting transfers between devices, swap(): return lax.ppermute(x, 'expert', [(i, i ^ distance) for i in range(count)])  14 us
    ppermute x13, waiting for transfers between devices, swap(): return lax.ppermute(x, 'expert', [(i, i ^ distance) for i in range(count)])  13.5 us
    pallas_call x1, Pallas kernels, shards(): pl.pallas_call(lambda *refs: hidden_kernel(256, fill, experts, *refs), ou...  4.08 us
    pallas_call x1, Pallas kernels, shards(): pl.pallas_call(lambda *refs: down_kernel(256, fill, part * width // parts...  2.08 us
    pallas_call x1, Pallas kernels, shards(): pl.pallas_call(lambda *refs: pack_kernel(experts, *refs), out_shape=jax.S...  1.06 us
  transfers between devices with their start and end apart: 13, of which 11 were waited for; matrix products, arithmetic and copies ran while one was open for 0% of the time, Pallas kernels for 0%

profile of v3, /device:TPU:0, one launch (start us, length us, event | category | flops | bytes accessed | tf_op | source)
XLA Modules:
  0.0 35.6 jit_solution(2346727524334396731)
XLA Ops:
  0.0 1.1 %pack.1.refs_0_ = bf16[4,3712]{1,0:T(4,128)(2,1)S(1)} custom-call(bf16[4,3584]{1,0:T(4,128)(2,1)} %refs_0_.1, s32[4,8]{1,0:T(4,128)} %refs_1_.1, f32[4,8]{1,0:T(4,128)} %refs_2_.2), custom_call_target="tpu_custom_call" | custom-call | flops 40000000000 | bytes 100000000 | tf_op jit(solution)/shard_map/pack/pallas_call | solution.py:212
  1.1 4.1 %collective-permute-start = (bf16[4,3712]{1,0:T(4,128)(2,1)S(1)}, bf16[4,3712]{1,0:T(4,128)(2,1)S(1)}, u32[]{:S(2)}, u32[]{:S(2)}) collective-permute-start(bf16[4,3712]{1,0:T(4,128)(2,1)S(1)} %pack.1.refs_0_), channel_id=1, source_target_pairs={{0,8},{1,9},{2,10},{3,11},{4,12},{5,13},{6,14},{7,15},{8,0},{9,1},... | collective-permute-start | bytes 89096 | tf_op jit(solution)/shard_map/ppermute | solution.py:80
  5.2 2.2 %collective-permute-done.refs_1_ = bf16[4,3712]{1,0:T(4,128)(2,1)S(1)} collective-permute-done((bf16[4,3712]{1,0:T(4,128)(2,1)S(1)}, bf16[4,3712]{1,0:T(4,128)(2,1)S(1)}, u32[]{:S(2)}, u32[]{:S(2)}) %collective-permute-start) | collective-permute-done | bytes 29728 | tf_op jit(solution)/shard_map/ppermute | solution.py:80
  7.4 0.0 slice-start.1
  7.4 0.0 slice-start.2
  7.4 0.0 slice-start.3
  7.4 2.6 %collective-permute-start.3 = (bf16[8,3712]{1,0:T(8,128)(2,1)S(1)}, bf16[8,3712]{1,0:T(8,128)(2,1)S(1)}, u32[]{:S(2)}, u32[]{:S(2)}) collective-permute-start(bf16[8,3712]{1,0:T(8,128)(2,1)S(1)} %join.1.refs_0_), channel_id=1, source_target_pairs={{0,6},{1,7},{2,4},{3,5},{4,2},{5,3},{6,0},{7,1},{8,14},{9,15},{10,... | collective-permute-start | bytes 178184 | tf_op jit(solution)/shard_map/ppermute | solution.py:80
  10.0 0.6 %collective-permute-start.2 = (bf16[8,3712]{1,0:T(8,128)(2,1)S(1)}, bf16[8,3712]{1,0:T(8,128)(2,1)S(1)}, u32[]{:S(2)}, u32[]{:S(2)}) collective-permute-start(bf16[8,3712]{1,0:T(8,128)(2,1)S(1)} %join.1.refs_0_), channel_id=1, source_target_pairs={{0,4},{1,5},{2,6},{3,7},{4,0},{5,1},{6,2},{7,3},{8,12},{9,13},{10,... | collective-permute-start | bytes 178184 | tf_op jit(solution)/shard_map/ppermute | solution.py:80
  10.6 0.3 collective-permute-start.1
  11.0 0.0 collective-permute-start.4
  11.0 1.6 %collective-permute-done.3.refs_3_ = bf16[8,3712]{1,0:T(8,128)(2,1)S(1)} collective-permute-done((bf16[8,3712]{1,0:T(8,128)(2,1)S(1)}, bf16[8,3712]{1,0:T(8,128)(2,1)S(1)}, u32[]{:S(2)}, u32[]{:S(2)}) %collective-permute-start.3) | collective-permute-done | bytes 59424 | tf_op jit(solution)/shard_map/ppermute | solution.py:80
  12.6 1.6 %collective-permute-done.2.refs_2_ = bf16[8,3712]{1,0:T(8,128)(2,1)S(1)} collective-permute-done((bf16[8,3712]{1,0:T(8,128)(2,1)S(1)}, bf16[8,3712]{1,0:T(8,128)(2,1)S(1)}, u32[]{:S(2)}, u32[]{:S(2)}) %collective-permute-start.2) | collective-permute-done | bytes 59424 | tf_op jit(solution)/shard_map/ppermute | solution.py:80
  14.2 0.6 %collective-permute-done.1.refs_1_ = bf16[8,3712]{1,0:T(8,128)(2,1)S(1)} collective-permute-done((bf16[8,3712]{1,0:T(8,128)(2,1)S(1)}, bf16[8,3712]{1,0:T(8,128)(2,1)S(1)}, u32[]{:S(2)}, u32[]{:S(2)}) %collective-permute-start.1) | collective-permute-done | bytes 59424 | tf_op jit(solution)/shard_map/ppermute | solution.py:80
  14.8 0.0 collective-permute-start.5
  14.8 0.0 collective-permute-done.4.refs_4_
  14.8 0.0 collective-permute-done.7.refs_7_
  14.9 0.6 %collective-permute-done.6.refs_6_ = bf16[8,3712]{1,0:T(8,128)(2,1)S(1)} collective-permute-done((bf16[8,3712]{1,0:T(8,128)(2,1)S(1)}, bf16[8,3712]{1,0:T(8,128)(2,1)S(1)}, u32[]{:S(2)}, u32[]{:S(2)}) %collective-permute-start.6) | collective-permute-done | bytes 59424 | tf_op jit(solution)/shard_map/ppermute | solution.py:80
  15.4 0.6 %collective-permute-done.5.refs_5_ = bf16[8,3712]{1,0:T(8,128)(2,1)S(1)} collective-permute-done((bf16[8,3712]{1,0:T(8,128)(2,1)S(1)}, bf16[8,3712]{1,0:T(8,128)(2,1)S(1)}, u32[]{:S(2)}, u32[]{:S(2)}) %collective-permute-start.5) | collective-permute-done | bytes 59424 | tf_op jit(solution)/shard_map/ppermute | solution.py:80
  16.1 4.1 %hidden.1 = (bf16[64,2048]{1,0:T(8,128)(2,1)S(1)}, f32[64,128]{1,0:T(8,128)S(1)}) custom-call(bf16[8,3712]{1,0:T(8,128)(2,1)S(1)} %join.1.refs_0_, bf16[8,3712]{1,0:T(8,128)(2,1)S(1)} %collective-permute-done.1.refs_1_, bf16[8,3712]{1,0:T(8,128)(2,1)S(1)} %collective-permute-done.2.refs_2_, bf16[8,3712]{1,0:T(8,128)(2,1)S(1)} %collective-permute-done.3.refs_3_, ...), custom_call_target="tpu_custom_call" | custom-call | tf_op jit(solution)/shard_map/hidden/pallas_call | solution.py:231
  20.2 2.1 %down.1 = (f32[32,3584]{1,0:T(8,128)S(1)}, bf16[32,3584]{1,0:T(8,128)(2,1)S(1)}) custom-call(bf16[64,2048]{1,0:T(8,128)(2,1)S(1)} %get-tuple-element.15.refs_0_, f32[64,128]{1,0:T(8,128)S(1)} %get-tuple-element.16.refs_1_, bf16[1,2048,3584]{2,1,0:T(8,128)(2,1)S(1)} %bitcast.1), custom_call_target="tpu_custom_call" | custom-call | flops 1879048192 | bytes 14680064 | tf_op jit(solution)/shard_map/down/pallas_call | solution.py:245
  22.3 0.2 collective-permute-start.8
  22.5 1.3 %collective-permute-done.8.refs_1_ = bf16[32,3584]{1,0:T(8,128)(2,1)S(1)} collective-permute-done((bf16[32,3584]{1,0:T(8,128)(2,1)S(1)}, bf16[32,3584]{1,0:T(8,128)(2,1)S(1)}, u32[]{:S(2)}, u32[]{:S(2)}) %collective-permute-start.8) | collective-permute-done | bytes 229408 | tf_op jit(solution)/shard_map/ppermute | solution.py:80
  23.9 0.1 first_add.1
  23.9 1.4 %collective-permute-start.9 = (bf16[8,3584]{1,0:T(8,128)(2,1)S(1)}, bf16[8,3584]{1,0:T(8,128)(2,1)S(1)}, u32[]{:S(2)}, u32[]{:S(2)}) collective-permute-start(bf16[8,3584]{1,0:T(8,128)(2,1)S(1)} %get-tuple-element.20), channel_id=1, source_target_pairs={{0,6},{1,7},{2,4},{3,5},{4,2},{5,3},{6,0},{7,1},{8,14},{9,15},{10,... | collective-permute-start | bytes 172040 | tf_op jit(solution)/shard_map/ppermute | solution.py:80
  25.4 0.4 %collective-permute-start.10 = (bf16[8,3584]{1,0:T(8,128)(2,1)S(1)}, bf16[8,3584]{1,0:T(8,128)(2,1)S(1)}, u32[]{:S(2)}, u32[]{:S(2)}) collective-permute-start(bf16[8,3584]{1,0:T(8,128)(2,1)S(1)} %get-tuple-element.21), channel_id=1, source_target_pairs={{0,4},{1,5},{2,6},{3,7},{4,0},{5,1},{6,2},{7,3},{8,12},{9,13},{10,... | collective-permute-start | bytes 172040 | tf_op jit(solution)/shard_map/ppermute | solution.py:80
  25.8 1.7 %collective-permute-start.11 = (bf16[8,3584]{1,0:T(8,128)(2,1)S(1)}, bf16[8,3584]{1,0:T(8,128)(2,1)S(1)}, u32[]{:S(2)}, u32[]{:S(2)}) collective-permute-start(bf16[8,3584]{1,0:T(8,128)(2,1)S(1)} %get-tuple-element.22), channel_id=1, source_target_pairs={{0,2},{1,3},{2,0},{3,1},{4,6},{5,7},{6,4},{7,5},{8,10},{9,11},{10,... | collective-permute-start | bytes 172040 | tf_op jit(solution)/shard_map/ppermute | solution.py:80
  27.5 1.9 %collective-permute-done.9.refs_0_ = bf16[8,3584]{1,0:T(8,128)(2,1)S(1)} collective-permute-done((bf16[8,3584]{1,0:T(8,128)(2,1)S(1)}, bf16[8,3584]{1,0:T(8,128)(2,1)S(1)}, u32[]{:S(2)}, u32[]{:S(2)}) %collective-permute-start.9) | collective-permute-done | bytes 57376 | tf_op jit(solution)/shard_map/ppermute | solution.py:80
  29.4 0.1 collective-permute-done.10.refs_1_
  29.5 0.6 %collective-permute-done.11.refs_2_ = bf16[8,3584]{1,0:T(8,128)(2,1)S(1)} collective-permute-done((bf16[8,3584]{1,0:T(8,128)(2,1)S(1)}, bf16[8,3584]{1,0:T(8,128)(2,1)S(1)}, u32[]{:S(2)}, u32[]{:S(2)}) %collective-permute-start.11) | collective-permute-done | bytes 57376 | tf_op jit(solution)/shard_map/ppermute | solution.py:80
  30.1 2.6 %collective-permute-start.12 = (bf16[4,3584]{1,0:T(4,128)(2,1)S(1)}, bf16[4,3584]{1,0:T(4,128)(2,1)S(1)}, u32[]{:S(2)}, u32[]{:S(2)}) collective-permute-start(bf16[4,3584]{1,0:T(4,128)(2,1)S(1)} %get-tuple-element.24), channel_id=1, source_target_pairs={{0,8},{1,9},{2,10},{3,11},{4,12},{5,13},{6,14},{7,15},{8,0},{9,1},... | collective-permute-start | bytes 86024 | tf_op jit(solution)/shard_map/ppermute | solution.py:80
  32.7 2.3 %collective-permute-done.12.got_ref = bf16[4,3584]{1,0:T(4,128)(2,1)S(1)} collective-permute-done((bf16[4,3584]{1,0:T(4,128)(2,1)S(1)}, bf16[4,3584]{1,0:T(4,128)(2,1)S(1)}, u32[]{:S(2)}, u32[]{:S(2)}) %collective-permute-start.12) | collective-permute-done | bytes 28704 | tf_op jit(solution)/shard_map/ppermute | solution.py:80
  35.0 0.6 %last.1 = bf16[4,3584]{1,0:T(4,128)(2,1)} custom-call(f32[4,3584]{1,0:T(4,128)S(1)} %get-tuple-element.23.kept_ref, bf16[4,3584]{1,0:T(4,128)(2,1)S(1)} %collective-permute-done.12.got_ref), custom_call_target="tpu_custom_call" | custom-call | tf_op jit(solution)/shard_map/last/pallas_call | solution.py:285
  (14 shorter events, 0.1 us)
Async XLA Ops:
  0.0 16.1 %copy-start.1 = (bf16[1,3584,2048]{2,1,0:T(8,128)(2,1)S(1)}, bf16[1,3584,2048]{2,1,0:T(8,128)(2,1)}, u32[]{:S(2)}) copy-start(bf16[1,3584,2048]{2,1,0:T(8,128)(2,1)} %refs_9_.1) | copy-start | bytes 44040196
  0.0 16.1 %copy-start = (bf16[1,3584,2048]{2,1,0:T(8,128)(2,1)S(1)}, bf16[1,3584,2048]{2,1,0:T(8,128)(2,1)}, u32[]{:S(2)}) copy-start(bf16[1,3584,2048]{2,1,0:T(8,128)(2,1)} %refs_8_.1) | copy-start | bytes 44040196
  1.1 6.3 %collective-permute-start = (bf16[4,3712]{1,0:T(4,128)(2,1)S(1)}, bf16[4,3712]{1,0:T(4,128)(2,1)S(1)}, u32[]{:S(2)}, u32[]{:S(2)}) collective-permute-start(bf16[4,3712]{1,0:T(4,128)(2,1)S(1)} %pack.1.refs_0_), channel_id=1, source_target_pairs={{0,8},{1,9},{2,10},{3,11},{4,12},{5,13},{6,14},{7,15},{8,0},{9,1},... | collective-permute-start | bytes 89096 | tf_op jit(solution)/shard_map/ppermute | solution.py:80
  7.4 12.8 %slice-start = ((s8[14680064]{0:T(1024)(128)(4,1)}), s8[4194304]{0:T(1024)(128)(4,1)S(1)}, s32[]{:S(2)}) async-start(s8[14680064]{0:T(1024)(128)(4,1)} %bitcast), calls=%async_computation | async-start | bytes 8388608
  7.4 12.8 %slice-start.1 = ((s8[14680064]{0:T(1024)(128)(4,1)}), s8[4194304]{0:T(1024)(128)(4,1)S(1)}, s32[]{:S(2)}) async-start(s8[14680064]{0:T(1024)(128)(4,1)} %bitcast), calls=%async_computation.1 | async-start | bytes 8388608
  7.4 12.8 %slice-start.2 = ((s8[14680064]{0:T(1024)(128)(4,1)}), s8[4194304]{0:T(1024)(128)(4,1)S(1)}, s32[]{:S(2)}) async-start(s8[14680064]{0:T(1024)(128)(4,1)} %bitcast), calls=%async_computation.2 | async-start | bytes 8388608
  7.4 12.8 %slice-start.3 = ((s8[14680064]{0:T(1024)(128)(4,1)}), s8[2097152]{0:T(1024)(128)(4,1)S(1)}, s32[]{:S(2)}) async-start(s8[14680064]{0:T(1024)(128)(4,1)} %bitcast), calls=%async_computation.3 | async-start | bytes 4194304
  7.4 5.2 %collective-permute-start.3 = (bf16[8,3712]{1,0:T(8,128)(2,1)S(1)}, bf16[8,3712]{1,0:T(8,128)(2,1)S(1)}, u32[]{:S(2)}, u32[]{:S(2)}) collective-permute-start(bf16[8,3712]{1,0:T(8,128)(2,1)S(1)} %join.1.refs_0_), channel_id=1, source_target_pairs={{0,6},{1,7},{2,4},{3,5},{4,2},{5,3},{6,0},{7,1},{8,14},{9,15},{10,... | collective-permute-start | bytes 178184 | tf_op jit(solution)/shard_map/ppermute | solution.py:80
  10.0 4.2 %collective-permute-start.2 = (bf16[8,3712]{1,0:T(8,128)(2,1)S(1)}, bf16[8,3712]{1,0:T(8,128)(2,1)S(1)}, u32[]{:S(2)}, u32[]{:S(2)}) collective-permute-start(bf16[8,3712]{1,0:T(8,128)(2,1)S(1)} %join.1.refs_0_), channel_id=1, source_target_pairs={{0,4},{1,5},{2,6},{3,7},{4,0},{5,1},{6,2},{7,3},{8,12},{9,13},{10,... | collective-permute-start | bytes 178184 | tf_op jit(solution)/shard_map/ppermute | solution.py:80
  10.6 4.2 %collective-permute-start.1 = (bf16[8,3712]{1,0:T(8,128)(2,1)S(1)}, bf16[8,3712]{1,0:T(8,128)(2,1)S(1)}, u32[]{:S(2)}, u32[]{:S(2)}) collective-permute-start(bf16[8,3712]{1,0:T(8,128)(2,1)S(1)} %join.1.refs_0_), channel_id=1, source_target_pairs={{0,2},{1,3},{2,0},{3,1},{4,6},{5,7},{6,4},{7,5},{8,10},{9,11},{10,... | collective-permute-start | bytes 178184 | tf_op jit(solution)/shard_map/ppermute | solution.py:80
  11.0 3.9 %collective-permute-start.4 = (bf16[8,3712]{1,0:T(8,128)(2,1)S(1)}, bf16[8,3712]{1,0:T(8,128)(2,1)S(1)}, u32[]{:S(2)}, u32[]{:S(2)}) collective-permute-start(bf16[8,3712]{1,0:T(8,128)(2,1)S(1)} %join.1.refs_0_), channel_id=1, source_target_pairs={{0,1},{1,0},{2,3},{3,2},{4,5},{5,4},{6,7},{7,6},{8,9},{9,8},{10,11... | collective-permute-start | bytes 178184 | tf_op jit(solution)/shard_map/ppermute | solution.py:80
  12.6 2.3 %collective-permute-start.7 = (bf16[8,3712]{1,0:T(8,128)(2,1)S(1)}, bf16[8,3712]{1,0:T(8,128)(2,1)S(1)}, u32[]{:S(2)}, u32[]{:S(2)}) collective-permute-start(bf16[8,3712]{1,0:T(8,128)(2,1)S(1)} %collective-permute-done.3.refs_3_), channel_id=1, source_target_pairs={{0,1},{1,0},{2,3},{3,2},{4,5},{5,4},{6,7},{7,6},{8,9},{9,8},{10,11... | collective-permute-start | bytes 178184 | tf_op jit(solution)/shard_map/ppermute | solution.py:80
  14.2 1.2 %collective-permute-start.6 = (bf16[8,3712]{1,0:T(8,128)(2,1)S(1)}, bf16[8,3712]{1,0:T(8,128)(2,1)S(1)}, u32[]{:S(2)}, u32[]{:S(2)}) collective-permute-start(bf16[8,3712]{1,0:T(8,128)(2,1)S(1)} %collective-permute-done.2.refs_2_), channel_id=1, source_target_pairs={{0,1},{1,0},{2,3},{3,2},{4,5},{5,4},{6,7},{7,6},{8,9},{9,8},{10,11... | collective-permute-start | bytes 178184 | tf_op jit(solution)/shard_map/ppermute | solution.py:80
  14.8 1.2 %collective-permute-start.5 = (bf16[8,3712]{1,0:T(8,128)(2,1)S(1)}, bf16[8,3712]{1,0:T(8,128)(2,1)S(1)}, u32[]{:S(2)}, u32[]{:S(2)}) collective-permute-start(bf16[8,3712]{1,0:T(8,128)(2,1)S(1)} %collective-permute-done.1.refs_1_), channel_id=1, source_target_pairs={{0,1},{1,0},{2,3},{3,2},{4,5},{5,4},{6,7},{7,6},{8,9},{9,8},{10,11... | collective-permute-start | bytes 178184 | tf_op jit(solution)/shard_map/ppermute | solution.py:80
  22.3 1.6 %collective-permute-start.8 = (bf16[32,3584]{1,0:T(8,128)(2,1)S(1)}, bf16[32,3584]{1,0:T(8,128)(2,1)S(1)}, u32[]{:S(2)}, u32[]{:S(2)}) collective-permute-start(bf16[32,3584]{1,0:T(8,128)(2,1)S(1)} %get-tuple-element.18), channel_id=1, source_target_pairs={{0,1},{1,0},{2,3},{3,2},{4,5},{5,4},{6,7},{7,6},{8,9},{9,8},{10,11... | collective-permute-start | bytes 688136 | tf_op jit(solution)/shard_map/ppermute | solution.py:80
  23.9 5.5 %collective-permute-start.9 = (bf16[8,3584]{1,0:T(8,128)(2,1)S(1)}, bf16[8,3584]{1,0:T(8,128)(2,1)S(1)}, u32[]{:S(2)}, u32[]{:S(2)}) collective-permute-start(bf16[8,3584]{1,0:T(8,128)(2,1)S(1)} %get-tuple-element.20), channel_id=1, source_target_pairs={{0,6},{1,7},{2,4},{3,5},{4,2},{5,3},{6,0},{7,1},{8,14},{9,15},{10,... | collective-permute-start | bytes 172040 | tf_op jit(solution)/shard_map/ppermute | solution.py:80
  25.4 4.2 %collective-permute-start.10 = (bf16[8,3584]{1,0:T(8,128)(2,1)S(1)}, bf16[8,3584]{1,0:T(8,128)(2,1)S(1)}, u32[]{:S(2)}, u32[]{:S(2)}) collective-permute-start(bf16[8,3584]{1,0:T(8,128)(2,1)S(1)} %get-tuple-element.21), channel_id=1, source_target_pairs={{0,4},{1,5},{2,6},{3,7},{4,0},{5,1},{6,2},{7,3},{8,12},{9,13},{10,... | collective-permute-start | bytes 172040 | tf_op jit(solution)/shard_map/ppermute | solution.py:80
  25.8 4.3 %collective-permute-start.11 = (bf16[8,3584]{1,0:T(8,128)(2,1)S(1)}, bf16[8,3584]{1,0:T(8,128)(2,1)S(1)}, u32[]{:S(2)}, u32[]{:S(2)}) collective-permute-start(bf16[8,3584]{1,0:T(8,128)(2,1)S(1)} %get-tuple-element.22), channel_id=1, source_target_pairs={{0,2},{1,3},{2,0},{3,1},{4,6},{5,7},{6,4},{7,5},{8,10},{9,11},{10,... | collective-permute-start | bytes 172040 | tf_op jit(solution)/shard_map/ppermute | solution.py:80
  30.1 4.8 %collective-permute-start.12 = (bf16[4,3584]{1,0:T(4,128)(2,1)S(1)}, bf16[4,3584]{1,0:T(4,128)(2,1)S(1)}, u32[]{:S(2)}, u32[]{:S(2)}) collective-permute-start(bf16[4,3584]{1,0:T(4,128)(2,1)S(1)} %get-tuple-element.24), channel_id=1, source_target_pairs={{0,8},{1,9},{2,10},{3,11},{4,12},{5,13},{6,14},{7,15},{8,0},{9,1},... | collective-permute-start | bytes 86024 | tf_op jit(solution)/shard_map/ppermute | solution.py:80

commit v4 on v3

--- a/solution.py
+++ b/solution.py
@@ -6,7 +6,6 @@
 from jax.sharding import PartitionSpec as P
 
 LANES = 128
-PARTS = 1
 
 
 def slot_table(ids, count):
@@ -153,34 +152,24 @@
         out_ref[:, cut] = (gate / (1.0 + jnp.exp(-gate)) * up).astype(jnp.bfloat16)
 
 
-def down_kernel(step, fill, base, hidden_ref, weight_ref, down_ref, keep_ref, send_ref):
-    half, width = keep_ref.shape
+def down_kernel(step, fill, hidden_ref, weight_ref, down_ref, *out_refs):
+    keep_refs, send_refs = out_refs[: len(out_refs) // 2], out_refs[len(out_refs) // 2 :]
     hidden = filled(hidden_ref[...], fill)
     weight = weight_ref[:, :1]
-    for start in range(0, width, step):
+    rows = keep_refs[0].shape[0]
+    for start in range(0, down_ref.shape[2], step):
         cut = slice(start, start + step)
-        columns = slice(base + start, base + start + step)
-        out = jnp.dot(hidden, down_ref[0, :, columns], preferred_element_type=jnp.float32)
-        part = out[: 2 * half].astype(jnp.bfloat16).astype(jnp.float32) * weight
-        keep_ref[:, cut] = part[:half]
-        send_ref[:, cut] = part[half:].astype(send_ref.dtype)
-
-
-def first_add_kernel(parts, *refs):
-    kept_refs, got_refs = refs[:parts], refs[parts : 2 * parts]
-    keep_ref, *send_refs = refs[2 * parts :]
-    rows = keep_ref.shape[0]
-    base = 0
-    for kept_ref, got_ref in zip(kept_refs, got_refs):
-        cut = slice(base, base + kept_ref.shape[1])
-        base += kept_ref.shape[1]
-        total = kept_ref[...] + got_ref[...].astype(jnp.float32)
-        keep_ref[:, cut] = total[:rows]
-        for i, send_ref in enumerate(send_refs):
-            send_ref[:, cut] = total[(i + 1) * rows : (i + 2) * rows].astype(send_ref.dtype)
-
-
-def second_add_kernel(kept_ref, *refs):
+        out = jnp.dot(hidden, down_ref[0, :, cut], preferred_element_type=jnp.float32)
+        part = out[: weight.shape[0]].astype(jnp.bfloat16).astype(jnp.float32) * weight
+        for i, ref in enumerate(keep_refs + send_refs):
+            ref[:, cut] = part[i * rows : (i + 1) * rows].astype(ref.dtype)
+
+
+def add_kernel(kept_ref, got_ref, out_ref):
+    out_ref[...] = (kept_ref[...] + got_ref[...].astype(jnp.float32)).astype(out_ref.dtype)
+
+
+def fold_kernel(kept_ref, *refs):
     got_refs, (keep_ref, send_ref) = refs[:-2], refs[-2:]
     total = kept_ref[...]
     for got_ref in got_refs:
@@ -190,8 +179,15 @@
     send_ref[...] = total[half:].astype(send_ref.dtype)
 
 
-def last_kernel(kept_ref, got_ref, out_ref):
-    out_ref[...] = (kept_ref[...] + got_ref[...].astype(jnp.float32)).astype(out_ref.dtype)
+def add(kept, got, params):
+    return pl.pallas_call(
+        add_kernel,
+        out_shape=jax.ShapeDtypeStruct(got.shape, got.dtype),
+        in_specs=vmem(2),
+        out_specs=vmem(1)[0],
+        compiler_params=params,
+        name="add",
+    )(kept, got)
 
 
 def shards(tokens, expert_ids, scores, gate_w, up_w, down_w):
@@ -239,57 +235,33 @@
         compiler_params=params,
         name="hidden",
     )(*pieces, gate_w, up_w)
-    parts = PARTS
-    keeps, gots = [], []
-    for part in range(parts):
-        keep, send = pl.pallas_call(
-            lambda *refs: down_kernel(256, fill, part * width // parts, *refs),
-            out_shape=[
-                jax.ShapeDtypeStruct((half, width // parts), jnp.float32),
-                jax.ShapeDtypeStruct((half, width // parts), jnp.bfloat16),
-            ],
-            in_specs=vmem(3),
-            out_specs=vmem(2),
-            compiler_params=params,
-            cost_estimate=pl.CostEstimate(
-                flops=2 * fill * units * width // parts,
-                bytes_accessed=2 * units * width // parts,
-                transcendentals=0,
-            ),
-            name="down",
-        )(hidden, weight, down_w)
-        keeps.append(keep)
-        gots.append(swap(send, 1))
-    keep, *sends = pl.pallas_call(
-        lambda *refs: first_add_kernel(parts, *refs),
-        out_shape=[jax.ShapeDtypeStruct((2 * rows, width), jnp.float32)]
-        + [jax.ShapeDtypeStruct((2 * rows, width), jnp.bfloat16)] * len(middle),
-        in_specs=vmem(2 * parts),
-        out_specs=vmem(1 + len(middle)),
-        compiler_params=params,
-        name="first_add",
-    )(*keeps, *gots)
-    gots = [swap(send, d) for send, d in list(zip(sends, middle))[::-1]]
+    count = len(middle) + 1
+    kept_and_sent = pl.pallas_call(
+        lambda *refs: down_kernel(256, fill, *refs),
+        out_shape=[jax.ShapeDtypeStruct((2 * rows, width), jnp.float32)] * count
+        + [jax.ShapeDtypeStruct((2 * rows, width), jnp.bfloat16)] * count,
+        in_specs=vmem(3),
+        out_specs=vmem(2 * count),
+        compiler_params=params,
+        name="down",
+    )(hidden, weight, down_w)
+    kept, sent = kept_and_sent[:count], kept_and_sent[count:]
+    gots = [
+        swap(add(kept[i], swap(sent[i], 1), params), middle[i - 1]) for i in range(count - 1, 0, -1)
+    ]
+    gots.append(swap(sent[0], 1))
     keep, send = pl.pallas_call(
-        second_add_kernel,
+        fold_kernel,
         out_shape=[
             jax.ShapeDtypeStruct((rows, width), jnp.float32),
             jax.ShapeDtypeStruct((rows, width), jnp.bfloat16),
         ],
-        in_specs=vmem(1 + len(middle)),
+        in_specs=vmem(1 + count),
         out_specs=vmem(2),
         compiler_params=params,
-        name="second_add",
-    )(keep, *gots)
-    got = swap(send, far)
-    return pl.pallas_call(
-        last_kernel,
-        out_shape=jax.ShapeDtypeStruct((rows, width), jnp.bfloat16),
-        in_specs=vmem(2),
-        out_specs=vmem(1)[0],
-        compiler_params=params,
-        name="last",
-    )(keep, got)
+        name="fold",
+    )(kept[0], *gots)
+    return add(keep, swap(send, far), params)
 
 
 def solution(mesh):

time: 35.7 us -> 35.5 us (level)
  waiting for transfers between devices: 13.5 us -> 12.1 us
  starting transfers between devices: 14 us -> 15.1 us
    ppermute x13 -> x16, waiting for transfers between devices: 13.5 us -> 12.1 us  [swap(): return lax.ppermute(x, 'expert', [(i, i ^ distance) for i in range(count)])]
    ppermute x13 -> x16, starting transfers between devices: 14 us -> 15.1 us  [swap(): return lax.ppermute(x, 'expert', [(i, i ^ distance) for i in range(count)])]
    pallas_call x4 -> x6, Pallas kernels: 2.8 us -> 2.79 us  [the longest x1 2.08 us: shards(): pl.pallas_call(lambda *refs: down_kernel(256, fill, *refs), out_shape=[ja...]
  transfers between devices with their start and end apart: 13 -> 16, of which waited for: 11 -> 11; matrix products, arithmetic and copies ran while one was open for 0% -> 0% of each run, Pallas kernels for 0% -> 0%
where the time goes in v4:
time: 35.5 us; the launch traced here: 35.4 us
  starting transfers between devices  15.1 us (43%)
  waiting for transfers between devices  12.1 us (34%)
  Pallas kernels  7.96 us (22%)
    ppermute x16, starting transfers between devices, swap(): return lax.ppermute(x, 'expert', [(i, i ^ distance) for i in range(count)])  15.1 us
    ppermute x16, waiting for transfers between devices, swap(): return lax.ppermute(x, 'expert', [(i, i ^ distance) for i in range(count)])  12.1 us
    pallas_call x1, Pallas kernels, shards(): pl.pallas_call(lambda *refs: hidden_kernel(256, fill, experts, *refs), ou...  4.08 us
    pallas_call x1, Pallas kernels, shards(): pl.pallas_call(lambda *refs: down_kernel(256, fill, *refs), out_shape=[ja...  2.08 us
    pallas_call x1, Pallas kernels, shards(): pl.pallas_call(lambda *refs: pack_kernel(experts, *refs), out_shape=jax.S...  1.06 us
  transfers between devices with their start and end apart: 16, of which 11 were waited for; matrix products, arithmetic and copies ran while one was open for 0% of the time, Pallas kernels for 0%

profile of v4, /device:TPU:0, one launch (start us, length us, event | category | flops | bytes accessed | tf_op | source)
XLA Modules:
  0.0 35.4 jit_solution(17879368895882667468)
XLA Ops:
  0.0 1.1 %pack.1.refs_0_ = bf16[4,3712]{1,0:T(4,128)(2,1)S(1)} custom-call(bf16[4,3584]{1,0:T(4,128)(2,1)} %refs_0_.1, s32[4,8]{1,0:T(4,128)} %refs_1_.1, f32[4,8]{1,0:T(4,128)} %refs_2_.2), custom_call_target="tpu_custom_call" | custom-call | flops 40000000000 | bytes 100000000 | tf_op jit(solution)/shard_map/pack/pallas_call | solution.py:208
  1.1 4.1 %collective-permute-start = (bf16[4,3712]{1,0:T(4,128)(2,1)S(1)}, bf16[4,3712]{1,0:T(4,128)(2,1)S(1)}, u32[]{:S(2)}, u32[]{:S(2)}) collective-permute-start(bf16[4,3712]{1,0:T(4,128)(2,1)S(1)} %pack.1.refs_0_), channel_id=1, source_target_pairs={{0,8},{1,9},{2,10},{3,11},{4,12},{5,13},{6,14},{7,15},{8,0},{9,1},... | collective-permute-start | bytes 89096 | tf_op jit(solution)/shard_map/ppermute | solution.py:79
  5.2 2.2 %collective-permute-done.refs_1_ = bf16[4,3712]{1,0:T(4,128)(2,1)S(1)} collective-permute-done((bf16[4,3712]{1,0:T(4,128)(2,1)S(1)}, bf16[4,3712]{1,0:T(4,128)(2,1)S(1)}, u32[]{:S(2)}, u32[]{:S(2)}) %collective-permute-start) | collective-permute-done | bytes 29728 | tf_op jit(solution)/shard_map/ppermute | solution.py:79
  7.4 0.0 slice-start.1
  7.4 0.0 slice-start.3
  7.4 2.6 %collective-permute-start.3 = (bf16[8,3712]{1,0:T(8,128)(2,1)S(1)}, bf16[8,3712]{1,0:T(8,128)(2,1)S(1)}, u32[]{:S(2)}, u32[]{:S(2)}) collective-permute-start(bf16[8,3712]{1,0:T(8,128)(2,1)S(1)} %join.1.refs_0_), channel_id=1, source_target_pairs={{0,6},{1,7},{2,4},{3,5},{4,2},{5,3},{6,0},{7,1},{8,14},{9,15},{10,... | collective-permute-start | bytes 178184 | tf_op jit(solution)/shard_map/ppermute | solution.py:79
  10.0 0.6 %collective-permute-start.2 = (bf16[8,3712]{1,0:T(8,128)(2,1)S(1)}, bf16[8,3712]{1,0:T(8,128)(2,1)S(1)}, u32[]{:S(2)}, u32[]{:S(2)}) collective-permute-start(bf16[8,3712]{1,0:T(8,128)(2,1)S(1)} %join.1.refs_0_), channel_id=1, source_target_pairs={{0,4},{1,5},{2,6},{3,7},{4,0},{5,1},{6,2},{7,3},{8,12},{9,13},{10,... | collective-permute-start | bytes 178184 | tf_op jit(solution)/shard_map/ppermute | solution.py:79
  10.6 0.3 collective-permute-start.1
  11.0 1.6 %collective-permute-done.3.refs_3_ = bf16[8,3712]{1,0:T(8,128)(2,1)S(1)} collective-permute-done((bf16[8,3712]{1,0:T(8,128)(2,1)S(1)}, bf16[8,3712]{1,0:T(8,128)(2,1)S(1)}, u32[]{:S(2)}, u32[]{:S(2)}) %collective-permute-start.3) | collective-permute-done | bytes 59424 | tf_op jit(solution)/shard_map/ppermute | solution.py:79
  12.6 0.0 collective-permute-start.7
  12.6 1.6 %collective-permute-done.2.refs_2_ = bf16[8,3712]{1,0:T(8,128)(2,1)S(1)} collective-permute-done((bf16[8,3712]{1,0:T(8,128)(2,1)S(1)}, bf16[8,3712]{1,0:T(8,128)(2,1)S(1)}, u32[]{:S(2)}, u32[]{:S(2)}) %collective-permute-start.2) | collective-permute-done | bytes 59424 | tf_op jit(solution)/shard_map/ppermute | solution.py:79
  14.2 0.0 collective-permute-start.6
  14.2 0.6 %collective-permute-done.1.refs_1_ = bf16[8,3712]{1,0:T(8,128)(2,1)S(1)} collective-permute-done((bf16[8,3712]{1,0:T(8,128)(2,1)S(1)}, bf16[8,3712]{1,0:T(8,128)(2,1)S(1)}, u32[]{:S(2)}, u32[]{:S(2)}) %collective-permute-start.1) | collective-permute-done | bytes 59424 | tf_op jit(solution)/shard_map/ppermute | solution.py:79
  14.9 0.6 %collective-permute-done.6.refs_6_ = bf16[8,3712]{1,0:T(8,128)(2,1)S(1)} collective-permute-done((bf16[8,3712]{1,0:T(8,128)(2,1)S(1)}, bf16[8,3712]{1,0:T(8,128)(2,1)S(1)}, u32[]{:S(2)}, u32[]{:S(2)}) %collective-permute-start.6) | collective-permute-done | bytes 59424 | tf_op jit(solution)/shard_map/ppermute | solution.py:79
  15.4 0.6 %collective-permute-done.5.refs_5_ = bf16[8,3712]{1,0:T(8,128)(2,1)S(1)} collective-permute-done((bf16[8,3712]{1,0:T(8,128)(2,1)S(1)}, bf16[8,3712]{1,0:T(8,128)(2,1)S(1)}, u32[]{:S(2)}, u32[]{:S(2)}) %collective-permute-start.5) | collective-permute-done | bytes 59424 | tf_op jit(solution)/shard_map/ppermute | solution.py:79
  16.1 4.1 %hidden.1 = (bf16[64,2048]{1,0:T(8,128)(2,1)S(1)}, f32[64,128]{1,0:T(8,128)S(1)}) custom-call(bf16[8,3712]{1,0:T(8,128)(2,1)S(1)} %join.1.refs_0_, bf16[8,3712]{1,0:T(8,128)(2,1)S(1)} %collective-permute-done.1.refs_1_, bf16[8,3712]{1,0:T(8,128)(2,1)S(1)} %collective-permute-done.2.refs_2_, bf16[8,3712]{1,0:T(8,128)(2,1)S(1)} %collective-permute-done.3.refs_3_, ...), custom_call_target="tpu_custom_call" | custom-call | tf_op jit(solution)/shard_map/hidden/pallas_call | solution.py:227
  20.2 2.1 %down.1 = (f32[8,3584]{1,0:T(8,128)S(1)}, f32[8,3584]{1,0:T(8,128)S(1)}, f32[8,3584]{1,0:T(8,128)S(1)}, f32[8,3584]{1,0:T(8,128)S(1)}, bf16[8,3584]{1,0:T(8,128)...) custom-call(bf16[64,2048]{1,0:T(8,128)(2,1)S(1)} %get-tuple-element.17.refs_0_, ...), custom_call_target="tpu_custom_call" | custom-call | tf_op jit(solution)/shard_map/down/pallas_call | solution.py:239
  22.3 0.2 collective-permute-start.8
  22.5 0.4 %collective-permute-start.10 = (bf16[8,3584]{1,0:T(8,128)(2,1)S(1)}, bf16[8,3584]{1,0:T(8,128)(2,1)S(1)}, u32[]{:S(2)}, u32[]{:S(2)}) collective-permute-start(bf16[8,3584]{1,0:T(8,128)(2,1)S(1)} %get-tuple-element.23), channel_id=1, source_target_pairs={{0,1},{1,0},{2,3},{3,2},{4,5},{5,4},{6,7},{7,6},{8,9},{9,8},{10,11... | collective-permute-start | bytes 172040 | tf_op jit(solution)/shard_map/ppermute | solution.py:79
  22.9 0.2 collective-permute-start.12
  23.1 0.4 %collective-permute-start.14 = (bf16[8,3584]{1,0:T(8,128)(2,1)S(1)}, bf16[8,3584]{1,0:T(8,128)(2,1)S(1)}, u32[]{:S(2)}, u32[]{:S(2)}) collective-permute-start(bf16[8,3584]{1,0:T(8,128)(2,1)S(1)} %get-tuple-element.26), channel_id=1, source_target_pairs={{0,1},{1,0},{2,3},{3,2},{4,5},{5,4},{6,7},{7,6},{8,9},{9,8},{10,11... | collective-permute-start | bytes 172040 | tf_op jit(solution)/shard_map/ppermute | solution.py:79
  23.4 0.2 collective-permute-done.8.got_ref
  23.6 1.4 %collective-permute-start.9 = (bf16[8,3584]{1,0:T(8,128)(2,1)S(1)}, bf16[8,3584]{1,0:T(8,128)(2,1)S(1)}, u32[]{:S(2)}, u32[]{:S(2)}) collective-permute-start(bf16[8,3584]{1,0:T(8,128)(2,1)S(1)} %add.4), channel_id=1, source_target_pairs={{0,6},{1,7},{2,4},{3,5},{4,2},{5,3},{6,0},{7,1},{8,14},{9,15},{10,... | collective-permute-start | bytes 172040 | tf_op jit(solution)/shard_map/ppermute | solution.py:79
  25.1 0.5 %collective-permute-start.11 = (bf16[8,3584]{1,0:T(8,128)(2,1)S(1)}, bf16[8,3584]{1,0:T(8,128)(2,1)S(1)}, u32[]{:S(2)}, u32[]{:S(2)}) collective-permute-start(bf16[8,3584]{1,0:T(8,128)(2,1)S(1)} %add.5), channel_id=1, source_target_pairs={{0,4},{1,5},{2,6},{3,7},{4,0},{5,1},{6,2},{7,3},{8,12},{9,13},{10,... | collective-permute-start | bytes 172040 | tf_op jit(solution)/shard_map/ppermute | solution.py:79
  25.6 0.0 collective-permute-done.12.got_ref
  25.6 1.8 %collective-permute-start.13 = (bf16[8,3584]{1,0:T(8,128)(2,1)S(1)}, bf16[8,3584]{1,0:T(8,128)(2,1)S(1)}, u32[]{:S(2)}, u32[]{:S(2)}) collective-permute-start(bf16[8,3584]{1,0:T(8,128)(2,1)S(1)} %add.6), channel_id=1, source_target_pairs={{0,2},{1,3},{2,0},{3,1},{4,6},{5,7},{6,4},{7,5},{8,10},{9,11},{10,... | collective-permute-start | bytes 172040 | tf_op jit(solution)/shard_map/ppermute | solution.py:79
  27.4 1.7 %collective-permute-done.9.refs_0_ = bf16[8,3584]{1,0:T(8,128)(2,1)S(1)} collective-permute-done((bf16[8,3584]{1,0:T(8,128)(2,1)S(1)}, bf16[8,3584]{1,0:T(8,128)(2,1)S(1)}, u32[]{:S(2)}, u32[]{:S(2)}) %collective-permute-start.9) | collective-permute-done | bytes 57376 | tf_op jit(solution)/shard_map/ppermute | solution.py:79
  29.1 0.2 collective-permute-done.11.refs_1_
  29.3 0.5 %collective-permute-done.13.refs_2_ = bf16[8,3584]{1,0:T(8,128)(2,1)S(1)} collective-permute-done((bf16[8,3584]{1,0:T(8,128)(2,1)S(1)}, bf16[8,3584]{1,0:T(8,128)(2,1)S(1)}, u32[]{:S(2)}, u32[]{:S(2)}) %collective-permute-start.13) | collective-permute-done | bytes 57376 | tf_op jit(solution)/shard_map/ppermute | solution.py:79
  29.9 2.7 %collective-permute-start.15 = (bf16[4,3584]{1,0:T(4,128)(2,1)S(1)}, bf16[4,3584]{1,0:T(4,128)(2,1)S(1)}, u32[]{:S(2)}, u32[]{:S(2)}) collective-permute-start(bf16[4,3584]{1,0:T(4,128)(2,1)S(1)} %get-tuple-element.28), channel_id=1, source_target_pairs={{0,8},{1,9},{2,10},{3,11},{4,12},{5,13},{6,14},{7,15},{8,0},{9,1},... | collective-permute-start | bytes 86024 | tf_op jit(solution)/shard_map/ppermute | solution.py:79
  32.6 2.2 %collective-permute-done.15.got_ref = bf16[4,3584]{1,0:T(4,128)(2,1)S(1)} collective-permute-done((bf16[4,3584]{1,0:T(4,128)(2,1)S(1)}, bf16[4,3584]{1,0:T(4,128)(2,1)S(1)}, u32[]{:S(2)}, u32[]{:S(2)}) %collective-permute-start.15) | collective-permute-done | bytes 28704 | tf_op jit(solution)/shard_map/ppermute | solution.py:79
  34.7 0.6 %add.7 = bf16[4,3584]{1,0:T(4,128)(2,1)} custom-call(f32[4,3584]{1,0:T(4,128)S(1)} %get-tuple-element.27.kept_ref, bf16[4,3584]{1,0:T(4,128)(2,1)S(1)} %collective-permute-done.15.got_ref), custom_call_target="tpu_custom_call" | custom-call | tf_op jit(solution)/shard_map/add/pallas_call | solution.py:183
  (22 shorter events, 0.1 us)
Async XLA Ops:
  0.0 16.1 %copy-start.1 = (bf16[1,3584,2048]{2,1,0:T(8,128)(2,1)S(1)}, bf16[1,3584,2048]{2,1,0:T(8,128)(2,1)}, u32[]{:S(2)}) copy-start(bf16[1,3584,2048]{2,1,0:T(8,128)(2,1)} %refs_9_.1) | copy-start | bytes 44040196
  0.0 16.1 %copy-start = (bf16[1,3584,2048]{2,1,0:T(8,128)(2,1)S(1)}, bf16[1,3584,2048]{2,1,0:T(8,128)(2,1)}, u32[]{:S(2)}) copy-start(bf16[1,3584,2048]{2,1,0:T(8,128)(2,1)} %refs_8_.1) | copy-start | bytes 44040196
  1.1 6.3 %collective-permute-start = (bf16[4,3712]{1,0:T(4,128)(2,1)S(1)}, bf16[4,3712]{1,0:T(4,128)(2,1)S(1)}, u32[]{:S(2)}, u32[]{:S(2)}) collective-permute-start(bf16[4,3712]{1,0:T(4,128)(2,1)S(1)} %pack.1.refs_0_), channel_id=1, source_target_pairs={{0,8},{1,9},{2,10},{3,11},{4,12},{5,13},{6,14},{7,15},{8,0},{9,1},... | collective-permute-start | bytes 89096 | tf_op jit(solution)/shard_map/ppermute | solution.py:79
  7.4 12.8 %slice-start = ((s8[14680064]{0:T(1024)(128)(4,1)}), s8[4194304]{0:T(1024)(128)(4,1)S(1)}, s32[]{:S(2)}) async-start(s8[14680064]{0:T(1024)(128)(4,1)} %bitcast), calls=%async_computation | async-start | bytes 8388608
  7.4 12.8 %slice-start.1 = ((s8[14680064]{0:T(1024)(128)(4,1)}), s8[4194304]{0:T(1024)(128)(4,1)S(1)}, s32[]{:S(2)}) async-start(s8[14680064]{0:T(1024)(128)(4,1)} %bitcast), calls=%async_computation.1 | async-start | bytes 8388608
  7.4 12.8 %slice-start.2 = ((s8[14680064]{0:T(1024)(128)(4,1)}), s8[4194304]{0:T(1024)(128)(4,1)S(1)}, s32[]{:S(2)}) async-start(s8[14680064]{0:T(1024)(128)(4,1)} %bitcast), calls=%async_computation.2 | async-start | bytes 8388608
  7.4 12.8 %slice-start.3 = ((s8[14680064]{0:T(1024)(128)(4,1)}), s8[2097152]{0:T(1024)(128)(4,1)S(1)}, s32[]{:S(2)}) async-start(s8[14680064]{0:T(1024)(128)(4,1)} %bitcast), calls=%async_computation.3 | async-start | bytes 4194304
  7.4 5.2 %collective-permute-start.3 = (bf16[8,3712]{1,0:T(8,128)(2,1)S(1)}, bf16[8,3712]{1,0:T(8,128)(2,1)S(1)}, u32[]{:S(2)}, u32[]{:S(2)}) collective-permute-start(bf16[8,3712]{1,0:T(8,128)(2,1)S(1)} %join.1.refs_0_), channel_id=1, source_target_pairs={{0,6},{1,7},{2,4},{3,5},{4,2},{5,3},{6,0},{7,1},{8,14},{9,15},{10,... | collective-permute-start | bytes 178184 | tf_op jit(solution)/shard_map/ppermute | solution.py:79
  10.0 4.2 %collective-permute-start.2 = (bf16[8,3712]{1,0:T(8,128)(2,1)S(1)}, bf16[8,3712]{1,0:T(8,128)(2,1)S(1)}, u32[]{:S(2)}, u32[]{:S(2)}) collective-permute-start(bf16[8,3712]{1,0:T(8,128)(2,1)S(1)} %join.1.refs_0_), channel_id=1, source_target_pairs={{0,4},{1,5},{2,6},{3,7},{4,0},{5,1},{6,2},{7,3},{8,12},{9,13},{10,... | collective-permute-start | bytes 178184 | tf_op jit(solution)/shard_map/ppermute | solution.py:79
  10.6 4.2 %collective-permute-start.1 = (bf16[8,3712]{1,0:T(8,128)(2,1)S(1)}, bf16[8,3712]{1,0:T(8,128)(2,1)S(1)}, u32[]{:S(2)}, u32[]{:S(2)}) collective-permute-start(bf16[8,3712]{1,0:T(8,128)(2,1)S(1)} %join.1.refs_0_), channel_id=1, source_target_pairs={{0,2},{1,3},{2,0},{3,1},{4,6},{5,7},{6,4},{7,5},{8,10},{9,11},{10,... | collective-permute-start | bytes 178184 | tf_op jit(solution)/shard_map/ppermute | solution.py:79
  11.0 3.9 %collective-permute-start.4 = (bf16[8,3712]{1,0:T(8,128)(2,1)S(1)}, bf16[8,3712]{1,0:T(8,128)(2,1)S(1)}, u32[]{:S(2)}, u32[]{:S(2)}) collective-permute-start(bf16[8,3712]{1,0:T(8,128)(2,1)S(1)} %join.1.refs_0_), channel_id=1, source_target_pairs={{0,1},{1,0},{2,3},{3,2},{4,5},{5,4},{6,7},{7,6},{8,9},{9,8},{10,11... | collective-permute-start | bytes 178184 | tf_op jit(solution)/shard_map/ppermute | solution.py:79
  12.6 2.3 %collective-permute-start.7 = (bf16[8,3712]{1,0:T(8,128)(2,1)S(1)}, bf16[8,3712]{1,0:T(8,128)(2,1)S(1)}, u32[]{:S(2)}, u32[]{:S(2)}) collective-permute-start(bf16[8,3712]{1,0:T(8,128)(2,1)S(1)} %collective-permute-done.3.refs_3_), channel_id=1, source_target_pairs={{0,1},{1,0},{2,3},{3,2},{4,5},{5,4},{6,7},{7,6},{8,9},{9,8},{10,11... | collective-permute-start | bytes 178184 | tf_op jit(solution)/shard_map/ppermute | solution.py:79
  14.2 1.2 %collective-permute-start.6 = (bf16[8,3712]{1,0:T(8,128)(2,1)S(1)}, bf16[8,3712]{1,0:T(8,128)(2,1)S(1)}, u32[]{:S(2)}, u32[]{:S(2)}) collective-permute-start(bf16[8,3712]{1,0:T(8,128)(2,1)S(1)} %collective-permute-done.2.refs_2_), channel_id=1, source_target_pairs={{0,1},{1,0},{2,3},{3,2},{4,5},{5,4},{6,7},{7,6},{8,9},{9,8},{10,11... | collective-permute-start | bytes 178184 | tf_op jit(solution)/shard_map/ppermute | solution.py:79
  14.8 1.2 %collective-permute-start.5 = (bf16[8,3712]{1,0:T(8,128)(2,1)S(1)}, bf16[8,3712]{1,0:T(8,128)(2,1)S(1)}, u32[]{:S(2)}, u32[]{:S(2)}) collective-permute-start(bf16[8,3712]{1,0:T(8,128)(2,1)S(1)} %collective-permute-done.1.refs_1_), channel_id=1, source_target_pairs={{0,1},{1,0},{2,3},{3,2},{4,5},{5,4},{6,7},{7,6},{8,9},{9,8},{10,11... | collective-permute-start | bytes 178184 | tf_op jit(solution)/shard_map/ppermute | solution.py:79
  22.3 1.3 %collective-permute-start.8 = (bf16[8,3584]{1,0:T(8,128)(2,1)S(1)}, bf16[8,3584]{1,0:T(8,128)(2,1)S(1)}, u32[]{:S(2)}, u32[]{:S(2)}) collective-permute-start(bf16[8,3584]{1,0:T(8,128)(2,1)S(1)} %get-tuple-element.21), channel_id=1, source_target_pairs={{0,1},{1,0},{2,3},{3,2},{4,5},{5,4},{6,7},{7,6},{8,9},{9,8},{10,11... | collective-permute-start | bytes 172040 | tf_op jit(solution)/shard_map/ppermute | solution.py:79
  22.5 2.5 %collective-permute-start.10 = (bf16[8,3584]{1,0:T(8,128)(2,1)S(1)}, bf16[8,3584]{1,0:T(8,128)(2,1)S(1)}, u32[]{:S(2)}, u32[]{:S(2)}) collective-permute-start(bf16[8,3584]{1,0:T(8,128)(2,1)S(1)} %get-tuple-element.23), channel_id=1, source_target_pairs={{0,1},{1,0},{2,3},{3,2},{4,5},{5,4},{6,7},{7,6},{8,9},{9,8},{10,11... | collective-permute-start | bytes 172040 | tf_op jit(solution)/shard_map/ppermute | solution.py:79
  22.9 2.7 %collective-permute-start.12 = (bf16[8,3584]{1,0:T(8,128)(2,1)S(1)}, bf16[8,3584]{1,0:T(8,128)(2,1)S(1)}, u32[]{:S(2)}, u32[]{:S(2)}) collective-permute-start(bf16[8,3584]{1,0:T(8,128)(2,1)S(1)} %get-tuple-element.25), channel_id=1, source_target_pairs={{0,1},{1,0},{2,3},{3,2},{4,5},{5,4},{6,7},{7,6},{8,9},{9,8},{10,11... | collective-permute-start | bytes 172040 | tf_op jit(solution)/shard_map/ppermute | solution.py:79
  23.1 4.3 %collective-permute-start.14 = (bf16[8,3584]{1,0:T(8,128)(2,1)S(1)}, bf16[8,3584]{1,0:T(8,128)(2,1)S(1)}, u32[]{:S(2)}, u32[]{:S(2)}) collective-permute-start(bf16[8,3584]{1,0:T(8,128)(2,1)S(1)} %get-tuple-element.26), channel_id=1, source_target_pairs={{0,1},{1,0},{2,3},{3,2},{4,5},{5,4},{6,7},{7,6},{8,9},{9,8},{10,11... | collective-permute-start | bytes 172040 | tf_op jit(solution)/shard_map/ppermute | solution.py:79
  23.6 5.5 %collective-permute-start.9 = (bf16[8,3584]{1,0:T(8,128)(2,1)S(1)}, bf16[8,3584]{1,0:T(8,128)(2,1)S(1)}, u32[]{:S(2)}, u32[]{:S(2)}) collective-permute-start(bf16[8,3584]{1,0:T(8,128)(2,1)S(1)} %add.4), channel_id=1, source_target_pairs={{0,6},{1,7},{2,4},{3,5},{4,2},{5,3},{6,0},{7,1},{8,14},{9,15},{10,... | collective-permute-start | bytes 172040 | tf_op jit(solution)/shard_map/ppermute | solution.py:79
  25.1 4.2 %collective-permute-start.11 = (bf16[8,3584]{1,0:T(8,128)(2,1)S(1)}, bf16[8,3584]{1,0:T(8,128)(2,1)S(1)}, u32[]{:S(2)}, u32[]{:S(2)}) collective-permute-start(bf16[8,3584]{1,0:T(8,128)(2,1)S(1)} %add.5), channel_id=1, source_target_pairs={{0,4},{1,5},{2,6},{3,7},{4,0},{5,1},{6,2},{7,3},{8,12},{9,13},{10,... | collective-permute-start | bytes 172040 | tf_op jit(solution)/shard_map/ppermute | solution.py:79
  25.6 4.2 %collective-permute-start.13 = (bf16[8,3584]{1,0:T(8,128)(2,1)S(1)}, bf16[8,3584]{1,0:T(8,128)(2,1)S(1)}, u32[]{:S(2)}, u32[]{:S(2)}) collective-permute-start(bf16[8,3584]{1,0:T(8,128)(2,1)S(1)} %add.6), channel_id=1, source_target_pairs={{0,2},{1,3},{2,0},{3,1},{4,6},{5,7},{6,4},{7,5},{8,10},{9,11},{10,... | collective-permute-start | bytes 172040 | tf_op jit(solution)/shard_map/ppermute | solution.py:79
  29.9 4.8 %collective-permute-start.15 = (bf16[4,3584]{1,0:T(4,128)(2,1)S(1)}, bf16[4,3584]{1,0:T(4,128)(2,1)S(1)}, u32[]{:S(2)}, u32[]{:S(2)}) collective-permute-start(bf16[4,3584]{1,0:T(4,128)(2,1)S(1)} %get-tuple-element.28), channel_id=1, source_target_pairs={{0,8},{1,9},{2,10},{3,11},{4,12},{5,13},{6,14},{7,15},{8,0},{9,1},... | collective-permute-start | bytes 86024 | tf_op jit(solution)/shard_map/ppermute | solution.py:79

commit v5 on v4

--- a/solution.py
+++ b/solution.py
@@ -133,36 +133,35 @@
     )(*pieces)
 
 
-def hidden_kernel(step, fill, experts, *refs):
-    *x_refs, gate_ref, up_ref, out_ref, weight_ref = refs
+def expert_kernel(step, fill, experts, count, *refs):
+    x_refs, (gate_ref, up_ref, down_ref) = refs[: 2 * count], refs[2 * count : 2 * count + 3]
+    out_refs, x_vmem, hidden_vmem = refs[2 * count + 3 : -2], refs[-2], refs[-1]
     width = gate_ref.shape[1]
-    rows = out_ref.shape[0]
+    units = gate_ref.shape[2]
     me = lax.axis_index("expert")
     spread = jnp.concatenate([ref[:, width:].astype(jnp.float32) for ref in x_refs], axis=0)
+    rows = spread.shape[0]
     lane = lax.broadcasted_iota(jnp.int32, spread.shape, 1)
     mine = (lane == me) | (lane == me + experts)
     weight = jnp.sum(jnp.where(mine, spread, 0.0), axis=1, keepdims=True)
-    weight_ref[...] = jnp.broadcast_to(weight, weight_ref.shape)
     x = jnp.concatenate([ref[:, :width].astype(jnp.float32) for ref in x_refs], axis=0)
-    x = filled(x.astype(jnp.bfloat16), fill)
-    for start in range(0, gate_ref.shape[2], step):
+    x_vmem[:rows] = x.astype(jnp.bfloat16)
+    x_vmem[rows:] = jnp.zeros((fill - rows, width), jnp.bfloat16)
+    hidden_vmem[rows:] = jnp.zeros((fill - rows, units), jnp.bfloat16)
+    x = x_vmem[...]
+    for start in range(0, units, step):
         cut = slice(start, start + step)
         gate = jnp.dot(x, gate_ref[0, :, cut], preferred_element_type=jnp.float32)[:rows]
         up = jnp.dot(x, up_ref[0, :, cut], preferred_element_type=jnp.float32)[:rows]
-        out_ref[:, cut] = (gate / (1.0 + jnp.exp(-gate)) * up).astype(jnp.bfloat16)
-
-
-def down_kernel(step, fill, hidden_ref, weight_ref, down_ref, *out_refs):
-    keep_refs, send_refs = out_refs[: len(out_refs) // 2], out_refs[len(out_refs) // 2 :]
-    hidden = filled(hidden_ref[...], fill)
-    weight = weight_ref[:, :1]
-    rows = keep_refs[0].shape[0]
-    for start in range(0, down_ref.shape[2], step):
+        hidden_vmem[:rows, cut] = (gate / (1.0 + jnp.exp(-gate)) * up).astype(jnp.bfloat16)
+    hidden = hidden_vmem[...]
+    for start in range(0, width, step):
         cut = slice(start, start + step)
         out = jnp.dot(hidden, down_ref[0, :, cut], preferred_element_type=jnp.float32)
-        part = out[: weight.shape[0]].astype(jnp.bfloat16).astype(jnp.float32) * weight
-        for i, ref in enumerate(keep_refs + send_refs):
-            ref[:, cut] = part[i * rows : (i + 1) * rows].astype(ref.dtype)
+        part = out[:rows].astype(jnp.bfloat16).astype(jnp.float32) * weight
+        piece = out_refs[0].shape[0]
+        for i, ref in enumerate(out_refs):
+            ref[:, cut] = part[i * piece : (i + 1) * piece].astype(ref.dtype)
 
 
 def add_kernel(kept_ref, got_ref, out_ref):
@@ -224,27 +223,20 @@
     near = join([packed, swap(packed, far)], params)
     pieces = [near] + [swap(near, d) for d in middle]
     pieces = pieces + [swap(piece, 1) for piece in pieces]
-    hidden, weight = pl.pallas_call(
-        lambda *refs: hidden_kernel(256, fill, experts, *refs),
-        out_shape=[
-            jax.ShapeDtypeStruct((2 * half, units), jnp.bfloat16),
-            jax.ShapeDtypeStruct((2 * half, LANES), jnp.float32),
-        ],
-        in_specs=vmem(len(pieces) + 2),
-        out_specs=vmem(2),
-        compiler_params=params,
-        name="hidden",
-    )(*pieces, gate_w, up_w)
     count = len(middle) + 1
     kept_and_sent = pl.pallas_call(
-        lambda *refs: down_kernel(256, fill, *refs),
+        lambda *refs: expert_kernel(256, fill, experts, count, *refs),
         out_shape=[jax.ShapeDtypeStruct((2 * rows, width), jnp.float32)] * count
         + [jax.ShapeDtypeStruct((2 * rows, width), jnp.bfloat16)] * count,
-        in_specs=vmem(3),
+        in_specs=vmem(2 * count + 3),
         out_specs=vmem(2 * count),
-        compiler_params=params,
-        name="down",
-    )(hidden, weight, down_w)
+        scratch_shapes=[
+            pltpu.VMEM((fill, width), jnp.bfloat16),
+            pltpu.VMEM((fill, units), jnp.bfloat16),
+        ],
+        compiler_params=params,
+        name="expert",
+    )(*pieces, gate_w, up_w, down_w)
     kept, sent = kept_and_sent[:count], kept_and_sent[count:]
     gots = [
         swap(add(kept[i], swap(sent[i], 1), params), middle[i - 1]) for i in range(count - 1, 0, -1)

time: 35.5 us -> 35.4 us (level)
    pallas_call x2 -> x1, Pallas kernels: 6.16 us -> 6.02 us  [shards(): pl.pallas_call(lambda *refs: expert_kernel(256, fill, experts, count, *re...]
where the time goes in v5:
time: 35.4 us; the launch traced here: 35.2 us
  starting transfers between devices  15.1 us (43%)
  waiting for transfers between devices  12.3 us (35%)
  Pallas kernels  7.81 us (22%)
    ppermute x16, starting transfers between devices, swap(): return lax.ppermute(x, 'expert', [(i, i ^ distance) for i in range(count)])  15.1 us
    ppermute x16, waiting for transfers between devices, swap(): return lax.ppermute(x, 'expert', [(i, i ^ distance) for i in range(count)])  12.3 us
    pallas_call x1, Pallas kernels, shards(): pl.pallas_call(lambda *refs: expert_kernel(256, fill, experts, count, *re...  6.02 us
    pallas_call x1, Pallas kernels, shards(): pl.pallas_call(lambda *refs: pack_kernel(experts, *refs), out_shape=jax.S...  1.06 us
  transfers between devices with their start and end apart: 16, of which 11 were waited for; matrix products, arithmetic and copies ran while one was open for 0% of the time, Pallas kernels for 0%

profile of v5, /device:TPU:0, one launch (start us, length us, event | category | flops | bytes accessed | tf_op | source)
XLA Modules:
  0.0 35.2 jit_solution(11664077332118151752)
XLA Ops:
  0.0 1.1 %pack.1.refs_0_ = bf16[4,3712]{1,0:T(4,128)(2,1)S(1)} custom-call(bf16[4,3584]{1,0:T(4,128)(2,1)} %refs_0_.1, s32[4,8]{1,0:T(4,128)} %refs_1_.1, f32[4,8]{1,0:T(4,128)} %refs_2_.1), custom_call_target="tpu_custom_call" | custom-call | flops 40000000000 | bytes 100000000 | tf_op jit(solution)/shard_map/pack/pallas_call | solution.py:207
  1.1 4.1 %collective-permute-start = (bf16[4,3712]{1,0:T(4,128)(2,1)S(1)}, bf16[4,3712]{1,0:T(4,128)(2,1)S(1)}, u32[]{:S(2)}, u32[]{:S(2)}) collective-permute-start(bf16[4,3712]{1,0:T(4,128)(2,1)S(1)} %pack.1.refs_0_), channel_id=1, source_target_pairs={{0,8},{1,9},{2,10},{3,11},{4,12},{5,13},{6,14},{7,15},{8,0},{9,1},... | collective-permute-start | bytes 89096 | tf_op jit(solution)/shard_map/ppermute | solution.py:79
  5.2 2.2 %collective-permute-done.refs_1_ = bf16[4,3712]{1,0:T(4,128)(2,1)S(1)} collective-permute-done((bf16[4,3712]{1,0:T(4,128)(2,1)S(1)}, bf16[4,3712]{1,0:T(4,128)(2,1)S(1)}, u32[]{:S(2)}, u32[]{:S(2)}) %collective-permute-start) | collective-permute-done | bytes 29728 | tf_op jit(solution)/shard_map/ppermute | solution.py:79
  7.4 2.6 %collective-permute-start.3 = (bf16[8,3712]{1,0:T(8,128)(2,1)S(1)}, bf16[8,3712]{1,0:T(8,128)(2,1)S(1)}, u32[]{:S(2)}, u32[]{:S(2)}) collective-permute-start(bf16[8,3712]{1,0:T(8,128)(2,1)S(1)} %join.1.refs_0_), channel_id=1, source_target_pairs={{0,6},{1,7},{2,4},{3,5},{4,2},{5,3},{6,0},{7,1},{8,14},{9,15},{10,... | collective-permute-start | bytes 178184 | tf_op jit(solution)/shard_map/ppermute | solution.py:79
  10.0 0.6 %collective-permute-start.2 = (bf16[8,3712]{1,0:T(8,128)(2,1)S(1)}, bf16[8,3712]{1,0:T(8,128)(2,1)S(1)}, u32[]{:S(2)}, u32[]{:S(2)}) collective-permute-start(bf16[8,3712]{1,0:T(8,128)(2,1)S(1)} %join.1.refs_0_), channel_id=1, source_target_pairs={{0,4},{1,5},{2,6},{3,7},{4,0},{5,1},{6,2},{7,3},{8,12},{9,13},{10,... | collective-permute-start | bytes 178184 | tf_op jit(solution)/shard_map/ppermute | solution.py:79
  10.6 0.3 collective-permute-start.1
  10.9 0.0 collective-permute-start.4
  10.9 1.6 %collective-permute-done.3.refs_3_ = bf16[8,3712]{1,0:T(8,128)(2,1)S(1)} collective-permute-done((bf16[8,3712]{1,0:T(8,128)(2,1)S(1)}, bf16[8,3712]{1,0:T(8,128)(2,1)S(1)}, u32[]{:S(2)}, u32[]{:S(2)}) %collective-permute-start.3) | collective-permute-done | bytes 59424 | tf_op jit(solution)/shard_map/ppermute | solution.py:79
  12.6 1.6 %collective-permute-done.2.refs_2_ = bf16[8,3712]{1,0:T(8,128)(2,1)S(1)} collective-permute-done((bf16[8,3712]{1,0:T(8,128)(2,1)S(1)}, bf16[8,3712]{1,0:T(8,128)(2,1)S(1)}, u32[]{:S(2)}, u32[]{:S(2)}) %collective-permute-start.2) | collective-permute-done | bytes 59424 | tf_op jit(solution)/shard_map/ppermute | solution.py:79
  14.2 0.6 %collective-permute-done.1.refs_1_ = bf16[8,3712]{1,0:T(8,128)(2,1)S(1)} collective-permute-done((bf16[8,3712]{1,0:T(8,128)(2,1)S(1)}, bf16[8,3712]{1,0:T(8,128)(2,1)S(1)}, u32[]{:S(2)}, u32[]{:S(2)}) %collective-permute-start.1) | collective-permute-done | bytes 59424 | tf_op jit(solution)/shard_map/ppermute | solution.py:79
  14.8 0.0 collective-permute-start.5
  14.8 0.0 collective-permute-done.4.refs_4_
  14.8 0.0 collective-permute-done.7.refs_7_
  14.8 0.6 %collective-permute-done.6.refs_6_ = bf16[8,3712]{1,0:T(8,128)(2,1)S(1)} collective-permute-done((bf16[8,3712]{1,0:T(8,128)(2,1)S(1)}, bf16[8,3712]{1,0:T(8,128)(2,1)S(1)}, u32[]{:S(2)}, u32[]{:S(2)}) %collective-permute-start.6) | collective-permute-done | bytes 59424 | tf_op jit(solution)/shard_map/ppermute | solution.py:79
  15.4 0.6 %collective-permute-done.5.refs_5_ = bf16[8,3712]{1,0:T(8,128)(2,1)S(1)} collective-permute-done((bf16[8,3712]{1,0:T(8,128)(2,1)S(1)}, bf16[8,3712]{1,0:T(8,128)(2,1)S(1)}, u32[]{:S(2)}, u32[]{:S(2)}) %collective-permute-start.5) | collective-permute-done | bytes 59424 | tf_op jit(solution)/shard_map/ppermute | solution.py:79
  16.1 6.0 %expert.1 = (f32[8,3584]{1,0:T(8,128)S(1)}, f32[8,3584]{1,0:T(8,128)S(1)}, f32[8,3584]{1,0:T(8,128)S(1)}, f32[8,3584]{1,0:T(8,128)S(1)}, bf16[8,3584]{1,0:T(8,12...) custom-call(bf16[8,3712]{1,0:T(8,128)(2,1)S(1)} %join.1.refs_0_, ...), custom_call_target="tpu_custom_call" | custom-call | tf_op jit(solution)/shard_map/expert/pallas_call | solution.py:227
  22.1 0.2 collective-permute-start.8
  22.3 0.4 %collective-permute-start.10 = (bf16[8,3584]{1,0:T(8,128)(2,1)S(1)}, bf16[8,3584]{1,0:T(8,128)(2,1)S(1)}, u32[]{:S(2)}, u32[]{:S(2)}) collective-permute-start(bf16[8,3584]{1,0:T(8,128)(2,1)S(1)} %get-tuple-element.19), channel_id=1, source_target_pairs={{0,1},{1,0},{2,3},{3,2},{4,5},{5,4},{6,7},{7,6},{8,9},{9,8},{10,11... | collective-permute-start | bytes 172040 | tf_op jit(solution)/shard_map/ppermute | solution.py:79
  22.7 0.1 collective-permute-start.12
  22.8 0.4 %collective-permute-start.14 = (bf16[8,3584]{1,0:T(8,128)(2,1)S(1)}, bf16[8,3584]{1,0:T(8,128)(2,1)S(1)}, u32[]{:S(2)}, u32[]{:S(2)}) collective-permute-start(bf16[8,3584]{1,0:T(8,128)(2,1)S(1)} %get-tuple-element.22), channel_id=1, source_target_pairs={{0,1},{1,0},{2,3},{3,2},{4,5},{5,4},{6,7},{7,6},{8,9},{9,8},{10,11... | collective-permute-start | bytes 172040 | tf_op jit(solution)/shard_map/ppermute | solution.py:79
  23.2 0.2 collective-permute-done.8.got_ref
  23.4 1.5 %collective-permute-start.9 = (bf16[8,3584]{1,0:T(8,128)(2,1)S(1)}, bf16[8,3584]{1,0:T(8,128)(2,1)S(1)}, u32[]{:S(2)}, u32[]{:S(2)}) collective-permute-start(bf16[8,3584]{1,0:T(8,128)(2,1)S(1)} %add.4), channel_id=1, source_target_pairs={{0,6},{1,7},{2,4},{3,5},{4,2},{5,3},{6,0},{7,1},{8,14},{9,15},{10,... | collective-permute-start | bytes 172040 | tf_op jit(solution)/shard_map/ppermute | solution.py:79
  24.9 0.0 collective-permute-done.10.got_ref
  25.0 0.5 %collective-permute-start.11 = (bf16[8,3584]{1,0:T(8,128)(2,1)S(1)}, bf16[8,3584]{1,0:T(8,128)(2,1)S(1)}, u32[]{:S(2)}, u32[]{:S(2)}) collective-permute-start(bf16[8,3584]{1,0:T(8,128)(2,1)S(1)} %add.5), channel_id=1, source_target_pairs={{0,4},{1,5},{2,6},{3,7},{4,0},{5,1},{6,2},{7,3},{8,12},{9,13},{10,... | collective-permute-start | bytes 172040 | tf_op jit(solution)/shard_map/ppermute | solution.py:79
  25.5 1.7 %collective-permute-start.13 = (bf16[8,3584]{1,0:T(8,128)(2,1)S(1)}, bf16[8,3584]{1,0:T(8,128)(2,1)S(1)}, u32[]{:S(2)}, u32[]{:S(2)}) collective-permute-start(bf16[8,3584]{1,0:T(8,128)(2,1)S(1)} %add.6), channel_id=1, source_target_pairs={{0,2},{1,3},{2,0},{3,1},{4,6},{5,7},{6,4},{7,5},{8,10},{9,11},{10,... | collective-permute-start | bytes 172040 | tf_op jit(solution)/shard_map/ppermute | solution.py:79
  27.1 0.0 collective-permute-done.14.refs_3_
  27.2 1.7 %collective-permute-done.9.refs_0_ = bf16[8,3584]{1,0:T(8,128)(2,1)S(1)} collective-permute-done((bf16[8,3584]{1,0:T(8,128)(2,1)S(1)}, bf16[8,3584]{1,0:T(8,128)(2,1)S(1)}, u32[]{:S(2)}, u32[]{:S(2)}) %collective-permute-start.9) | collective-permute-done | bytes 57376 | tf_op jit(solution)/shard_map/ppermute | solution.py:79
  28.9 0.3 collective-permute-done.11.refs_1_
  29.2 0.5 %collective-permute-done.13.refs_2_ = bf16[8,3584]{1,0:T(8,128)(2,1)S(1)} collective-permute-done((bf16[8,3584]{1,0:T(8,128)(2,1)S(1)}, bf16[8,3584]{1,0:T(8,128)(2,1)S(1)}, u32[]{:S(2)}, u32[]{:S(2)}) %collective-permute-start.13) | collective-permute-done | bytes 57376 | tf_op jit(solution)/shard_map/ppermute | solution.py:79
  29.8 2.7 %collective-permute-start.15 = (bf16[4,3584]{1,0:T(4,128)(2,1)S(1)}, bf16[4,3584]{1,0:T(4,128)(2,1)S(1)}, u32[]{:S(2)}, u32[]{:S(2)}) collective-permute-start(bf16[4,3584]{1,0:T(4,128)(2,1)S(1)} %get-tuple-element.24), channel_id=1, source_target_pairs={{0,8},{1,9},{2,10},{3,11},{4,12},{5,13},{6,14},{7,15},{8,0},{9,1},... | collective-permute-start | bytes 86024 | tf_op jit(solution)/shard_map/ppermute | solution.py:79
  32.4 2.2 %collective-permute-done.15.got_ref = bf16[4,3584]{1,0:T(4,128)(2,1)S(1)} collective-permute-done((bf16[4,3584]{1,0:T(4,128)(2,1)S(1)}, bf16[4,3584]{1,0:T(4,128)(2,1)S(1)}, u32[]{:S(2)}, u32[]{:S(2)}) %collective-permute-start.15) | collective-permute-done | bytes 28704 | tf_op jit(solution)/shard_map/ppermute | solution.py:79
  34.6 0.6 %add.7 = bf16[4,3584]{1,0:T(4,128)(2,1)} custom-call(f32[4,3584]{1,0:T(4,128)S(1)} %get-tuple-element.23.kept_ref, bf16[4,3584]{1,0:T(4,128)(2,1)S(1)} %collective-permute-done.15.got_ref), custom_call_target="tpu_custom_call" | custom-call | tf_op jit(solution)/shard_map/add/pallas_call | solution.py:182
  (14 shorter events, 0.1 us)
Async XLA Ops:
  0.0 16.1 %copy-start.2 = (bf16[1,2048,3584]{2,1,0:T(8,128)(2,1)S(1)}, bf16[1,2048,3584]{2,1,0:T(8,128)(2,1)}, u32[]{:S(2)}) copy-start(bf16[1,2048,3584]{2,1,0:T(8,128)(2,1)} %refs_10_.1) | copy-start | bytes 44040196
  0.0 16.1 %copy-start.1 = (bf16[1,3584,2048]{2,1,0:T(8,128)(2,1)S(1)}, bf16[1,3584,2048]{2,1,0:T(8,128)(2,1)}, u32[]{:S(2)}) copy-start(bf16[1,3584,2048]{2,1,0:T(8,128)(2,1)} %refs_9_.1) | copy-start | bytes 44040196
  0.0 16.1 %copy-start = (bf16[1,3584,2048]{2,1,0:T(8,128)(2,1)S(1)}, bf16[1,3584,2048]{2,1,0:T(8,128)(2,1)}, u32[]{:S(2)}) copy-start(bf16[1,3584,2048]{2,1,0:T(8,128)(2,1)} %refs_8_.1) | copy-start | bytes 44040196
  1.1 6.3 %collective-permute-start = (bf16[4,3712]{1,0:T(4,128)(2,1)S(1)}, bf16[4,3712]{1,0:T(4,128)(2,1)S(1)}, u32[]{:S(2)}, u32[]{:S(2)}) collective-permute-start(bf16[4,3712]{1,0:T(4,128)(2,1)S(1)} %pack.1.refs_0_), channel_id=1, source_target_pairs={{0,8},{1,9},{2,10},{3,11},{4,12},{5,13},{6,14},{7,15},{8,0},{9,1},... | collective-permute-start | bytes 89096 | tf_op jit(solution)/shard_map/ppermute | solution.py:79
  7.4 5.2 %collective-permute-start.3 = (bf16[8,3712]{1,0:T(8,128)(2,1)S(1)}, bf16[8,3712]{1,0:T(8,128)(2,1)S(1)}, u32[]{:S(2)}, u32[]{:S(2)}) collective-permute-start(bf16[8,3712]{1,0:T(8,128)(2,1)S(1)} %join.1.refs_0_), channel_id=1, source_target_pairs={{0,6},{1,7},{2,4},{3,5},{4,2},{5,3},{6,0},{7,1},{8,14},{9,15},{10,... | collective-permute-start | bytes 178184 | tf_op jit(solution)/shard_map/ppermute | solution.py:79
  10.0 4.2 %collective-permute-start.2 = (bf16[8,3712]{1,0:T(8,128)(2,1)S(1)}, bf16[8,3712]{1,0:T(8,128)(2,1)S(1)}, u32[]{:S(2)}, u32[]{:S(2)}) collective-permute-start(bf16[8,3712]{1,0:T(8,128)(2,1)S(1)} %join.1.refs_0_), channel_id=1, source_target_pairs={{0,4},{1,5},{2,6},{3,7},{4,0},{5,1},{6,2},{7,3},{8,12},{9,13},{10,... | collective-permute-start | bytes 178184 | tf_op jit(solution)/shard_map/ppermute | solution.py:79
  10.6 4.2 %collective-permute-start.1 = (bf16[8,3712]{1,0:T(8,128)(2,1)S(1)}, bf16[8,3712]{1,0:T(8,128)(2,1)S(1)}, u32[]{:S(2)}, u32[]{:S(2)}) collective-permute-start(bf16[8,3712]{1,0:T(8,128)(2,1)S(1)} %join.1.refs_0_), channel_id=1, source_target_pairs={{0,2},{1,3},{2,0},{3,1},{4,6},{5,7},{6,4},{7,5},{8,10},{9,11},{10,... | collective-permute-start | bytes 178184 | tf_op jit(solution)/shard_map/ppermute | solution.py:79
  10.9 3.9 %collective-permute-start.4 = (bf16[8,3712]{1,0:T(8,128)(2,1)S(1)}, bf16[8,3712]{1,0:T(8,128)(2,1)S(1)}, u32[]{:S(2)}, u32[]{:S(2)}) collective-permute-start(bf16[8,3712]{1,0:T(8,128)(2,1)S(1)} %join.1.refs_0_), channel_id=1, source_target_pairs={{0,1},{1,0},{2,3},{3,2},{4,5},{5,4},{6,7},{7,6},{8,9},{9,8},{10,11... | collective-permute-start | bytes 178184 | tf_op jit(solution)/shard_map/ppermute | solution.py:79
  12.5 2.3 %collective-permute-start.7 = (bf16[8,3712]{1,0:T(8,128)(2,1)S(1)}, bf16[8,3712]{1,0:T(8,128)(2,1)S(1)}, u32[]{:S(2)}, u32[]{:S(2)}) collective-permute-start(bf16[8,3712]{1,0:T(8,128)(2,1)S(1)} %collective-permute-done.3.refs_3_), channel_id=1, source_target_pairs={{0,1},{1,0},{2,3},{3,2},{4,5},{5,4},{6,7},{7,6},{8,9},{9,8},{10,11... | collective-permute-start | bytes 178184 | tf_op jit(solution)/shard_map/ppermute | solution.py:79
  14.2 1.2 %collective-permute-start.6 = (bf16[8,3712]{1,0:T(8,128)(2,1)S(1)}, bf16[8,3712]{1,0:T(8,128)(2,1)S(1)}, u32[]{:S(2)}, u32[]{:S(2)}) collective-permute-start(bf16[8,3712]{1,0:T(8,128)(2,1)S(1)} %collective-permute-done.2.refs_2_), channel_id=1, source_target_pairs={{0,1},{1,0},{2,3},{3,2},{4,5},{5,4},{6,7},{7,6},{8,9},{9,8},{10,11... | collective-permute-start | bytes 178184 | tf_op jit(solution)/shard_map/ppermute | solution.py:79
  14.8 1.2 %collective-permute-start.5 = (bf16[8,3712]{1,0:T(8,128)(2,1)S(1)}, bf16[8,3712]{1,0:T(8,128)(2,1)S(1)}, u32[]{:S(2)}, u32[]{:S(2)}) collective-permute-start(bf16[8,3712]{1,0:T(8,128)(2,1)S(1)} %collective-permute-done.1.refs_1_), channel_id=1, source_target_pairs={{0,1},{1,0},{2,3},{3,2},{4,5},{5,4},{6,7},{7,6},{8,9},{9,8},{10,11... | collective-permute-start | bytes 178184 | tf_op jit(solution)/shard_map/ppermute | solution.py:79
  22.1 1.3 %collective-permute-start.8 = (bf16[8,3584]{1,0:T(8,128)(2,1)S(1)}, bf16[8,3584]{1,0:T(8,128)(2,1)S(1)}, u32[]{:S(2)}, u32[]{:S(2)}) collective-permute-start(bf16[8,3584]{1,0:T(8,128)(2,1)S(1)} %get-tuple-element.17), channel_id=1, source_target_pairs={{0,1},{1,0},{2,3},{3,2},{4,5},{5,4},{6,7},{7,6},{8,9},{9,8},{10,11... | collective-permute-start | bytes 172040 | tf_op jit(solution)/shard_map/ppermute | solution.py:79
  22.3 2.6 %collective-permute-start.10 = (bf16[8,3584]{1,0:T(8,128)(2,1)S(1)}, bf16[8,3584]{1,0:T(8,128)(2,1)S(1)}, u32[]{:S(2)}, u32[]{:S(2)}) collective-permute-start(bf16[8,3584]{1,0:T(8,128)(2,1)S(1)} %get-tuple-element.19), channel_id=1, source_target_pairs={{0,1},{1,0},{2,3},{3,2},{4,5},{5,4},{6,7},{7,6},{8,9},{9,8},{10,11... | collective-permute-start | bytes 172040 | tf_op jit(solution)/shard_map/ppermute | solution.py:79
  22.7 2.8 %collective-permute-start.12 = (bf16[8,3584]{1,0:T(8,128)(2,1)S(1)}, bf16[8,3584]{1,0:T(8,128)(2,1)S(1)}, u32[]{:S(2)}, u32[]{:S(2)}) collective-permute-start(bf16[8,3584]{1,0:T(8,128)(2,1)S(1)} %get-tuple-element.21), channel_id=1, source_target_pairs={{0,1},{1,0},{2,3},{3,2},{4,5},{5,4},{6,7},{7,6},{8,9},{9,8},{10,11... | collective-permute-start | bytes 172040 | tf_op jit(solution)/shard_map/ppermute | solution.py:79
  22.8 4.3 %collective-permute-start.14 = (bf16[8,3584]{1,0:T(8,128)(2,1)S(1)}, bf16[8,3584]{1,0:T(8,128)(2,1)S(1)}, u32[]{:S(2)}, u32[]{:S(2)}) collective-permute-start(bf16[8,3584]{1,0:T(8,128)(2,1)S(1)} %get-tuple-element.22), channel_id=1, source_target_pairs={{0,1},{1,0},{2,3},{3,2},{4,5},{5,4},{6,7},{7,6},{8,9},{9,8},{10,11... | collective-permute-start | bytes 172040 | tf_op jit(solution)/shard_map/ppermute | solution.py:79
  23.4 5.5 %collective-permute-start.9 = (bf16[8,3584]{1,0:T(8,128)(2,1)S(1)}, bf16[8,3584]{1,0:T(8,128)(2,1)S(1)}, u32[]{:S(2)}, u32[]{:S(2)}) collective-permute-start(bf16[8,3584]{1,0:T(8,128)(2,1)S(1)} %add.4), channel_id=1, source_target_pairs={{0,6},{1,7},{2,4},{3,5},{4,2},{5,3},{6,0},{7,1},{8,14},{9,15},{10,... | collective-permute-start | bytes 172040 | tf_op jit(solution)/shard_map/ppermute | solution.py:79
  25.0 4.2 %collective-permute-start.11 = (bf16[8,3584]{1,0:T(8,128)(2,1)S(1)}, bf16[8,3584]{1,0:T(8,128)(2,1)S(1)}, u32[]{:S(2)}, u32[]{:S(2)}) collective-permute-start(bf16[8,3584]{1,0:T(8,128)(2,1)S(1)} %add.5), channel_id=1, source_target_pairs={{0,4},{1,5},{2,6},{3,7},{4,0},{5,1},{6,2},{7,3},{8,12},{9,13},{10,... | collective-permute-start | bytes 172040 | tf_op jit(solution)/shard_map/ppermute | solution.py:79
  25.5 4.2 %collective-permute-start.13 = (bf16[8,3584]{1,0:T(8,128)(2,1)S(1)}, bf16[8,3584]{1,0:T(8,128)(2,1)S(1)}, u32[]{:S(2)}, u32[]{:S(2)}) collective-permute-start(bf16[8,3584]{1,0:T(8,128)(2,1)S(1)} %add.6), channel_id=1, source_target_pairs={{0,2},{1,3},{2,0},{3,1},{4,6},{5,7},{6,4},{7,5},{8,10},{9,11},{10,... | collective-permute-start | bytes 172040 | tf_op jit(solution)/shard_map/ppermute | solution.py:79
  29.8 4.8 %collective-permute-start.15 = (bf16[4,3584]{1,0:T(4,128)(2,1)S(1)}, bf16[4,3584]{1,0:T(4,128)(2,1)S(1)}, u32[]{:S(2)}, u32[]{:S(2)}) collective-permute-start(bf16[4,3584]{1,0:T(4,128)(2,1)S(1)} %get-tuple-element.24), channel_id=1, source_target_pairs={{0,8},{1,9},{2,10},{3,11},{4,12},{5,13},{6,14},{7,15},{8,0},{9,1},... | collective-permute-start | bytes 86024 | tf_op jit(solution)/shard_map/ppermute | solution.py:79

commit v6 on v5

--- a/solution.py
+++ b/solution.py
@@ -193,9 +193,9 @@
     experts = lax.axis_size("expert")
     rows, width = tokens.shape
     units = gate_w.shape[2]
-    far = experts // 2
-    middle = [d for d in range(2, far, 2)]
-    half = rows * far
+    far = experts // 2 + 1
+    middle = [d + 1 for d in range(2, far - 1, 2)]
+    half = rows * experts // 2
     fill = max(2 * half, 128)
     params = pltpu.CompilerParams(vmem_limit_bytes=6 * 2**20)
     gate_w = pltpu.with_memory_space_constraint(gate_w, pltpu.VMEM)

time: 35.4 us -> 34.2 us (0.966)
  waiting for transfers between devices: 12.3 us -> 11.6 us
  starting transfers between devices: 15.1 us -> 14.6 us
    ppermute x16, waiting for transfers between devices: 12.3 us -> 11.6 us  [swap(): return lax.ppermute(x, 'expert', [(i, i ^ distance) for i in range(count)])]
    ppermute x16, starting transfers between devices: 15.1 us -> 14.6 us  [swap(): return lax.ppermute(x, 'expert', [(i, i ^ distance) for i in range(count)])]
where the time goes in v6:
time: 34.2 us; the launch traced here: 34.1 us
  starting transfers between devices  14.6 us (43%)
  waiting for transfers between devices  11.6 us (34%)
  Pallas kernels  7.81 us (23%)
    ppermute x16, starting transfers between devices, swap(): return lax.ppermute(x, 'expert', [(i, i ^ distance) for i in range(count)])  14.6 us
    ppermute x16, waiting for transfers between devices, swap(): return lax.ppermute(x, 'expert', [(i, i ^ distance) for i in range(count)])  11.6 us
    pallas_call x1, Pallas kernels, shards(): pl.pallas_call(lambda *refs: expert_kernel(256, fill, experts, count, *re...  6.02 us
    pallas_call x1, Pallas kernels, shards(): pl.pallas_call(lambda *refs: pack_kernel(experts, *refs), out_shape=jax.S...  1.06 us
  transfers between devices with their start and end apart: 16, of which 11 were waited for; matrix products, arithmetic and copies ran while one was open for 0% of the time, Pallas kernels for 0%

profile of v6, /device:TPU:0, one launch (start us, length us, event | category | flops | bytes accessed | tf_op | source)
XLA Modules:
  0.0 34.1 jit_solution(11762331862719337998)
XLA Ops:
  0.0 1.1 %pack.1.refs_0_ = bf16[4,3712]{1,0:T(4,128)(2,1)S(1)} custom-call(bf16[4,3584]{1,0:T(4,128)(2,1)} %refs_0_.1, s32[4,8]{1,0:T(4,128)} %refs_1_.1, f32[4,8]{1,0:T(4,128)} %refs_2_.1), custom_call_target="tpu_custom_call" | custom-call | flops 40000000000 | bytes 100000000 | tf_op jit(solution)/shard_map/pack/pallas_call | solution.py:207
  1.1 3.5 %collective-permute-start = (bf16[4,3712]{1,0:T(4,128)(2,1)S(1)}, bf16[4,3712]{1,0:T(4,128)(2,1)S(1)}, u32[]{:S(2)}, u32[]{:S(2)}) collective-permute-start(bf16[4,3712]{1,0:T(4,128)(2,1)S(1)} %pack.1.refs_0_), channel_id=1, source_target_pairs={{0,9},{1,8},{2,11},{3,10},{4,13},{5,12},{6,15},{7,14},{8,1},{9,0},... | collective-permute-start | bytes 89096 | tf_op jit(solution)/shard_map/ppermute | solution.py:79
  4.6 1.7 %collective-permute-done.refs_1_ = bf16[4,3712]{1,0:T(4,128)(2,1)S(1)} collective-permute-done((bf16[4,3712]{1,0:T(4,128)(2,1)S(1)}, bf16[4,3712]{1,0:T(4,128)(2,1)S(1)}, u32[]{:S(2)}, u32[]{:S(2)}) %collective-permute-start) | collective-permute-done | bytes 29728 | tf_op jit(solution)/shard_map/ppermute | solution.py:79
  6.4 2.8 %collective-permute-start.3 = (bf16[8,3712]{1,0:T(8,128)(2,1)S(1)}, bf16[8,3712]{1,0:T(8,128)(2,1)S(1)}, u32[]{:S(2)}, u32[]{:S(2)}) collective-permute-start(bf16[8,3712]{1,0:T(8,128)(2,1)S(1)} %join.1.refs_0_), channel_id=1, source_target_pairs={{0,7},{1,6},{2,5},{3,4},{4,3},{5,2},{6,1},{7,0},{8,15},{9,14},{10,... | collective-permute-start | bytes 178184 | tf_op jit(solution)/shard_map/ppermute | solution.py:79
  9.2 0.5 %collective-permute-start.2 = (bf16[8,3712]{1,0:T(8,128)(2,1)S(1)}, bf16[8,3712]{1,0:T(8,128)(2,1)S(1)}, u32[]{:S(2)}, u32[]{:S(2)}) collective-permute-start(bf16[8,3712]{1,0:T(8,128)(2,1)S(1)} %join.1.refs_0_), channel_id=1, source_target_pairs={{0,5},{1,4},{2,7},{3,6},{4,1},{5,0},{6,3},{7,2},{8,13},{9,12},{10,... | collective-permute-start | bytes 178184 | tf_op jit(solution)/shard_map/ppermute | solution.py:79
  9.7 0.2 collective-permute-start.1
  9.9 0.1 collective-permute-start.4
  9.9 1.6 %collective-permute-done.3.refs_3_ = bf16[8,3712]{1,0:T(8,128)(2,1)S(1)} collective-permute-done((bf16[8,3712]{1,0:T(8,128)(2,1)S(1)}, bf16[8,3712]{1,0:T(8,128)(2,1)S(1)}, u32[]{:S(2)}, u32[]{:S(2)}) %collective-permute-start.3) | collective-permute-done | bytes 59424 | tf_op jit(solution)/shard_map/ppermute | solution.py:79
  11.5 0.0 collective-permute-start.7
  11.5 1.4 %collective-permute-done.2.refs_2_ = bf16[8,3712]{1,0:T(8,128)(2,1)S(1)} collective-permute-done((bf16[8,3712]{1,0:T(8,128)(2,1)S(1)}, bf16[8,3712]{1,0:T(8,128)(2,1)S(1)}, u32[]{:S(2)}, u32[]{:S(2)}) %collective-permute-start.2) | collective-permute-done | bytes 59424 | tf_op jit(solution)/shard_map/ppermute | solution.py:79
  12.9 0.7 %collective-permute-start.6 = (bf16[8,3712]{1,0:T(8,128)(2,1)S(1)}, bf16[8,3712]{1,0:T(8,128)(2,1)S(1)}, u32[]{:S(2)}, u32[]{:S(2)}) collective-permute-start(bf16[8,3712]{1,0:T(8,128)(2,1)S(1)} %collective-permute-done.2.refs_2_), channel_id=1, source_target_pairs={{0,1},{1,0},{2,3},{3,2},{4,5},{5,4},{6,7},{7,6},{8,9},{9,8},{10,11... | collective-permute-start | bytes 178184 | tf_op jit(solution)/shard_map/ppermute | solution.py:79
  13.6 0.1 collective-permute-done.1.refs_1_
  13.7 0.1 collective-permute-start.5
  13.8 0.0 collective-permute-done.4.refs_4_
  13.8 0.7 %collective-permute-done.6.refs_6_ = bf16[8,3712]{1,0:T(8,128)(2,1)S(1)} collective-permute-done((bf16[8,3712]{1,0:T(8,128)(2,1)S(1)}, bf16[8,3712]{1,0:T(8,128)(2,1)S(1)}, u32[]{:S(2)}, u32[]{:S(2)}) %collective-permute-start.6) | collective-permute-done | bytes 59424 | tf_op jit(solution)/shard_map/ppermute | solution.py:79
  14.5 0.5 %collective-permute-done.5.refs_5_ = bf16[8,3712]{1,0:T(8,128)(2,1)S(1)} collective-permute-done((bf16[8,3712]{1,0:T(8,128)(2,1)S(1)}, bf16[8,3712]{1,0:T(8,128)(2,1)S(1)}, u32[]{:S(2)}, u32[]{:S(2)}) %collective-permute-start.5) | collective-permute-done | bytes 59424 | tf_op jit(solution)/shard_map/ppermute | solution.py:79
  14.9 6.0 %expert.1 = (f32[8,3584]{1,0:T(8,128)S(1)}, f32[8,3584]{1,0:T(8,128)S(1)}, f32[8,3584]{1,0:T(8,128)S(1)}, f32[8,3584]{1,0:T(8,128)S(1)}, bf16[8,3584]{1,0:T(8,12...) custom-call(bf16[8,3712]{1,0:T(8,128)(2,1)S(1)} %join.1.refs_0_, ...), custom_call_target="tpu_custom_call" | custom-call | tf_op jit(solution)/shard_map/expert/pallas_call | solution.py:227
  20.9 0.2 collective-permute-start.8
  21.2 0.4 %collective-permute-start.10 = (bf16[8,3584]{1,0:T(8,128)(2,1)S(1)}, bf16[8,3584]{1,0:T(8,128)(2,1)S(1)}, u32[]{:S(2)}, u32[]{:S(2)}) collective-permute-start(bf16[8,3584]{1,0:T(8,128)(2,1)S(1)} %get-tuple-element.19), channel_id=1, source_target_pairs={{0,1},{1,0},{2,3},{3,2},{4,5},{5,4},{6,7},{7,6},{8,9},{9,8},{10,11... | collective-permute-start | bytes 172040 | tf_op jit(solution)/shard_map/ppermute | solution.py:79
  21.5 0.1 collective-permute-start.12
  21.7 0.4 %collective-permute-start.14 = (bf16[8,3584]{1,0:T(8,128)(2,1)S(1)}, bf16[8,3584]{1,0:T(8,128)(2,1)S(1)}, u32[]{:S(2)}, u32[]{:S(2)}) collective-permute-start(bf16[8,3584]{1,0:T(8,128)(2,1)S(1)} %get-tuple-element.22), channel_id=1, source_target_pairs={{0,1},{1,0},{2,3},{3,2},{4,5},{5,4},{6,7},{7,6},{8,9},{9,8},{10,11... | collective-permute-start | bytes 172040 | tf_op jit(solution)/shard_map/ppermute | solution.py:79
  22.0 0.2 collective-permute-done.8.got_ref
  22.3 2.4 %collective-permute-start.9 = (bf16[8,3584]{1,0:T(8,128)(2,1)S(1)}, bf16[8,3584]{1,0:T(8,128)(2,1)S(1)}, u32[]{:S(2)}, u32[]{:S(2)}) collective-permute-start(bf16[8,3584]{1,0:T(8,128)(2,1)S(1)} %add.4), channel_id=1, source_target_pairs={{0,7},{1,6},{2,5},{3,4},{4,3},{5,2},{6,1},{7,0},{8,15},{9,14},{10,... | collective-permute-start | bytes 172040 | tf_op jit(solution)/shard_map/ppermute | solution.py:79
  24.7 0.5 %collective-permute-start.11 = (bf16[8,3584]{1,0:T(8,128)(2,1)S(1)}, bf16[8,3584]{1,0:T(8,128)(2,1)S(1)}, u32[]{:S(2)}, u32[]{:S(2)}) collective-permute-start(bf16[8,3584]{1,0:T(8,128)(2,1)S(1)} %add.5), channel_id=1, source_target_pairs={{0,5},{1,4},{2,7},{3,6},{4,1},{5,0},{6,3},{7,2},{8,13},{9,12},{10,... | collective-permute-start | bytes 172040 | tf_op jit(solution)/shard_map/ppermute | solution.py:79
  25.2 0.3 collective-permute-start.13
  25.5 0.0 collective-permute-done.14.refs_3_
  25.5 1.6 %collective-permute-done.9.refs_0_ = bf16[8,3584]{1,0:T(8,128)(2,1)S(1)} collective-permute-done((bf16[8,3584]{1,0:T(8,128)(2,1)S(1)}, bf16[8,3584]{1,0:T(8,128)(2,1)S(1)}, u32[]{:S(2)}, u32[]{:S(2)}) %collective-permute-start.9) | collective-permute-done | bytes 57376 | tf_op jit(solution)/shard_map/ppermute | solution.py:79
  27.1 1.4 %collective-permute-done.11.refs_1_ = bf16[8,3584]{1,0:T(8,128)(2,1)S(1)} collective-permute-done((bf16[8,3584]{1,0:T(8,128)(2,1)S(1)}, bf16[8,3584]{1,0:T(8,128)(2,1)S(1)}, u32[]{:S(2)}, u32[]{:S(2)}) %collective-permute-start.11) | collective-permute-done | bytes 57376 | tf_op jit(solution)/shard_map/ppermute | solution.py:79
  28.5 0.6 %collective-permute-done.13.refs_2_ = bf16[8,3584]{1,0:T(8,128)(2,1)S(1)} collective-permute-done((bf16[8,3584]{1,0:T(8,128)(2,1)S(1)}, bf16[8,3584]{1,0:T(8,128)(2,1)S(1)}, u32[]{:S(2)}, u32[]{:S(2)}) %collective-permute-start.13) | collective-permute-done | bytes 57376 | tf_op jit(solution)/shard_map/ppermute | solution.py:79
  29.2 2.4 %collective-permute-start.15 = (bf16[4,3584]{1,0:T(4,128)(2,1)S(1)}, bf16[4,3584]{1,0:T(4,128)(2,1)S(1)}, u32[]{:S(2)}, u32[]{:S(2)}) collective-permute-start(bf16[4,3584]{1,0:T(4,128)(2,1)S(1)} %get-tuple-element.24), channel_id=1, source_target_pairs={{0,9},{1,8},{2,11},{3,10},{4,13},{5,12},{6,15},{7,14},{8,1},{9,0},... | collective-permute-start | bytes 86024 | tf_op jit(solution)/shard_map/ppermute | solution.py:79
  31.6 1.8 %collective-permute-done.15.got_ref = bf16[4,3584]{1,0:T(4,128)(2,1)S(1)} collective-permute-done((bf16[4,3584]{1,0:T(4,128)(2,1)S(1)}, bf16[4,3584]{1,0:T(4,128)(2,1)S(1)}, u32[]{:S(2)}, u32[]{:S(2)}) %collective-permute-start.15) | collective-permute-done | bytes 28704 | tf_op jit(solution)/shard_map/ppermute | solution.py:79
  33.5 0.6 %add.7 = bf16[4,3584]{1,0:T(4,128)(2,1)} custom-call(f32[4,3584]{1,0:T(4,128)S(1)} %get-tuple-element.23.kept_ref, bf16[4,3584]{1,0:T(4,128)(2,1)S(1)} %collective-permute-done.15.got_ref), custom_call_target="tpu_custom_call" | custom-call | tf_op jit(solution)/shard_map/add/pallas_call | solution.py:182
  (14 shorter events, 0.1 us)
Async XLA Ops:
  0.0 14.9 %copy-start.2 = (bf16[1,2048,3584]{2,1,0:T(8,128)(2,1)S(1)}, bf16[1,2048,3584]{2,1,0:T(8,128)(2,1)}, u32[]{:S(2)}) copy-start(bf16[1,2048,3584]{2,1,0:T(8,128)(2,1)} %refs_10_.1) | copy-start | bytes 44040196
  0.0 14.9 %copy-start.1 = (bf16[1,3584,2048]{2,1,0:T(8,128)(2,1)S(1)}, bf16[1,3584,2048]{2,1,0:T(8,128)(2,1)}, u32[]{:S(2)}) copy-start(bf16[1,3584,2048]{2,1,0:T(8,128)(2,1)} %refs_9_.1) | copy-start | bytes 44040196
  0.0 14.9 %copy-start = (bf16[1,3584,2048]{2,1,0:T(8,128)(2,1)S(1)}, bf16[1,3584,2048]{2,1,0:T(8,128)(2,1)}, u32[]{:S(2)}) copy-start(bf16[1,3584,2048]{2,1,0:T(8,128)(2,1)} %refs_8_.1) | copy-start | bytes 44040196
  1.1 5.3 %collective-permute-start = (bf16[4,3712]{1,0:T(4,128)(2,1)S(1)}, bf16[4,3712]{1,0:T(4,128)(2,1)S(1)}, u32[]{:S(2)}, u32[]{:S(2)}) collective-permute-start(bf16[4,3712]{1,0:T(4,128)(2,1)S(1)} %pack.1.refs_0_), channel_id=1, source_target_pairs={{0,9},{1,8},{2,11},{3,10},{4,13},{5,12},{6,15},{7,14},{8,1},{9,0},... | collective-permute-start | bytes 89096 | tf_op jit(solution)/shard_map/ppermute | solution.py:79
  6.4 5.2 %collective-permute-start.3 = (bf16[8,3712]{1,0:T(8,128)(2,1)S(1)}, bf16[8,3712]{1,0:T(8,128)(2,1)S(1)}, u32[]{:S(2)}, u32[]{:S(2)}) collective-permute-start(bf16[8,3712]{1,0:T(8,128)(2,1)S(1)} %join.1.refs_0_), channel_id=1, source_target_pairs={{0,7},{1,6},{2,5},{3,4},{4,3},{5,2},{6,1},{7,0},{8,15},{9,14},{10,... | collective-permute-start | bytes 178184 | tf_op jit(solution)/shard_map/ppermute | solution.py:79
  9.2 3.7 %collective-permute-start.2 = (bf16[8,3712]{1,0:T(8,128)(2,1)S(1)}, bf16[8,3712]{1,0:T(8,128)(2,1)S(1)}, u32[]{:S(2)}, u32[]{:S(2)}) collective-permute-start(bf16[8,3712]{1,0:T(8,128)(2,1)S(1)} %join.1.refs_0_), channel_id=1, source_target_pairs={{0,5},{1,4},{2,7},{3,6},{4,1},{5,0},{6,3},{7,2},{8,13},{9,12},{10,... | collective-permute-start | bytes 178184 | tf_op jit(solution)/shard_map/ppermute | solution.py:79
  9.7 4.0 %collective-permute-start.1 = (bf16[8,3712]{1,0:T(8,128)(2,1)S(1)}, bf16[8,3712]{1,0:T(8,128)(2,1)S(1)}, u32[]{:S(2)}, u32[]{:S(2)}) collective-permute-start(bf16[8,3712]{1,0:T(8,128)(2,1)S(1)} %join.1.refs_0_), channel_id=1, source_target_pairs={{0,3},{1,2},{2,1},{3,0},{4,7},{5,6},{6,5},{7,4},{8,11},{9,10},{10,... | collective-permute-start | bytes 178184 | tf_op jit(solution)/shard_map/ppermute | solution.py:79
  9.9 3.9 %collective-permute-start.4 = (bf16[8,3712]{1,0:T(8,128)(2,1)S(1)}, bf16[8,3712]{1,0:T(8,128)(2,1)S(1)}, u32[]{:S(2)}, u32[]{:S(2)}) collective-permute-start(bf16[8,3712]{1,0:T(8,128)(2,1)S(1)} %join.1.refs_0_), channel_id=1, source_target_pairs={{0,1},{1,0},{2,3},{3,2},{4,5},{5,4},{6,7},{7,6},{8,9},{9,8},{10,11... | collective-permute-start | bytes 178184 | tf_op jit(solution)/shard_map/ppermute | solution.py:79
  11.5 2.3 %collective-permute-start.7 = (bf16[8,3712]{1,0:T(8,128)(2,1)S(1)}, bf16[8,3712]{1,0:T(8,128)(2,1)S(1)}, u32[]{:S(2)}, u32[]{:S(2)}) collective-permute-start(bf16[8,3712]{1,0:T(8,128)(2,1)S(1)} %collective-permute-done.3.refs_3_), channel_id=1, source_target_pairs={{0,1},{1,0},{2,3},{3,2},{4,5},{5,4},{6,7},{7,6},{8,9},{9,8},{10,11... | collective-permute-start | bytes 178184 | tf_op jit(solution)/shard_map/ppermute | solution.py:79
  12.9 1.6 %collective-permute-start.6 = (bf16[8,3712]{1,0:T(8,128)(2,1)S(1)}, bf16[8,3712]{1,0:T(8,128)(2,1)S(1)}, u32[]{:S(2)}, u32[]{:S(2)}) collective-permute-start(bf16[8,3712]{1,0:T(8,128)(2,1)S(1)} %collective-permute-done.2.refs_2_), channel_id=1, source_target_pairs={{0,1},{1,0},{2,3},{3,2},{4,5},{5,4},{6,7},{7,6},{8,9},{9,8},{10,11... | collective-permute-start | bytes 178184 | tf_op jit(solution)/shard_map/ppermute | solution.py:79
  13.7 1.2 %collective-permute-start.5 = (bf16[8,3712]{1,0:T(8,128)(2,1)S(1)}, bf16[8,3712]{1,0:T(8,128)(2,1)S(1)}, u32[]{:S(2)}, u32[]{:S(2)}) collective-permute-start(bf16[8,3712]{1,0:T(8,128)(2,1)S(1)} %collective-permute-done.1.refs_1_), channel_id=1, source_target_pairs={{0,1},{1,0},{2,3},{3,2},{4,5},{5,4},{6,7},{7,6},{8,9},{9,8},{10,11... | collective-permute-start | bytes 178184 | tf_op jit(solution)/shard_map/ppermute | solution.py:79
  20.9 1.3 %collective-permute-start.8 = (bf16[8,3584]{1,0:T(8,128)(2,1)S(1)}, bf16[8,3584]{1,0:T(8,128)(2,1)S(1)}, u32[]{:S(2)}, u32[]{:S(2)}) collective-permute-start(bf16[8,3584]{1,0:T(8,128)(2,1)S(1)} %get-tuple-element.17), channel_id=1, source_target_pairs={{0,1},{1,0},{2,3},{3,2},{4,5},{5,4},{6,7},{7,6},{8,9},{9,8},{10,11... | collective-permute-start | bytes 172040 | tf_op jit(solution)/shard_map/ppermute | solution.py:79
  21.2 3.5 %collective-permute-start.10 = (bf16[8,3584]{1,0:T(8,128)(2,1)S(1)}, bf16[8,3584]{1,0:T(8,128)(2,1)S(1)}, u32[]{:S(2)}, u32[]{:S(2)}) collective-permute-start(bf16[8,3584]{1,0:T(8,128)(2,1)S(1)} %get-tuple-element.19), channel_id=1, source_target_pairs={{0,1},{1,0},{2,3},{3,2},{4,5},{5,4},{6,7},{7,6},{8,9},{9,8},{10,11... | collective-permute-start | bytes 172040 | tf_op jit(solution)/shard_map/ppermute | solution.py:79
  21.5 3.7 %collective-permute-start.12 = (bf16[8,3584]{1,0:T(8,128)(2,1)S(1)}, bf16[8,3584]{1,0:T(8,128)(2,1)S(1)}, u32[]{:S(2)}, u32[]{:S(2)}) collective-permute-start(bf16[8,3584]{1,0:T(8,128)(2,1)S(1)} %get-tuple-element.21), channel_id=1, source_target_pairs={{0,1},{1,0},{2,3},{3,2},{4,5},{5,4},{6,7},{7,6},{8,9},{9,8},{10,11... | collective-permute-start | bytes 172040 | tf_op jit(solution)/shard_map/ppermute | solution.py:79
  21.7 3.8 %collective-permute-start.14 = (bf16[8,3584]{1,0:T(8,128)(2,1)S(1)}, bf16[8,3584]{1,0:T(8,128)(2,1)S(1)}, u32[]{:S(2)}, u32[]{:S(2)}) collective-permute-start(bf16[8,3584]{1,0:T(8,128)(2,1)S(1)} %get-tuple-element.22), channel_id=1, source_target_pairs={{0,1},{1,0},{2,3},{3,2},{4,5},{5,4},{6,7},{7,6},{8,9},{9,8},{10,11... | collective-permute-start | bytes 172040 | tf_op jit(solution)/shard_map/ppermute | solution.py:79
  22.3 4.8 %collective-permute-start.9 = (bf16[8,3584]{1,0:T(8,128)(2,1)S(1)}, bf16[8,3584]{1,0:T(8,128)(2,1)S(1)}, u32[]{:S(2)}, u32[]{:S(2)}) collective-permute-start(bf16[8,3584]{1,0:T(8,128)(2,1)S(1)} %add.4), channel_id=1, source_target_pairs={{0,7},{1,6},{2,5},{3,4},{4,3},{5,2},{6,1},{7,0},{8,15},{9,14},{10,... | collective-permute-start | bytes 172040 | tf_op jit(solution)/shard_map/ppermute | solution.py:79
  24.7 3.8 %collective-permute-start.11 = (bf16[8,3584]{1,0:T(8,128)(2,1)S(1)}, bf16[8,3584]{1,0:T(8,128)(2,1)S(1)}, u32[]{:S(2)}, u32[]{:S(2)}) collective-permute-start(bf16[8,3584]{1,0:T(8,128)(2,1)S(1)} %add.5), channel_id=1, source_target_pairs={{0,5},{1,4},{2,7},{3,6},{4,1},{5,0},{6,3},{7,2},{8,13},{9,12},{10,... | collective-permute-start | bytes 172040 | tf_op jit(solution)/shard_map/ppermute | solution.py:79
  25.2 3.9 %collective-permute-start.13 = (bf16[8,3584]{1,0:T(8,128)(2,1)S(1)}, bf16[8,3584]{1,0:T(8,128)(2,1)S(1)}, u32[]{:S(2)}, u32[]{:S(2)}) collective-permute-start(bf16[8,3584]{1,0:T(8,128)(2,1)S(1)} %add.6), channel_id=1, source_target_pairs={{0,3},{1,2},{2,1},{3,0},{4,7},{5,6},{6,5},{7,4},{8,11},{9,10},{10,... | collective-permute-start | bytes 172040 | tf_op jit(solution)/shard_map/ppermute | solution.py:79
  29.2 4.3 %collective-permute-start.15 = (bf16[4,3584]{1,0:T(4,128)(2,1)S(1)}, bf16[4,3584]{1,0:T(4,128)(2,1)S(1)}, u32[]{:S(2)}, u32[]{:S(2)}) collective-permute-start(bf16[4,3584]{1,0:T(4,128)(2,1)S(1)} %get-tuple-element.24), channel_id=1, source_target_pairs={{0,9},{1,8},{2,11},{3,10},{4,13},{5,12},{6,15},{7,14},{8,1},{9,0},... | collective-permute-start | bytes 86024 | tf_op jit(solution)/shard_map/ppermute | solution.py:79

commit v7 on v4

--- a/solution.py
+++ b/solution.py
@@ -153,24 +153,32 @@
 
 
 def down_kernel(step, fill, hidden_ref, weight_ref, down_ref, *out_refs):
-    keep_refs, send_refs = out_refs[: len(out_refs) // 2], out_refs[len(out_refs) // 2 :]
     hidden = filled(hidden_ref[...], fill)
     weight = weight_ref[:, :1]
-    rows = keep_refs[0].shape[0]
     for start in range(0, down_ref.shape[2], step):
         cut = slice(start, start + step)
         out = jnp.dot(hidden, down_ref[0, :, cut], preferred_element_type=jnp.float32)
         part = out[: weight.shape[0]].astype(jnp.bfloat16).astype(jnp.float32) * weight
-        for i, ref in enumerate(keep_refs + send_refs):
-            ref[:, cut] = part[i * rows : (i + 1) * rows].astype(ref.dtype)
+        base = 0
+        for ref in out_refs:
+            ref[:, cut] = part[base : base + ref.shape[0]].astype(ref.dtype)
+            base += ref.shape[0]
+
+
+def split_kernel(kept_ref, got_ref, *out_refs):
+    total = kept_ref[...] + got_ref[...].astype(jnp.float32)
+    base = 0
+    for ref in out_refs:
+        ref[...] = total[base : base + ref.shape[0]].astype(ref.dtype)
+        base += ref.shape[0]
 
 
 def add_kernel(kept_ref, got_ref, out_ref):
     out_ref[...] = (kept_ref[...] + got_ref[...].astype(jnp.float32)).astype(out_ref.dtype)
 
 
-def fold_kernel(kept_ref, *refs):
-    got_refs, (keep_ref, send_ref) = refs[:-2], refs[-2:]
+def fold_kernel(*refs):
+    got_refs, (kept_ref, keep_ref, send_ref) = refs[:-3], refs[-3:]
     total = kept_ref[...]
     for got_ref in got_refs:
         total = total + got_ref[...].astype(jnp.float32)
@@ -179,6 +187,18 @@
     send_ref[...] = total[half:].astype(send_ref.dtype)
 
 
+def split(kept, got, dtypes, params):
+    rows, width = kept.shape
+    return pl.pallas_call(
+        split_kernel,
+        out_shape=[jax.ShapeDtypeStruct((rows // len(dtypes), width), dtype) for dtype in dtypes],
+        in_specs=vmem(2),
+        out_specs=vmem(len(dtypes)),
+        compiler_params=params,
+        name="split",
+    )(kept, got)
+
+
 def add(kept, got, params):
     return pl.pallas_call(
         add_kernel,
@@ -194,9 +214,9 @@
     experts = lax.axis_size("expert")
     rows, width = tokens.shape
     units = gate_w.shape[2]
-    far = experts // 2
-    middle = [d for d in range(2, far, 2)]
-    half = rows * far
+    far = experts // 2 + 1
+    middle = [d + 1 for d in range(2, far - 1, 2)]
+    half = rows * experts // 2
     fill = max(2 * half, 128)
     params = pltpu.CompilerParams(vmem_limit_bytes=6 * 2**20)
     gate_w = pltpu.with_memory_space_constraint(gate_w, pltpu.VMEM)
@@ -238,29 +258,30 @@
     count = len(middle) + 1
     kept_and_sent = pl.pallas_call(
         lambda *refs: down_kernel(256, fill, *refs),
-        out_shape=[jax.ShapeDtypeStruct((2 * rows, width), jnp.float32)] * count
-        + [jax.ShapeDtypeStruct((2 * rows, width), jnp.bfloat16)] * count,
+        out_shape=[
+            jax.ShapeDtypeStruct((half // 2, width), dtype)
+            for dtype in (jnp.float32, jnp.float32, jnp.bfloat16, jnp.bfloat16)
+        ],
         in_specs=vmem(3),
-        out_specs=vmem(2 * count),
+        out_specs=vmem(4),
         compiler_params=params,
         name="down",
     )(hidden, weight, down_w)
-    kept, sent = kept_and_sent[:count], kept_and_sent[count:]
-    gots = [
-        swap(add(kept[i], swap(sent[i], 1), params), middle[i - 1]) for i in range(count - 1, 0, -1)
-    ]
-    gots.append(swap(sent[0], 1))
+    kept_low, kept_high, sent_low, sent_high = kept_and_sent
+    third, corner = split(kept_high, swap(sent_high, 1), (jnp.bfloat16, jnp.bfloat16), params)
+    near, second = split(kept_low, swap(sent_low, 1), (jnp.float32, jnp.bfloat16), params)
+    gots = [swap(send, d) for send, d in zip((corner, third, second), middle[::-1])]
     keep, send = pl.pallas_call(
         fold_kernel,
         out_shape=[
             jax.ShapeDtypeStruct((rows, width), jnp.float32),
             jax.ShapeDtypeStruct((rows, width), jnp.bfloat16),
         ],
-        in_specs=vmem(1 + count),
+        in_specs=vmem(count),
         out_specs=vmem(2),
         compiler_params=params,
         name="fold",
-    )(kept[0], *gots)
+    )(*gots, near)
     return add(keep, swap(send, far), params)
 
 

time: 35.5 us -> 34.1 us (0.961)
  starting transfers between devices: 15.1 us -> 14.4 us
  waiting for transfers between devices: 12.1 us -> 11.5 us
    ppermute x16 -> x14, starting transfers between devices: 15.1 us -> 14.4 us  [swap(): return lax.ppermute(x, 'expert', [(i, i ^ distance) for i in range(count)])]
    ppermute x16 -> x14, waiting for transfers between devices: 12.1 us -> 11.5 us  [swap(): return lax.ppermute(x, 'expert', [(i, i ^ distance) for i in range(count)])]
  transfers between devices with their start and end apart: 16 -> 14, of which waited for: 11 -> 11; matrix products, arithmetic and copies ran while one was open for 0% -> 0% of each run, Pallas kernels for 0% -> 0%
where the time goes in v7:
time: 34.1 us; the launch traced here: 34 us
  starting transfers between devices  14.4 us (42%)
  waiting for transfers between devices  11.5 us (34%)
  Pallas kernels  7.98 us (23%)
    ppermute x14, starting transfers between devices, swap(): return lax.ppermute(x, 'expert', [(i, i ^ distance) for i in range(count)])  14.4 us
    ppermute x14, waiting for transfers between devices, swap(): return lax.ppermute(x, 'expert', [(i, i ^ distance) for i in range(count)])  11.5 us
    pallas_call x1, Pallas kernels, shards(): pl.pallas_call(lambda *refs: hidden_kernel(256, fill, experts, *refs), ou...  4.08 us
    pallas_call x1, Pallas kernels, shards(): pl.pallas_call(lambda *refs: down_kernel(256, fill, *refs), out_shape=[ja...  2.09 us
    pallas_call x1, Pallas kernels, shards(): pl.pallas_call(lambda *refs: pack_kernel(experts, *refs), out_shape=jax.S...  1.06 us
  transfers between devices with their start and end apart: 14, of which 11 were waited for; matrix products, arithmetic and copies ran while one was open for 0% of the time, Pallas kernels for 0%

profile of v7, /device:TPU:0, one launch (start us, length us, event | category | flops | bytes accessed | tf_op | source)
XLA Modules:
  0.0 34.0 jit_solution(6378328434491048207)
XLA Ops:
  0.0 1.1 %pack.1.refs_0_ = bf16[4,3712]{1,0:T(4,128)(2,1)S(1)} custom-call(bf16[4,3584]{1,0:T(4,128)(2,1)} %refs_0_.1, s32[4,8]{1,0:T(4,128)} %refs_1_.1, f32[4,8]{1,0:T(4,128)} %refs_2_.2), custom_call_target="tpu_custom_call" | custom-call | flops 40000000000 | bytes 100000000 | tf_op jit(solution)/shard_map/pack/pallas_call | solution.py:228
  1.1 3.5 %collective-permute-start = (bf16[4,3712]{1,0:T(4,128)(2,1)S(1)}, bf16[4,3712]{1,0:T(4,128)(2,1)S(1)}, u32[]{:S(2)}, u32[]{:S(2)}) collective-permute-start(bf16[4,3712]{1,0:T(4,128)(2,1)S(1)} %pack.1.refs_0_), channel_id=1, source_target_pairs={{0,9},{1,8},{2,11},{3,10},{4,13},{5,12},{6,15},{7,14},{8,1},{9,0},... | collective-permute-start | bytes 89096 | tf_op jit(solution)/shard_map/ppermute | solution.py:79
  4.6 1.7 %collective-permute-done.refs_1_ = bf16[4,3712]{1,0:T(4,128)(2,1)S(1)} collective-permute-done((bf16[4,3712]{1,0:T(4,128)(2,1)S(1)}, bf16[4,3712]{1,0:T(4,128)(2,1)S(1)}, u32[]{:S(2)}, u32[]{:S(2)}) %collective-permute-start) | collective-permute-done | bytes 29728 | tf_op jit(solution)/shard_map/ppermute | solution.py:79
  6.4 0.0 slice-start.1
  6.4 0.0 slice-start.2
  6.4 0.0 slice-start.3
  6.4 2.8 %collective-permute-start.3 = (bf16[8,3712]{1,0:T(8,128)(2,1)S(1)}, bf16[8,3712]{1,0:T(8,128)(2,1)S(1)}, u32[]{:S(2)}, u32[]{:S(2)}) collective-permute-start(bf16[8,3712]{1,0:T(8,128)(2,1)S(1)} %join.1.refs_0_), channel_id=1, source_target_pairs={{0,7},{1,6},{2,5},{3,4},{4,3},{5,2},{6,1},{7,0},{8,15},{9,14},{10,... | collective-permute-start | bytes 178184 | tf_op jit(solution)/shard_map/ppermute | solution.py:79
  9.2 0.5 %collective-permute-start.2 = (bf16[8,3712]{1,0:T(8,128)(2,1)S(1)}, bf16[8,3712]{1,0:T(8,128)(2,1)S(1)}, u32[]{:S(2)}, u32[]{:S(2)}) collective-permute-start(bf16[8,3712]{1,0:T(8,128)(2,1)S(1)} %join.1.refs_0_), channel_id=1, source_target_pairs={{0,5},{1,4},{2,7},{3,6},{4,1},{5,0},{6,3},{7,2},{8,13},{9,12},{10,... | collective-permute-start | bytes 178184 | tf_op jit(solution)/shard_map/ppermute | solution.py:79
  9.7 0.2 collective-permute-start.1
  9.9 0.1 collective-permute-start.4
  10.0 1.6 %collective-permute-done.3.refs_3_ = bf16[8,3712]{1,0:T(8,128)(2,1)S(1)} collective-permute-done((bf16[8,3712]{1,0:T(8,128)(2,1)S(1)}, bf16[8,3712]{1,0:T(8,128)(2,1)S(1)}, u32[]{:S(2)}, u32[]{:S(2)}) %collective-permute-start.3) | collective-permute-done | bytes 59424 | tf_op jit(solution)/shard_map/ppermute | solution.py:79
  11.6 0.0 collective-permute-start.7
  11.6 1.4 %collective-permute-done.2.refs_2_ = bf16[8,3712]{1,0:T(8,128)(2,1)S(1)} collective-permute-done((bf16[8,3712]{1,0:T(8,128)(2,1)S(1)}, bf16[8,3712]{1,0:T(8,128)(2,1)S(1)}, u32[]{:S(2)}, u32[]{:S(2)}) %collective-permute-start.2) | collective-permute-done | bytes 59424 | tf_op jit(solution)/shard_map/ppermute | solution.py:79
  12.9 0.7 %collective-permute-start.6 = (bf16[8,3712]{1,0:T(8,128)(2,1)S(1)}, bf16[8,3712]{1,0:T(8,128)(2,1)S(1)}, u32[]{:S(2)}, u32[]{:S(2)}) collective-permute-start(bf16[8,3712]{1,0:T(8,128)(2,1)S(1)} %collective-permute-done.2.refs_2_), channel_id=1, source_target_pairs={{0,1},{1,0},{2,3},{3,2},{4,5},{5,4},{6,7},{7,6},{8,9},{9,8},{10,11... | collective-permute-start | bytes 178184 | tf_op jit(solution)/shard_map/ppermute | solution.py:79
  13.6 0.1 collective-permute-done.1.refs_1_
  13.7 0.1 collective-permute-start.5
  13.8 0.7 %collective-permute-done.6.refs_6_ = bf16[8,3712]{1,0:T(8,128)(2,1)S(1)} collective-permute-done((bf16[8,3712]{1,0:T(8,128)(2,1)S(1)}, bf16[8,3712]{1,0:T(8,128)(2,1)S(1)}, u32[]{:S(2)}, u32[]{:S(2)}) %collective-permute-start.6) | collective-permute-done | bytes 59424 | tf_op jit(solution)/shard_map/ppermute | solution.py:79
  14.5 0.5 %collective-permute-done.5.refs_5_ = bf16[8,3712]{1,0:T(8,128)(2,1)S(1)} collective-permute-done((bf16[8,3712]{1,0:T(8,128)(2,1)S(1)}, bf16[8,3712]{1,0:T(8,128)(2,1)S(1)}, u32[]{:S(2)}, u32[]{:S(2)}) %collective-permute-start.5) | collective-permute-done | bytes 59424 | tf_op jit(solution)/shard_map/ppermute | solution.py:79
  14.9 4.1 %hidden.1 = (bf16[64,2048]{1,0:T(8,128)(2,1)S(1)}, f32[64,128]{1,0:T(8,128)S(1)}) custom-call(bf16[8,3712]{1,0:T(8,128)(2,1)S(1)} %join.1.refs_0_, bf16[8,3712]{1,0:T(8,128)(2,1)S(1)} %collective-permute-done.1.refs_1_, bf16[8,3712]{1,0:T(8,128)(2,1)S(1)} %collective-permute-done.2.refs_2_, bf16[8,3712]{1,0:T(8,128)(2,1)S(1)} %collective-permute-done.3.refs_3_, ...), custom_call_target="tpu_custom_call" | custom-call | tf_op jit(solution)/shard_map/hidden/pallas_call | solution.py:247
  19.1 2.1 %down.1 = (f32[16,3584]{1,0:T(8,128)S(1)}, f32[16,3584]{1,0:T(8,128)S(1)}, bf16[16,3584]{1,0:T(8,128)(2,1)S(1)}, bf16[16,3584]{1,0:T(8,128)(2,1)S(1)}) custom-call(bf16[64,2048]{1,0:T(8,128)(2,1)S(1)} %get-tuple-element.17.refs_0_, f32[64,128]{1,0:T(8,128)S(1)} %get-tuple-element.18.refs_1_, bf16[1,2048,3584]{2,1,0:T(8,128)(2,1)S(1)} %bitcast.1), custom_call_target="tpu_custom_call" | custom-call | tf_op jit(solution)/shard_map/down/pallas_call | solution.py:259
  21.2 0.2 collective-permute-start.8
  21.4 0.4 %collective-permute-start.11 = (bf16[16,3584]{1,0:T(8,128)(2,1)S(1)}, bf16[16,3584]{1,0:T(8,128)(2,1)S(1)}, u32[]{:S(2)}, u32[]{:S(2)}) collective-permute-start(bf16[16,3584]{1,0:T(8,128)(2,1)S(1)} %get-tuple-element.24), channel_id=1, source_target_pairs={{0,1},{1,0},{2,3},{3,2},{4,5},{5,4},{6,7},{7,6},{8,9},{9,8},{10,11... | collective-permute-start | bytes 344072 | tf_op jit(solution)/shard_map/ppermute | solution.py:79
  21.8 0.8 %collective-permute-done.8.got_ref = bf16[16,3584]{1,0:T(8,128)(2,1)S(1)} collective-permute-done((bf16[16,3584]{1,0:T(8,128)(2,1)S(1)}, bf16[16,3584]{1,0:T(8,128)(2,1)S(1)}, u32[]{:S(2)}, u32[]{:S(2)}) %collective-permute-start.8) | collective-permute-done | bytes 114720 | tf_op jit(solution)/shard_map/ppermute | solution.py:79
  22.6 2.0 %collective-permute-start.9 = (bf16[8,3584]{1,0:T(8,128)(2,1)S(1)}, bf16[8,3584]{1,0:T(8,128)(2,1)S(1)}, u32[]{:S(2)}, u32[]{:S(2)}) collective-permute-start(bf16[8,3584]{1,0:T(8,128)(2,1)S(1)} %get-tuple-element.21), channel_id=1, source_target_pairs={{0,7},{1,6},{2,5},{3,4},{4,3},{5,2},{6,1},{7,0},{8,15},{9,14},{10,... | collective-permute-start | bytes 172040 | tf_op jit(solution)/shard_map/ppermute | solution.py:79
  24.6 0.4 %collective-permute-start.10 = (bf16[8,3584]{1,0:T(8,128)(2,1)S(1)}, bf16[8,3584]{1,0:T(8,128)(2,1)S(1)}, u32[]{:S(2)}, u32[]{:S(2)}) collective-permute-start(bf16[8,3584]{1,0:T(8,128)(2,1)S(1)} %get-tuple-element.22), channel_id=1, source_target_pairs={{0,5},{1,4},{2,7},{3,6},{4,1},{5,0},{6,3},{7,2},{8,13},{9,12},{10,... | collective-permute-start | bytes 172040 | tf_op jit(solution)/shard_map/ppermute | solution.py:79
  25.0 0.7 %collective-permute-start.12 = (bf16[8,3584]{1,0:T(8,128)(2,1)S(1)}, bf16[8,3584]{1,0:T(8,128)(2,1)S(1)}, u32[]{:S(2)}, u32[]{:S(2)}) collective-permute-start(bf16[8,3584]{1,0:T(8,128)(2,1)S(1)} %get-tuple-element.25), channel_id=1, source_target_pairs={{0,3},{1,2},{2,1},{3,0},{4,7},{5,6},{6,5},{7,4},{8,11},{9,10},{10,... | collective-permute-start | bytes 172040 | tf_op jit(solution)/shard_map/ppermute | solution.py:79
  25.8 1.7 %collective-permute-done.9.refs_0_ = bf16[8,3584]{1,0:T(8,128)(2,1)S(1)} collective-permute-done((bf16[8,3584]{1,0:T(8,128)(2,1)S(1)}, bf16[8,3584]{1,0:T(8,128)(2,1)S(1)}, u32[]{:S(2)}, u32[]{:S(2)}) %collective-permute-start.9) | collective-permute-done | bytes 57376 | tf_op jit(solution)/shard_map/ppermute | solution.py:79
  27.5 0.9 %collective-permute-done.10.refs_1_ = bf16[8,3584]{1,0:T(8,128)(2,1)S(1)} collective-permute-done((bf16[8,3584]{1,0:T(8,128)(2,1)S(1)}, bf16[8,3584]{1,0:T(8,128)(2,1)S(1)}, u32[]{:S(2)}, u32[]{:S(2)}) %collective-permute-start.10) | collective-permute-done | bytes 57376 | tf_op jit(solution)/shard_map/ppermute | solution.py:79
  28.3 0.7 %collective-permute-done.12.refs_2_ = bf16[8,3584]{1,0:T(8,128)(2,1)S(1)} collective-permute-done((bf16[8,3584]{1,0:T(8,128)(2,1)S(1)}, bf16[8,3584]{1,0:T(8,128)(2,1)S(1)}, u32[]{:S(2)}, u32[]{:S(2)}) %collective-permute-start.12) | collective-permute-done | bytes 57376 | tf_op jit(solution)/shard_map/ppermute | solution.py:79
  29.0 2.8 %collective-permute-start.13 = (bf16[4,3584]{1,0:T(4,128)(2,1)S(1)}, bf16[4,3584]{1,0:T(4,128)(2,1)S(1)}, u32[]{:S(2)}, u32[]{:S(2)}) collective-permute-start(bf16[4,3584]{1,0:T(4,128)(2,1)S(1)} %get-tuple-element.28), channel_id=1, source_target_pairs={{0,9},{1,8},{2,11},{3,10},{4,13},{5,12},{6,15},{7,14},{8,1},{9,0},... | collective-permute-start | bytes 86024 | tf_op jit(solution)/shard_map/ppermute | solution.py:79
  31.8 1.6 %collective-permute-done.13.got_ref = bf16[4,3584]{1,0:T(4,128)(2,1)S(1)} collective-permute-done((bf16[4,3584]{1,0:T(4,128)(2,1)S(1)}, bf16[4,3584]{1,0:T(4,128)(2,1)S(1)}, u32[]{:S(2)}, u32[]{:S(2)}) %collective-permute-start.13) | collective-permute-done | bytes 28704 | tf_op jit(solution)/shard_map/ppermute | solution.py:79
  33.4 0.6 %add.1 = bf16[4,3584]{1,0:T(4,128)(2,1)} custom-call(f32[4,3584]{1,0:T(4,128)S(1)} %get-tuple-element.27.kept_ref, bf16[4,3584]{1,0:T(4,128)(2,1)S(1)} %collective-permute-done.13.got_ref), custom_call_target="tpu_custom_call" | custom-call | tf_op jit(solution)/shard_map/add/pallas_call | solution.py:203
  (17 shorter events, 0.1 us)
Async XLA Ops:
  0.0 14.9 %copy-start.1 = (bf16[1,3584,2048]{2,1,0:T(8,128)(2,1)S(1)}, bf16[1,3584,2048]{2,1,0:T(8,128)(2,1)}, u32[]{:S(2)}) copy-start(bf16[1,3584,2048]{2,1,0:T(8,128)(2,1)} %refs_9_.1) | copy-start | bytes 44040196
  0.0 14.9 %copy-start = (bf16[1,3584,2048]{2,1,0:T(8,128)(2,1)S(1)}, bf16[1,3584,2048]{2,1,0:T(8,128)(2,1)}, u32[]{:S(2)}) copy-start(bf16[1,3584,2048]{2,1,0:T(8,128)(2,1)} %refs_8_.1) | copy-start | bytes 44040196
  1.1 5.3 %collective-permute-start = (bf16[4,3712]{1,0:T(4,128)(2,1)S(1)}, bf16[4,3712]{1,0:T(4,128)(2,1)S(1)}, u32[]{:S(2)}, u32[]{:S(2)}) collective-permute-start(bf16[4,3712]{1,0:T(4,128)(2,1)S(1)} %pack.1.refs_0_), channel_id=1, source_target_pairs={{0,9},{1,8},{2,11},{3,10},{4,13},{5,12},{6,15},{7,14},{8,1},{9,0},... | collective-permute-start | bytes 89096 | tf_op jit(solution)/shard_map/ppermute | solution.py:79
  6.3 12.7 %slice-start = ((s8[14680064]{0:T(1024)(128)(4,1)}), s8[4194304]{0:T(1024)(128)(4,1)S(1)}, s32[]{:S(2)}) async-start(s8[14680064]{0:T(1024)(128)(4,1)} %bitcast), calls=%async_computation | async-start | bytes 8388608
  6.4 12.7 %slice-start.1 = ((s8[14680064]{0:T(1024)(128)(4,1)}), s8[4194304]{0:T(1024)(128)(4,1)S(1)}, s32[]{:S(2)}) async-start(s8[14680064]{0:T(1024)(128)(4,1)} %bitcast), calls=%async_computation.1 | async-start | bytes 8388608
  6.4 12.7 %slice-start.2 = ((s8[14680064]{0:T(1024)(128)(4,1)}), s8[4194304]{0:T(1024)(128)(4,1)S(1)}, s32[]{:S(2)}) async-start(s8[14680064]{0:T(1024)(128)(4,1)} %bitcast), calls=%async_computation.2 | async-start | bytes 8388608
  6.4 12.7 %slice-start.3 = ((s8[14680064]{0:T(1024)(128)(4,1)}), s8[2097152]{0:T(1024)(128)(4,1)S(1)}, s32[]{:S(2)}) async-start(s8[14680064]{0:T(1024)(128)(4,1)} %bitcast), calls=%async_computation.3 | async-start | bytes 4194304
  6.4 5.2 %collective-permute-start.3 = (bf16[8,3712]{1,0:T(8,128)(2,1)S(1)}, bf16[8,3712]{1,0:T(8,128)(2,1)S(1)}, u32[]{:S(2)}, u32[]{:S(2)}) collective-permute-start(bf16[8,3712]{1,0:T(8,128)(2,1)S(1)} %join.1.refs_0_), channel_id=1, source_target_pairs={{0,7},{1,6},{2,5},{3,4},{4,3},{5,2},{6,1},{7,0},{8,15},{9,14},{10,... | collective-permute-start | bytes 178184 | tf_op jit(solution)/shard_map/ppermute | solution.py:79
  9.2 3.7 %collective-permute-start.2 = (bf16[8,3712]{1,0:T(8,128)(2,1)S(1)}, bf16[8,3712]{1,0:T(8,128)(2,1)S(1)}, u32[]{:S(2)}, u32[]{:S(2)}) collective-permute-start(bf16[8,3712]{1,0:T(8,128)(2,1)S(1)} %join.1.refs_0_), channel_id=1, source_target_pairs={{0,5},{1,4},{2,7},{3,6},{4,1},{5,0},{6,3},{7,2},{8,13},{9,12},{10,... | collective-permute-start | bytes 178184 | tf_op jit(solution)/shard_map/ppermute | solution.py:79
  9.7 4.0 %collective-permute-start.1 = (bf16[8,3712]{1,0:T(8,128)(2,1)S(1)}, bf16[8,3712]{1,0:T(8,128)(2,1)S(1)}, u32[]{:S(2)}, u32[]{:S(2)}) collective-permute-start(bf16[8,3712]{1,0:T(8,128)(2,1)S(1)} %join.1.refs_0_), channel_id=1, source_target_pairs={{0,3},{1,2},{2,1},{3,0},{4,7},{5,6},{6,5},{7,4},{8,11},{9,10},{10,... | collective-permute-start | bytes 178184 | tf_op jit(solution)/shard_map/ppermute | solution.py:79
  9.9 3.9 %collective-permute-start.4 = (bf16[8,3712]{1,0:T(8,128)(2,1)S(1)}, bf16[8,3712]{1,0:T(8,128)(2,1)S(1)}, u32[]{:S(2)}, u32[]{:S(2)}) collective-permute-start(bf16[8,3712]{1,0:T(8,128)(2,1)S(1)} %join.1.refs_0_), channel_id=1, source_target_pairs={{0,1},{1,0},{2,3},{3,2},{4,5},{5,4},{6,7},{7,6},{8,9},{9,8},{10,11... | collective-permute-start | bytes 178184 | tf_op jit(solution)/shard_map/ppermute | solution.py:79
  11.6 2.3 %collective-permute-start.7 = (bf16[8,3712]{1,0:T(8,128)(2,1)S(1)}, bf16[8,3712]{1,0:T(8,128)(2,1)S(1)}, u32[]{:S(2)}, u32[]{:S(2)}) collective-permute-start(bf16[8,3712]{1,0:T(8,128)(2,1)S(1)} %collective-permute-done.3.refs_3_), channel_id=1, source_target_pairs={{0,1},{1,0},{2,3},{3,2},{4,5},{5,4},{6,7},{7,6},{8,9},{9,8},{10,11... | collective-permute-start | bytes 178184 | tf_op jit(solution)/shard_map/ppermute | solution.py:79
  12.9 1.6 %collective-permute-start.6 = (bf16[8,3712]{1,0:T(8,128)(2,1)S(1)}, bf16[8,3712]{1,0:T(8,128)(2,1)S(1)}, u32[]{:S(2)}, u32[]{:S(2)}) collective-permute-start(bf16[8,3712]{1,0:T(8,128)(2,1)S(1)} %collective-permute-done.2.refs_2_), channel_id=1, source_target_pairs={{0,1},{1,0},{2,3},{3,2},{4,5},{5,4},{6,7},{7,6},{8,9},{9,8},{10,11... | collective-permute-start | bytes 178184 | tf_op jit(solution)/shard_map/ppermute | solution.py:79
  13.7 1.2 %collective-permute-start.5 = (bf16[8,3712]{1,0:T(8,128)(2,1)S(1)}, bf16[8,3712]{1,0:T(8,128)(2,1)S(1)}, u32[]{:S(2)}, u32[]{:S(2)}) collective-permute-start(bf16[8,3712]{1,0:T(8,128)(2,1)S(1)} %collective-permute-done.1.refs_1_), channel_id=1, source_target_pairs={{0,1},{1,0},{2,3},{3,2},{4,5},{5,4},{6,7},{7,6},{8,9},{9,8},{10,11... | collective-permute-start | bytes 178184 | tf_op jit(solution)/shard_map/ppermute | solution.py:79
  21.2 1.4 %collective-permute-start.8 = (bf16[16,3584]{1,0:T(8,128)(2,1)S(1)}, bf16[16,3584]{1,0:T(8,128)(2,1)S(1)}, u32[]{:S(2)}, u32[]{:S(2)}) collective-permute-start(bf16[16,3584]{1,0:T(8,128)(2,1)S(1)} %get-tuple-element.20), channel_id=1, source_target_pairs={{0,1},{1,0},{2,3},{3,2},{4,5},{5,4},{6,7},{7,6},{8,9},{9,8},{10,11... | collective-permute-start | bytes 344072 | tf_op jit(solution)/shard_map/ppermute | solution.py:79
  21.4 3.6 %collective-permute-start.11 = (bf16[16,3584]{1,0:T(8,128)(2,1)S(1)}, bf16[16,3584]{1,0:T(8,128)(2,1)S(1)}, u32[]{:S(2)}, u32[]{:S(2)}) collective-permute-start(bf16[16,3584]{1,0:T(8,128)(2,1)S(1)} %get-tuple-element.24), channel_id=1, source_target_pairs={{0,1},{1,0},{2,3},{3,2},{4,5},{5,4},{6,7},{7,6},{8,9},{9,8},{10,11... | collective-permute-start | bytes 344072 | tf_op jit(solution)/shard_map/ppermute | solution.py:79
  22.6 4.8 %collective-permute-start.9 = (bf16[8,3584]{1,0:T(8,128)(2,1)S(1)}, bf16[8,3584]{1,0:T(8,128)(2,1)S(1)}, u32[]{:S(2)}, u32[]{:S(2)}) collective-permute-start(bf16[8,3584]{1,0:T(8,128)(2,1)S(1)} %get-tuple-element.21), channel_id=1, source_target_pairs={{0,7},{1,6},{2,5},{3,4},{4,3},{5,2},{6,1},{7,0},{8,15},{9,14},{10,... | collective-permute-start | bytes 172040 | tf_op jit(solution)/shard_map/ppermute | solution.py:79
  24.6 3.7 %collective-permute-start.10 = (bf16[8,3584]{1,0:T(8,128)(2,1)S(1)}, bf16[8,3584]{1,0:T(8,128)(2,1)S(1)}, u32[]{:S(2)}, u32[]{:S(2)}) collective-permute-start(bf16[8,3584]{1,0:T(8,128)(2,1)S(1)} %get-tuple-element.22), channel_id=1, source_target_pairs={{0,5},{1,4},{2,7},{3,6},{4,1},{5,0},{6,3},{7,2},{8,13},{9,12},{10,... | collective-permute-start | bytes 172040 | tf_op jit(solution)/shard_map/ppermute | solution.py:79
  25.0 3.9 %collective-permute-start.12 = (bf16[8,3584]{1,0:T(8,128)(2,1)S(1)}, bf16[8,3584]{1,0:T(8,128)(2,1)S(1)}, u32[]{:S(2)}, u32[]{:S(2)}) collective-permute-start(bf16[8,3584]{1,0:T(8,128)(2,1)S(1)} %get-tuple-element.25), channel_id=1, source_target_pairs={{0,3},{1,2},{2,1},{3,0},{4,7},{5,6},{6,5},{7,4},{8,11},{9,10},{10,... | collective-permute-start | bytes 172040 | tf_op jit(solution)/shard_map/ppermute | solution.py:79
  29.0 4.3 %collective-permute-start.13 = (bf16[4,3584]{1,0:T(4,128)(2,1)S(1)}, bf16[4,3584]{1,0:T(4,128)(2,1)S(1)}, u32[]{:S(2)}, u32[]{:S(2)}) collective-permute-start(bf16[4,3584]{1,0:T(4,128)(2,1)S(1)} %get-tuple-element.28), channel_id=1, source_target_pairs={{0,9},{1,8},{2,11},{3,10},{4,13},{5,12},{6,15},{7,14},{8,1},{9,0},... | collective-permute-start | bytes 86024 | tf_op jit(solution)/shard_map/ppermute | solution.py:79
